TPU v7x, 32 devices: a whole 2x2x4 slice. The times are simulated.
32 devices in a mesh: seq: 16 (over z, y, core), ch: 2 (over x).
Axes of the slice: x: 2, y: 2, z: 4, core: 2. Of those that a mesh axis runs over, the one named last changes fastest.
Arguments:
- tokens: bfloat16 [2, 32768, 1280], P(None, 'seq', 'ch'), may hold values from -6 to 6
- cotangent: bfloat16 [2, 32768, 1280], P(None, 'seq', 'ch'), may hold values from -6 to 6
- seq_lengths: int32 [2, 128], replicated, may hold values from 1 to 1024, 32768 in all within a row
- residue_mask: int32 [2, 32768], P(None, 'seq'), may hold values 0 or 1
- first_gain: float32 [1280], P('ch'), may hold values from 0.25 to 1.75
- first_shift: float32 [1280], P('ch'), may hold values from -2.5 to 2.5
- proj_in: bfloat16 [1280, 640], P('seq', 'ch'), may hold values from -0.15625 to 0.15625
- in_bias: float32 [640], P('ch'), may hold values from -2.5 to 2.5
- mid_gain: float32 [640], P('ch'), may hold values from 0.25 to 1.75
- mid_shift: float32 [640], P('ch'), may hold values from -2.5 to 2.5
- conv_weight: bfloat16 [5, 640, 640], P(None, 'seq', 'ch'), may hold values from -0.109375 to 0.109375
- conv_bias: float32 [640], P('ch'), may hold values from -2.5 to 2.5
- last_gain: float32 [640], P('ch'), may hold values from 0.25 to 1.75
- last_shift: float32 [640], P('ch'), may hold values from -2.5 to 2.5
- proj_out: bfloat16 [640, 1280], P('ch', 'seq'), may hold values from -0.25 to 0.25
- out_bias: float32 [1280], P('ch'), may hold values from -2.5 to 2.5
Outputs:
- block_out: bfloat16 [2, 32768, 1280], P(None, 'seq', 'ch')
- grad_tokens: float32 [2, 32768, 1280], P(None, 'seq', 'ch')
- grad_first_gain: float32 [1280], P('ch')
- grad_first_shift: float32 [1280], P('ch')
- grad_proj_in: float32 [1280, 640], P('seq', 'ch')
- grad_in_bias: float32 [640], P('ch')
- grad_mid_gain: float32 [640], P('ch')
- grad_mid_shift: float32 [640], P('ch')
- grad_conv_weight: float32 [5, 640, 640], P(None, 'seq', 'ch')
- grad_conv_bias: float32 [640], P('ch')
- grad_last_gain: float32 [640], P('ch')
- grad_last_shift: float32 [640], P('ch')
- grad_proj_out: float32 [640, 1280], P('ch', 'seq')
- grad_out_bias: float32 [1280], P('ch')
Inputs may be any that keep to these rules, and one draw needn't show every extreme that they name: `seq_lengths`: each row sums to 32768; the longest protein of each row has exactly 1024 residues.
All inputs are finite; a program needn't handle non-finite values. No bound on the sum of `residue_mask` on one device may be relied on, other than what follows from the above.
Results may differ from a plain program's by a relative error of at most 0.0067.
Values may be sent and summed in bfloat16 or wider, within the bound.
A program may use at most 256 MiB of HBM per device.

v0:
```python
import jax
import jax.numpy as jnp
from jax import lax
from jax.sharding import PartitionSpec as P

KERNEL_TAPS = 5
DILATION_STEP = 32
HALO = 64


EPSILON = 1e-05
ROOT_HALF = 0.7071067811865476
ROOT_TAU = 0.3989422804014327


def extended(block, sides, width):
    for axis, dim in sides:
        count = lax.axis_size(axis)
        forward = [(i, i + 1) for i in range(count - 1)]
        backward = [(target, source) for source, target in forward]
        low = lax.ppermute(
            lax.slice_in_dim(block, block.shape[dim] - width, None, axis=dim), axis, forward
        )
        high = lax.ppermute(lax.slice_in_dim(block, 0, width, axis=dim), axis, backward)
        block = jnp.concatenate([low, block, high], axis=dim)
    return block


def gelu_value(value):
    return 0.5 * value * (1.0 + lax.erf(value * ROOT_HALF))


def gelu_slope(value):
    return (
        0.5 * (1.0 + lax.erf(value * ROOT_HALF)) + value * jnp.exp(-0.5 * value * value) * ROOT_TAU
    )


def row_sums(first, second):
    return lax.psum((jnp.sum(first, axis=1), jnp.sum(second, axis=1)), "ch")


def channel_whole(value):
    return lax.all_gather(value, "ch", axis=1, tiled=True)


def channel_share(value):
    return lax.psum_scatter(value, "ch", scatter_dimension=1, tiled=True)


def norm_share(value, gain, shift, width):
    totals, squares = row_sums(value, value * value)
    middle = totals / width
    scale = lax.rsqrt(squares / width - middle * middle + EPSILON)
    normed = (value - middle[:, None]) * scale[:, None]
    return (normed, scale, normed * gain + shift)


def norm_share_back(grad_zed, normed, scale, gain, width):
    grad_normed = grad_zed * gain
    first, second = row_sums(grad_normed, grad_normed * normed)
    grad_value = scale[:, None] * (
        grad_normed - first[:, None] / width - normed * (second[:, None] / width)
    )
    return (grad_value, jnp.sum(grad_zed * normed, axis=0), jnp.sum(grad_zed, axis=0))


def hidden_rows(left, right):
    return lax.dot_general(
        left, right, (((0,), (0,)), ((), ())), preferred_element_type=jnp.float32
    )


def inner_cols(left, right):
    return lax.dot_general(
        left, right, (((1,), (1,)), ((), ())), preferred_element_type=jnp.float32
    )


def body(
    tokens,
    cotangent,
    seq_lengths,
    residue_mask,
    first_gain,
    first_shift,
    proj_in,
    in_bias,
    mid_gain,
    mid_shift,
    conv_weight,
    conv_bias,
    last_gain,
    last_shift,
    proj_out,
    out_bias,
):
    micro, token_rows, half_model = tokens.shape
    inner_share = in_bias.shape[0]
    width_model = half_model * lax.axis_size("ch")
    width_inner = inner_share * lax.axis_size("ch")
    total_rows = token_rows * lax.axis_size("seq")
    places = (
        lax.axis_index("seq") * token_rows
        + jnp.arange(token_rows + 2 * HALO, dtype=jnp.int32)
        - HALO
    )
    inside = (places >= 0) & (places < total_rows)
    small_sums = None
    outputs = []
    grad_inputs = []
    for index in range(micro):
        gathered = (
            lax.all_gather(proj_in, "seq", axis=0, tiled=True),
            lax.all_gather(conv_weight, "seq", axis=1, tiled=True),
            lax.all_gather(proj_out, "seq", axis=1, tiled=True),
        )
        weight_in, weight_conv, weight_out = gathered
        bounds = jnp.cumsum(seq_lengths[index])[:-1]
        sequence_segment = jnp.sum((places[:, None] >= bounds[None, :]).astype(jnp.int32), axis=1)
        sequence_segment = jnp.where(inside, sequence_segment, -1)
        middle_tap = sequence_segment[HALO : HALO + token_rows]
        taps = [
            (
                sequence_segment[tap_index * DILATION_STEP : tap_index * DILATION_STEP + token_rows]
                == middle_tap
            ).astype(jnp.bfloat16)[:, None]
            for tap_index in range(KERNEL_TAPS)
        ]
        keep_mask = residue_mask[index].astype(jnp.float32)[:, None]
        value = tokens[index].astype(jnp.float32)
        normed_one, scale_one, zed_one = norm_share(value, first_gain, first_shift, width_model)
        act_one = channel_whole(gelu_value(zed_one).astype(jnp.bfloat16))
        hidden_one = jnp.dot(act_one, weight_in, preferred_element_type=jnp.float32) + in_bias
        normed_two, scale_two, zed_two = norm_share(hidden_one, mid_gain, mid_shift, width_inner)
        act_two = channel_whole((gelu_value(zed_two) * keep_mask).astype(jnp.bfloat16))
        framed_rows = extended(act_two, (("seq", 0),), HALO)
        hidden_three = jnp.zeros((token_rows, inner_share), jnp.float32) + conv_bias
        for tap_index in range(KERNEL_TAPS):
            sliding_window = framed_rows[
                tap_index * DILATION_STEP : tap_index * DILATION_STEP + token_rows
            ]
            hidden_three = hidden_three + taps[tap_index].astype(jnp.float32) * jnp.dot(
                sliding_window, weight_conv[tap_index], preferred_element_type=jnp.float32
            )
        normed_three, scale_three, zed_three = norm_share(
            hidden_three, last_gain, last_shift, width_inner
        )
        act_three = gelu_value(zed_three).astype(jnp.bfloat16)
        mixed = channel_share(jnp.dot(act_three, weight_out, preferred_element_type=jnp.float32))
        outputs.append((value + mixed + out_bias).astype(jnp.bfloat16))
        grad_y = cotangent[index]
        grad_full = channel_whole(grad_y)
        grad_out = hidden_rows(act_three, grad_full)
        grad_out_bias = jnp.sum(grad_y.astype(jnp.float32), axis=0)
        grad_act_three = inner_cols(grad_full, weight_out)
        grad_three, grad_last_gain, grad_last_shift = norm_share_back(
            grad_act_three * gelu_slope(zed_three),
            normed_three,
            scale_three,
            last_gain,
            width_inner,
        )
        grad_three_low = grad_three.astype(jnp.bfloat16)
        grad_conv_bias = jnp.sum(grad_three_low.astype(jnp.float32), axis=0)
        spread_gradient = jnp.zeros((token_rows + 2 * HALO, width_inner), jnp.float32)
        convolution_terms = []
        for tap_index in range(KERNEL_TAPS):
            masked_rows = grad_three_low * taps[tap_index]
            convolution_terms.append(
                hidden_rows(
                    framed_rows[tap_index * DILATION_STEP : tap_index * DILATION_STEP + token_rows],
                    masked_rows,
                )
            )
            spread_gradient = spread_gradient.at[
                tap_index * DILATION_STEP : tap_index * DILATION_STEP + token_rows
            ].add(inner_cols(masked_rows, weight_conv[tap_index]))
        grad_conv = jnp.stack(convolution_terms, 0)
        own_back = channel_share(spread_gradient)
        rims = jnp.concatenate([own_back[:HALO], own_back[token_rows + HALO :]], 0)
        framed_rims = extended(rims.astype(jnp.bfloat16), (("seq", 0),), HALO).astype(rims.dtype)
        middle_rows = own_back[HALO : HALO + token_rows]
        middle_rows = middle_rows.at[:HALO].add(framed_rims[:HALO])
        middle_rows = middle_rows.at[token_rows - HALO :].add(framed_rims[3 * HALO :])
        grad_zed_two = middle_rows * keep_mask * gelu_slope(zed_two)
        grad_one, grad_mid_gain, grad_mid_shift = norm_share_back(
            grad_zed_two, normed_two, scale_two, mid_gain, width_inner
        )
        grad_one_low = grad_one.astype(jnp.bfloat16)
        grad_in_bias = jnp.sum(grad_one_low.astype(jnp.float32), axis=0)
        grad_in = hidden_rows(act_one, grad_one_low)
        grad_act_one = channel_share(inner_cols(grad_one_low, weight_in))
        grad_value, grad_first_gain, grad_first_shift = norm_share_back(
            grad_act_one * gelu_slope(zed_one), normed_one, scale_one, first_gain, width_model
        )
        grad_inputs.append(grad_y.astype(jnp.float32) + grad_value)
        smalls = (
            grad_first_gain,
            grad_first_shift,
            grad_in_bias,
            grad_mid_gain,
            grad_mid_shift,
            grad_conv_bias,
            grad_last_gain,
            grad_last_shift,
            grad_out_bias,
        )
        small_sums = smalls if small_sums is None else jax.tree.map(jnp.add, small_sums, smalls)
        shares = (
            lax.psum_scatter(grad_in, "seq", scatter_dimension=0, tiled=True),
            lax.psum_scatter(grad_conv, "seq", scatter_dimension=1, tiled=True),
            lax.psum_scatter(grad_out, "seq", scatter_dimension=1, tiled=True),
        )
        if index == 0:
            share_sums = shares
        else:
            share_sums = jax.tree.map(jnp.add, share_sums, shares)
    totals = lax.psum(small_sums, "seq")
    return (
        jnp.stack(outputs, 0),
        jnp.stack(grad_inputs, 0),
        totals[0],
        totals[1],
        share_sums[0],
        totals[2],
        totals[3],
        totals[4],
        share_sums[1],
        totals[5],
        totals[6],
        totals[7],
        share_sums[2],
        totals[8],
    )


def solution(mesh):
    placed = (
        P(None, "seq", "ch"),
        P(None, "seq", "ch"),
        P(),
        P(None, "seq"),
        P("ch"),
        P("ch"),
        P("seq", "ch"),
        P("ch"),
        P("ch"),
        P("ch"),
        P(None, "seq", "ch"),
        P("ch"),
        P("ch"),
        P("ch"),
        P("ch", "seq"),
        P("ch"),
    )
    return jax.shard_map(
        body,
        mesh=mesh,
        in_specs=placed,
        out_specs=(
            P(None, "seq", "ch"),
            P(None, "seq", "ch"),
            P("ch"),
            P("ch"),
            P("seq", "ch"),
            P("ch"),
            P("ch"),
            P("ch"),
            P(None, "seq", "ch"),
            P("ch"),
            P("ch"),
            P("ch"),
            P("ch", "seq"),
            P("ch"),
        ),
        check_vma=False,
    )
```

profile of v0, /device:TPU:24, one launch (start us, length us, event | category | flops | bytes accessed | tf_op | source)
XLA Modules:
  0.0 1505.3 jit_solution(738775183280770456)
XLA Ops:
  7.2 3.4 convert_reduce_fusion.3
  12.4 8.4 all-reduce.8
  20.8 10.4 fusion.16
  32.1 21.0 %all_gather.31 = bf16[1280,320]{1,0:T(8,128)(2,1)} all-gather(bf16[80,320]{1,0:T(8,128)(2,1)S(1)} %copy-done.45), channel_id=1, replica_groups=mesh['seq'=16,'ch'=2] {'seq'}, dimensions={0}, use_global_device_ids=true | all-gather | bytes 870400 | tf_op jit(solution)/shard_map/all_gather | solution.py:114
  53.1 46.9 %all-gather.16.cloned.1.call-done = bf16[2048,1280]{1,0:T(8,128)(2,1)} async-done(((bf16[2048,640]{1,0:T(8,128)(2,1)}), bf16[2048,1280]{1,0:T(8,128)(2,1)}) %all-gather.16.cloned.1.call-update) | async-done | bytes 5242896 | tf_op jit(solution)/shard_map/all_gather | solution.py:44
  100.1 4.8 fusion.210
  104.9 65.9 %all-gather.10.cloned.1.call-done = bf16[2048,1280]{1,0:T(8,128)(2,1)} async-done(((bf16[2048,640]{1,0:T(8,128)(2,1)}), bf16[2048,1280]{1,0:T(8,128)(2,1)}) %all-gather.10.cloned.1.call-update) | async-done | bytes 5242896 | tf_op jit(solution)/shard_map/all_gather | solution.py:44
  170.8 6.3 fusion.208
  177.0 7.4 all-reduce.7
  184.6 4.4 multiply_convert_fusion.7
  190.3 5.3 fusion.233
  198.3 21.0 %all_gather.34 = bf16[320,1280]{0,1:T(8,128)(2,1)} all-gather(bf16[320,80]{0,1:T(8,128)(2,1)S(1)} %copy-done.46), channel_id=1, replica_groups=mesh['seq'=16,'ch'=2] {'seq'}, dimensions={1}, use_global_device_ids=true | all-gather | bytes 870400 | tf_op jit(solution)/shard_map/all_gather | solution.py:116
  219.3 9.8 all-gather.18.cloned.1.call-done
  234.9 35.2 %all-gather.12.cloned.1.call-done = bf16[2048,640]{0,1:T(8,128)(2,1)} async-done(((bf16[2048,320]{0,1:T(8,128)(2,1)}), bf16[2048,640]{0,1:T(8,128)(2,1)}) %all-gather.12.cloned.1.call-update) | async-done | bytes 2621456 | tf_op jit(solution)/shard_map/all_gather | solution.py:44
  277.2 36.7 %all-gather.14.cloned.1.call-done = bf16[5,640,320]{2,1,0:T(8,128)(2,1)} async-done(((bf16[5,40,320]{2,1,0:T(8,128)(2,1)}), bf16[5,640,320]{2,1,0:T(8,128)(2,1)}) %all-gather.14.cloned.1.call-update) | async-done | bytes 2048016 | tf_op jit(solution)/shard_map/all_gather | solution.py:115
  331.3 3.7 fusion.209
  338.3 9.0 all-reduce.6
  347.3 37.3 %all-gather.22.cloned.1.call-done = bf16[1,2048,1280]{2,1,0:T(8,128)(2,1)} async-done(((bf16[1,2048,640]{2,1,0:T(8,128)(2,1)}), bf16[1,2048,1280]{2,1,0:T(8,128)(2,1)}) %all-gather.22.cloned.1.call-update) | async-done | bytes 5242896 | tf_op jit(solution)/shard_map/all_gather | solution.py:44
  384.6 7.8 fusion.82
  392.4 62.3 %all-gather.20.cloned.1.call-done = bf16[1,2048,1280]{2,1,0:T(8,128)(2,1)} async-done(((bf16[1,2048,640]{2,1,0:T(8,128)(2,1)}), bf16[1,2048,1280]{2,1,0:T(8,128)(2,1)}) %all-gather.20.cloned.1.call-update) | async-done | bytes 5242896 | tf_op jit(solution)/shard_map/all_gather | solution.py:44
  454.7 9.0 multiply_reduce_fusion.3
  463.7 7.6 all-reduce.5
  471.4 7.2 convert_reduce_fusion.4
  484.0 5.0 slice_add_fusion.7
  489.0 27.2 %scatter-add.49 = f32[2176,640]{0,1:T(8,128)} dynamic-update-slice(f32[2176,640]{0,1:T(8,128)} %scatter-add.46, f32[2048,640]{0,1:T(8,128)} %slice_add_fusion.7, s32[]{:T(128)} %constant.403.clone.1, s32[]{:T(128)} %constant.391.clone.1) | dynamic-update-slice | bytes 10485764 | tf_op jit(solution)/shard_map/scatter-add | solution.py:178
  516.2 6.6 slice_add_fusion.5
  522.8 27.2 %scatter-add.50 = f32[2176,640]{0,1:T(8,128)} dynamic-update-slice(f32[2176,640]{0,1:T(8,128)} %scatter-add.49, f32[2048,640]{0,1:T(8,128)} %slice_add_fusion.5, s32[]{:T(128)} %constant.404.clone.1, s32[]{:T(128)} %constant.391.clone.1) | dynamic-update-slice | bytes 10485764 | tf_op jit(solution)/shard_map/scatter-add | solution.py:178
  550.0 6.6 slice_add_fusion.4
  556.6 27.2 %scatter-add.51 = f32[2176,640]{0,1:T(8,128)} dynamic-update-slice(f32[2176,640]{0,1:T(8,128)} %scatter-add.50, f32[2048,640]{0,1:T(8,128)} %slice_add_fusion.4, s32[]{:T(128)} %constant.405.clone.1, s32[]{:T(128)} %constant.391.clone.1) | dynamic-update-slice | bytes 10485764 | tf_op jit(solution)/shard_map/scatter-add | solution.py:178
  583.8 6.5 fusion.59
  596.0 5.1 slice_add_fusion.6
  601.1 27.4 %scatter-add.60 = f32[2176,640]{0,1:T(8,128)} dynamic-update-slice(f32[2176,640]{0,1:T(8,128)} %scatter-add.59, f32[2048,640]{0,1:T(8,128)} %slice_add_fusion.6, s32[]{:T(128)} %constant.403.clone.1, s32[]{:T(128)} %constant.391.clone.1) | dynamic-update-slice | bytes 10485764 | tf_op jit(solution)/shard_map/scatter-add | solution.py:178
  628.5 6.8 slice_add_fusion.2
  635.3 27.3 %scatter-add.61 = f32[2176,640]{0,1:T(8,128)} dynamic-update-slice(f32[2176,640]{0,1:T(8,128)} %scatter-add.60, f32[2048,640]{0,1:T(8,128)} %slice_add_fusion.2, s32[]{:T(128)} %constant.404.clone.1, s32[]{:T(128)} %constant.391.clone.1) | dynamic-update-slice | bytes 10485764 | tf_op jit(solution)/shard_map/scatter-add | solution.py:178
  662.5 6.7 slice_add_fusion.1
  669.2 27.2 %scatter-add.64 = f32[2176,640]{0,1:T(8,128)} dynamic-update-slice(f32[2176,640]{0,1:T(8,128)} %scatter-add.61, f32[2048,640]{0,1:T(8,128)} %slice_add_fusion.1, s32[]{:T(128)} %constant.405.clone.1, s32[]{:T(128)} %constant.391.clone.1) | dynamic-update-slice | bytes 10485764 | tf_op jit(solution)/shard_map/scatter-add | solution.py:178
  696.4 6.5 fusion.58
  723.5 7.4 copy.82
  732.6 5.6 fusion.239
  739.5 5.5 fusion.238
  749.2 4.5 collective-permute-start.5
  753.8 19.7 %reduce-scatter.18.cloned.1.call-done = f32[2176,320]{0,1:T(8,128)} async-done(((f32[2176,640]{0,1:T(8,128)}), f32[2176,320]{0,1:T(8,128)}) %reduce-scatter.18.cloned.1.call-update) | async-done | bytes 2785296 | tf_op jit(solution)/shard_map/reduce_scatter | solution.py:48
  777.4 4.8 collective-permute-start.7
  799.6 8.5 multiply_reduce_fusion.5
  808.1 7.8 all-reduce.4
  815.9 6.2 convert_reduce_fusion.6
  823.2 5.6 fusion.241
  830.4 5.6 fusion.240
  837.4 5.0 fusion.60
  842.4 6.8 fusion.68
  853.0 18.5 %reduce-scatter.24.cloned.1.call-done = f32[5,40,320]{2,0,1:T(8,128)} async-done(((f32[5,640,320]{2,0,1:T(8,128)}), f32[5,40,320]{2,0,1:T(8,128)}) %reduce-scatter.24.cloned.1.call-update) | async-done | bytes 256016 | tf_op jit(solution)/shard_map/reduce_scatter | solution.py:212
  873.4 5.0 fusion.242
  878.5 6.8 convolution_add_fusion
  885.3 111.4 %reduce-scatter.12.cloned.1.call-done = f32[2048,640]{1,0:T(8,128)} async-done(((f32[2048,1280]{1,0:T(8,128)}), f32[2048,640]{1,0:T(8,128)}) %reduce-scatter.12.cloned.1.call-update) | async-done | bytes 5242896 | tf_op jit(solution)/shard_map/reduce_scatter | solution.py:48
  996.7 124.1 %reduce-scatter.10.cloned.1.call-done = f32[2048,640]{1,0:T(8,128)} async-done(((f32[2048,1280]{1,0:T(8,128)}), f32[2048,640]{1,0:T(8,128)}) %reduce-scatter.10.cloned.1.call-update) | async-done | bytes 5242896 | tf_op jit(solution)/shard_map/reduce_scatter | solution.py:48
  1120.8 124.2 %reduce-scatter.20.cloned.1.call-done = f32[2048,640]{1,0:T(8,128)} async-done(((f32[2048,1280]{1,0:T(8,128)}), f32[2048,640]{1,0:T(8,128)}) %reduce-scatter.20.cloned.1.call-update) | async-done | bytes 5242896 | tf_op jit(solution)/shard_map/reduce_scatter | solution.py:48
  1245.0 124.6 %reduce-scatter.16.cloned.1.call-done = f32[2048,640]{1,0:T(8,128)} async-done(((f32[2048,1280]{1,0:T(8,128)}), f32[2048,640]{1,0:T(8,128)}) %reduce-scatter.16.cloned.1.call-update) | async-done | bytes 5242896 | tf_op jit(solution)/shard_map/reduce_scatter | solution.py:48
  1369.6 19.7 %fusion.27 = (f32[640]{0:T(1024)S(1)}, f32[2048]{0:T(1024)S(1)}, f32[2048]{0:T(1024)S(1)}, f32[640]{0:T(1024)S(1)}, f32[2048]{0:T(1024)S(1)}, /*index=5*/f32[204...) fusion(f32[2048]{0:T(1024)S(1)} %copy-done.40, ...), kind=kLoop, calls=%fused_computation.38 | loop fusion | flops 57660928 | bytes 52512256 | tf_op jit(solution)/shard_map/reduce_sum | solution.py:65
  1389.3 7.4 all-reduce.3
  1396.7 50.6 %all-reduce.2 = (f32[640]{0:T(1024)}, f32[640]{0:T(1024)}, f32[320]{0:T(512)}, f32[320]{0:T(512)}, f32[320]{0:T(512)}, /*index=5*/f32[320]{0:T(512)}, f32[320]{0:T(512)}, f32[320]{0:T(512)}, f32[640]{0:T(1024)}) all-reduce(f32[640]{0:T(1024)S(1)} %add.481, f32[640]{0:T(1024)S(1)} %add.482, ...), channel_id=1, replica_groups=mesh['seq'=16,'ch'=2] {'seq'}, use_global_device_ids=true, to_apply=%region_60.61 | all-reduce | flops 3840 | bytes 30720 | tf_op jit(solution)/shard_map/psum | solution.py:219
  1447.3 5.2 pad_maximum_fusion.1
  1454.4 8.3 fusion.26
  1462.7 4.8 pad_maximum_fusion
  1467.5 30.8 %reduce-scatter.22.cloned.1.call-done = f32[80,320]{1,0:T(8,128)} async-done(((f32[1280,320]{1,0:T(8,128)}), f32[80,320]{1,0:T(8,128)}) %reduce-scatter.22.cloned.1.call-update) | async-done | bytes 102416 | tf_op jit(solution)/shard_map/reduce_scatter | solution.py:211
  (275 shorter events, 111.2 us)
Async XLA Ops:
  7.2 92.9 %all-gather.16.cloned.1.call-start = ((), (), s32[]{:S(2)}) async-start(), calls=%async_computation.13 | async-start | bytes 7864320 | tf_op jit(solution)/shard_map/all_gather | solution.py:44
  11.3 9.5 copy-start.47
  11.3 9.5 copy-start.52
  20.8 10.4 copy-start.35
  20.8 10.4 copy-start.37
  20.8 10.4 copy-start.39
  20.8 10.4 copy-start.41
  31.2 21.9 %copy-start.51 = (s32[2,2048]{1,0:T(2,128)S(1)}, s32[2,2048]{1,0:T(2,128)}, u32[]{:S(2)}) copy-start(s32[2,2048]{1,0:T(2,128)} %param.47) | copy-start | bytes 49156
  31.2 68.8 %copy-start.65 = (f32[320]{0:T(512)S(1)}, f32[320]{0:T(512)}, u32[]{:S(2)}) copy-start(f32[320]{0:T(512)} %param.51) | copy-start | bytes 3844
  31.3 139.5 %all-gather.10.cloned.1.call-start = ((), (), s32[]{:S(2)}) async-start(), calls=%async_computation.9 | async-start | bytes 7864320 | tf_op jit(solution)/shard_map/all_gather | solution.py:44
  32.0 197.1 %all-gather.18.cloned.1.call-start = ((), (), s32[]{:S(2)}) async-start(), calls=%async_computation.14 | async-start | bytes 3932160 | tf_op jit(solution)/shard_map/all_gather | solution.py:44
  53.1 131.4 %copy-start.43 = (f32[1,2048]{1,0:T(1,128)}, f32[1,2048]{1,0:T(1,128)S(1)}, u32[]{:S(2)}) copy-start(f32[1,2048]{1,0:T(1,128)S(1)} %get-tuple-element.365) | copy-start | bytes 24580
  53.1 131.4 %copy-start.44 = (f32[1,2048]{1,0:T(1,128)}, f32[1,2048]{1,0:T(1,128)S(1)}, u32[]{:S(2)}) copy-start(f32[1,2048]{1,0:T(1,128)S(1)} %get-tuple-element.366) | copy-start | bytes 24580
  104.8 79.7 %copy-start.6 = (f32[2048,320]{0,1:T(8,128)}, f32[2048,320]{0,1:T(8,128)S(1)}, u32[]{:S(2)}) copy-start(f32[2048,320]{0,1:T(8,128)S(1)} %get-tuple-element.409) | copy-start | bytes 7864324
  104.9 79.7 %copy-start.49 = (f32[320]{0:T(512)S(1)}, f32[320]{0:T(512)}, u32[]{:S(2)}) copy-start(f32[320]{0:T(512)} %param.52) | copy-start | bytes 3844
  104.9 79.7 %copy-start.54 = (f32[320]{0:T(512)S(1)}, f32[320]{0:T(512)}, u32[]{:S(2)}) copy-start(f32[320]{0:T(512)} %param.53) | copy-start | bytes 3844
  189.0 81.1 %all-gather.12.cloned.1.call-start = ((), (), s32[]{:S(2)}) async-start(), calls=%async_computation.10 | async-start | bytes 3932160 | tf_op jit(solution)/shard_map/all_gather | solution.py:44
  189.6 124.2 %all-gather.14.cloned.1.call-start = ((), (), s32[]{:S(2)}) async-start(), calls=%async_computation.11 | async-start | bytes 2611200 | tf_op jit(solution)/shard_map/all_gather | solution.py:115
  190.2 194.4 %all-gather.22.cloned.1.call-start = ((), (), s32[]{:S(2)}) async-start(), calls=%async_computation.21 | async-start | bytes 7864320 | tf_op jit(solution)/shard_map/all_gather | solution.py:44
  195.6 259.1 %all-gather.20.cloned.1.call-start = ((), (), s32[]{:S(2)}) async-start(), calls=%async_computation.20 | async-start | bytes 7864320 | tf_op jit(solution)/shard_map/all_gather | solution.py:44
  196.3 548.8 %reduce-scatter.14.cloned.1.call-start = ((), (), s32[]{:S(2)}) async-start(), calls=%async_computation.16 | async-start | bytes 8355840 | tf_op jit(solution)/shard_map/reduce_scatter | solution.py:48
  230.2 91.0 %collective-permute-start.3 = (bf16[64,640]{0,1:T(8,128)(2,1)S(1)}, bf16[64,640]{0,1:T(8,128)(2,1)}, u32[]{:S(2)}, u32[]{:S(2)}) collective-permute-start(bf16[64,640]{0,1:T(8,128)(2,1)S(1)} %get-tuple-element.359), channel_id=1, source_target_pairs={{2,0},{4,2},{6,4},{8,6},{10,8},{12,10},{14,12},{16,14},{18,16},{20... | collective-permute-start | bytes 245768 | tf_op jit(solution)/shard_map/ppermute | solution.py:24
  233.0 90.5 %collective-permute-start.2 = (bf16[64,640]{0,1:T(8,128)(2,1)S(1)}, bf16[64,640]{0,1:T(8,128)(2,1)S(1)}, u32[]{:S(2)}, u32[]{:S(2)}) collective-permute-start(bf16[64,640]{0,1:T(8,128)(2,1)S(1)} %get-tuple-element.360), channel_id=1, source_target_pairs={{0,2},{2,4},{4,6},{6,8},{8,10},{10,12},{12,14},{14,16},{16,18},{18... | collective-permute-start | bytes 245768 | tf_op jit(solution)/shard_map/ppermute | solution.py:21
  271.9 50.3 %collective-permute-start.1 = (bf16[64,640]{0,1:T(8,128)(2,1)S(1)}, bf16[64,640]{0,1:T(8,128)(2,1)}, u32[]{:S(2)}, u32[]{:S(2)}) collective-permute-start(bf16[64,640]{0,1:T(8,128)(2,1)S(1)} %get-tuple-element.357), channel_id=1, source_target_pairs={{2,0},{4,2},{6,4},{8,6},{10,8},{12,10},{14,12},{16,14},{18,16},{20... | collective-permute-start | bytes 245768 | tf_op jit(solution)/shard_map/ppermute | solution.py:24
  274.7 42.3 %copy-start.3 = (bf16[2048,640]{0,1:T(8,128)(2,1)S(1)}, bf16[2048,640]{0,1:T(8,128)(2,1)}, u32[]{:S(2)}) copy-start(bf16[2048,640]{0,1:T(8,128)(2,1)} %all-gather.12.cloned.1.call-done) | copy-start | bytes 7864324
  274.8 44.5 %collective-permute-start = (bf16[64,640]{0,1:T(8,128)(2,1)}, bf16[64,640]{0,1:T(8,128)(2,1)S(1)}, u32[]{:S(2)}, u32[]{:S(2)}) collective-permute-start(bf16[64,640]{0,1:T(8,128)(2,1)} %get-tuple-element.358), channel_id=1, source_target_pairs={{0,2},{2,4},{4,6},{6,8},{8,10},{10,12},{12,14},{14,16},{16,18},{18... | collective-permute-start | bytes 245768 | tf_op jit(solution)/shard_map/ppermute | solution.py:21
  322.2 9.1 copy-start.11
  323.4 11.6 copy-start.9
  335.0 49.6 %copy-start.17 = (bf16[320,1280]{0,1:T(8,128)(2,1)S(1)}, bf16[320,1280]{0,1:T(8,128)(2,1)}, u32[]{:S(2)}) copy-start(bf16[320,1280]{0,1:T(8,128)(2,1)} %all_gather.34) | copy-start | bytes 2457604
  335.0 49.6 %copy-start.58 = (f32[320]{0:T(512)S(1)}, f32[320]{0:T(512)}, u32[]{:S(2)}) copy-start(f32[320]{0:T(512)} %param.56) | copy-start | bytes 3844
  335.0 49.6 %copy-start.59 = (f32[320]{0:T(512)S(1)}, f32[320]{0:T(512)}, u32[]{:S(2)}) copy-start(f32[320]{0:T(512)} %param.57) | copy-start | bytes 3844
  590.3 183.1 %reduce-scatter.18.cloned.1.call-start = ((), (), s32[]{:S(2)}) async-start(), calls=%async_computation.18 | async-start | bytes 8355840 | tf_op jit(solution)/shard_map/reduce_scatter | solution.py:48
  703.0 168.6 %reduce-scatter.24.cloned.1.call-start = ((), (), s32[]{:S(2)}) async-start(), calls=%async_computation.23 | async-start | bytes 8355840 | tf_op jit(solution)/shard_map/reduce_scatter | solution.py:212
  731.0 265.7 %reduce-scatter.12.cloned.1.call-start = ((), (), s32[]{:S(2)}) async-start(), calls=%async_computation.15 | async-start | bytes 15728640 | tf_op jit(solution)/shard_map/reduce_scatter | solution.py:48
  738.2 382.5 %reduce-scatter.10.cloned.1.call-start = ((), (), s32[]{:S(2)}) async-start(), calls=%async_computation.12 | async-start | bytes 15728640 | tf_op jit(solution)/shard_map/reduce_scatter | solution.py:48
  745.1 499.9 %reduce-scatter.20.cloned.1.call-start = ((), (), s32[]{:S(2)}) async-start(), calls=%async_computation.19 | async-start | bytes 15728640 | tf_op jit(solution)/shard_map/reduce_scatter | solution.py:48
  747.1 35.2 %copy-start.13 = (f32[2176,320]{0,1:T(8,128)S(1)}, f32[2176,320]{0,1:T(8,128)}, u32[]{:S(2)}) copy-start(f32[2176,320]{0,1:T(8,128)} %reduce-scatter.14.cloned.1.call-done) | copy-start | bytes 8355844
  747.2 39.6 %collective-permute-start.4 = (bf16[64,320]{0,1:T(8,128)(2,1)S(1)}, bf16[64,320]{0,1:T(8,128)(2,1)S(1)}, u32[]{:S(2)}, u32[]{:S(2)}) collective-permute-start(bf16[64,320]{0,1:T(8,128)(2,1)S(1)} %get-tuple-element.361), channel_id=1, source_target_pairs={{0,2},{2,4},{4,6},{6,8},{8,10},{10,12},{12,14},{14,16},{16,18},{18... | collective-permute-start | bytes 122888 | tf_op jit(solution)/shard_map/ppermute | solution.py:21
  749.2 37.6 %collective-permute-start.5 = (bf16[64,320]{0,1:T(8,128)(2,1)S(1)}, bf16[64,320]{0,1:T(8,128)(2,1)}, u32[]{:S(2)}, u32[]{:S(2)}) collective-permute-start(bf16[64,320]{0,1:T(8,128)(2,1)S(1)} %get-tuple-element.362), channel_id=1, source_target_pairs={{2,0},{4,2},{6,4},{8,6},{10,8},{12,10},{14,12},{16,14},{18,16},{20... | collective-permute-start | bytes 122888 | tf_op jit(solution)/shard_map/ppermute | solution.py:24
  775.5 18.2 %collective-permute-start.6 = (bf16[64,320]{0,1:T(8,128)(2,1)S(1)}, bf16[64,320]{0,1:T(8,128)(2,1)S(1)}, u32[]{:S(2)}, u32[]{:S(2)}) collective-permute-start(bf16[64,320]{0,1:T(8,128)(2,1)S(1)} %get-tuple-element.363), channel_id=1, source_target_pairs={{0,2},{2,4},{4,6},{6,8},{8,10},{10,12},{12,14},{14,16},{16,18},{18... | collective-permute-start | bytes 122888 | tf_op jit(solution)/shard_map/ppermute | solution.py:21
  777.4 7.1 copy-start.14
  777.4 16.2 %collective-permute-start.7 = (bf16[64,320]{0,1:T(8,128)(2,1)S(1)}, bf16[64,320]{0,1:T(8,128)(2,1)S(1)}, u32[]{:S(2)}, u32[]{:S(2)}) collective-permute-start(bf16[64,320]{0,1:T(8,128)(2,1)S(1)} %get-tuple-element.364), channel_id=1, source_target_pairs={{2,0},{4,2},{6,4},{8,6},{10,8},{12,10},{14,12},{16,14},{18,16},{20... | collective-permute-start | bytes 122888 | tf_op jit(solution)/shard_map/ppermute | solution.py:24
  786.8 12.8 copy-start.7
  786.8 12.8 copy-start.28
  786.8 12.8 copy-start.30
  786.8 12.8 copy-start.32
  786.8 12.8 copy-start.34
  799.6 16.3 %copy-start.50 = (f32[320]{0:T(512)S(1)}, f32[320]{0:T(512)}, u32[]{:S(2)}) copy-start(f32[320]{0:T(512)} %param.52) | copy-start | bytes 3844
  815.9 7.3 copy-start.15
  828.8 540.8 %reduce-scatter.16.cloned.1.call-start = ((), (), s32[]{:S(2)}) async-start(), calls=%async_computation.17 | async-start | bytes 15728640 | tf_op jit(solution)/shard_map/reduce_scatter | solution.py:48
  836.0 6.3 copy-start.20
  836.1 631.4 %reduce-scatter.26.cloned.1.call-start = ((), (), s32[]{:S(2)}) async-start(), calls=%async_computation.24 | async-start | bytes 2088960 | tf_op jit(solution)/shard_map/reduce_scatter | solution.py:213
  849.3 24.1 %copy-start.26 = (bf16[2048,320]{0,1:T(8,128)(2,1)S(1)}, bf16[2048,320]{0,1:T(8,128)(2,1)}, u32[]{:S(2)}) copy-start(bf16[2048,320]{0,1:T(8,128)(2,1)} %get-tuple-element.402) | copy-start | bytes 3932164
  849.3 649.0 %reduce-scatter.22.cloned.1.call-start = ((), (), s32[]{:S(2)}) async-start(), calls=%async_computation.22 | async-start | bytes 2088960 | tf_op jit(solution)/shard_map/reduce_scatter | solution.py:211
  878.4 491.2 %copy-start.36 = (f32[2048]{0:T(1024)S(1)}, f32[2048]{0:T(1024)}, u32[]{:S(2)}) copy-start(f32[2048]{0:T(1024)} %copy-done.35) | copy-start | bytes 24580
  878.4 491.2 %copy-start.38 = (f32[2048]{0:T(1024)S(1)}, f32[2048]{0:T(1024)}, u32[]{:S(2)}) copy-start(f32[2048]{0:T(1024)} %copy-done.37) | copy-start | bytes 24580
  878.4 491.2 %copy-start.40 = (f32[2048]{0:T(1024)S(1)}, f32[2048]{0:T(1024)}, u32[]{:S(2)}) copy-start(f32[2048]{0:T(1024)} %copy-done.39) | copy-start | bytes 24580
  878.4 491.2 %copy-start.42 = (f32[2048]{0:T(1024)S(1)}, f32[2048]{0:T(1024)}, u32[]{:S(2)}) copy-start(f32[2048]{0:T(1024)} %copy-done.41) | copy-start | bytes 24580
  878.4 491.2 %copy-start.48 = (f32[640]{0:T(1024)S(1)}, f32[640]{0:T(1024)}, u32[]{:S(2)}) copy-start(f32[640]{0:T(1024)} %param.48) | copy-start | bytes 7684
  878.4 491.2 %copy-start.53 = (f32[640]{0:T(1024)S(1)}, f32[640]{0:T(1024)}, u32[]{:S(2)}) copy-start(f32[640]{0:T(1024)} %param.49) | copy-start | bytes 7684
  878.5 491.2 %copy-start.57 = (f32[640]{0:T(1024)S(1)}, f32[640]{0:T(1024)}, u32[]{:S(2)}) copy-start(f32[640]{0:T(1024)} %param.59) | copy-start | bytes 7684
  1447.3 5.2 slice-start
  1447.3 5.2 slice-start.1
  1447.3 7.1 copy-start.8
  (29 other events, 77.9 us)
Sparse Core Ops, SparseCore 0:
  31.4 68.6 all-gather.15
  102.2 68.5 all-gather.9
  189.2 39.9 all-gather.17
  231.1 39.0 all-gather.11
  272.2 41.6 all-gather.13
  315.3 69.2 all-gather.21
  386.1 68.5 all-gather.19
  590.5 70.1 reduce-scatter.13
  703.1 70.3 reduce-scatter.17
  777.3 94.1 reduce-scatter.23
  873.9 122.8 reduce-scatter.11
  998.9 121.8 reduce-scatter.9
  1123.1 121.8 reduce-scatter.19
  1247.7 121.8 reduce-scatter.15
  1373.7 60.1 reduce-scatter.25
  1438.1 60.1 reduce-scatter.21
where the time goes:
time: 1520 us; the launch traced here: 1510 us
  waiting for transfers between devices  850 us (56%)
  local copies, waits for them, and re-layouts  213 us (14%)
  matrix products  165 us (11%)
  blocking collectives  140 us (9%)
  other arithmetic  96 us (6%)
  starting transfers between devices  24.7 us (2%)
  between operations  15.8 us (1%)
    reduce_scatter x6, waiting for transfers between devices, channel_share(): return lax.psum_scatter(value, 'ch', scatter_dimension=1, tiled=True)  504 us
    all_gather x6, waiting for transfers between devices, channel_whole(): return lax.all_gather(value, 'ch', axis=1, tiled=True)  257 us
    scatter-add x8, local copies, waits for them, and re-layouts, body(): spread_gradient = spread_gradient.at[tap_index * DILATION_STEP:tap_index...  169 us
    dot_general x14, matrix products, inner_cols(): lax.dot_general(left, right, (((1,), (1,)), ((), ())), preferred_element_...  82.8 us
    psum x1, blocking collectives, body(): totals = lax.psum(small_sums, 'seq')  50.6 us
    psum x6, blocking collectives, row_sums(): return lax.psum((jnp.sum(first, axis=1), jnp.sum(second, axis=1)), 'ch')  47.4 us
    dot_general x14, matrix products, hidden_rows(): lax.dot_general(left, right, (((0,), (0,)), ((), ())), preferred_element_...  39.7 us
    all_gather x1, waiting for transfers between devices, body(): lax.all_gather(conv_weight, 'seq', axis=1, tiled=True)  36.7 us
  transfers between devices with their start and end apart: 24, of which 14 were waited for; matrix products, arithmetic and copies ran while one was open for 21% of the time, Pallas kernels for 0%

commit v1 on v0

v1 whole, which is shorter than its diff:
```python
import jax
import jax.numpy as jnp
from jax import lax
from jax.sharding import PartitionSpec as P

KERNEL_TAPS = 5
DILATION_STEP = 32
HALO = 64

EPSILON = 1e-05
ROOT_HALF = 0.7071067811865476
ROOT_TAU = 0.3989422804014327
SWAP = [(0, 1), (1, 0)]


def gelu_both(value):
    half = 0.5 * (1.0 + lax.erf(value * ROOT_HALF))
    return value * half, half + value * jnp.exp(-0.5 * value * value) * ROOT_TAU


def norm(value, gain, shift):
    middle = jnp.mean(value, axis=1, keepdims=True)
    centred = value - middle
    scale = lax.rsqrt(jnp.mean(centred * centred, axis=1, keepdims=True) + EPSILON)
    normed = centred * scale
    return normed, scale, normed * gain + shift


def norm_back(grad_zed, normed, scale, gain):
    grad_normed = grad_zed * gain
    first = jnp.mean(grad_normed, axis=1, keepdims=True)
    second = jnp.mean(grad_normed * normed, axis=1, keepdims=True)
    grad_value = scale * (grad_normed - first - normed * second)
    return grad_value, jnp.sum(grad_zed * normed, axis=0), jnp.sum(grad_zed, axis=0)


def dot(left, right, over=((1,), (0,))):
    return lax.dot_general(left, right, (over, ((), ())), preferred_element_type=jnp.float32)


def framed(block, width):
    count = lax.axis_size("seq")
    forward = [(i, i + 1) for i in range(count - 1)]
    backward = [(i + 1, i) for i in range(count - 1)]
    low = lax.ppermute(block[block.shape[0] - width :], "seq", forward)
    high = lax.ppermute(block[:width], "seq", backward)
    return jnp.concatenate([low, block, high], axis=0)


def windows(block, taps, rows):
    return jnp.concatenate(
        [
            block[tap * DILATION_STEP : tap * DILATION_STEP + rows] * taps[tap]
            for tap in range(KERNEL_TAPS)
        ],
        axis=1,
    )


def body(
    tokens,
    cotangent,
    seq_lengths,
    residue_mask,
    first_gain,
    first_shift,
    proj_in,
    in_bias,
    mid_gain,
    mid_shift,
    conv_weight,
    conv_bias,
    last_gain,
    last_shift,
    proj_out,
    out_bias,
):
    micro, rows, half = tokens.shape
    inner_half = in_bias.shape[0]
    inner = 2 * inner_half
    side = lax.axis_index("ch")
    low_side = side == 0

    def swap(value):
        return lax.ppermute(value, "ch", SWAP)

    def whole(own, other, axis):
        return jnp.where(
            low_side,
            jnp.concatenate([own, other], axis=axis),
            jnp.concatenate([other, own], axis=axis),
        )

    def own_of(value):
        return lax.dynamic_index_in_dim(value, side, 0, keepdims=False)

    def other_of(value):
        return lax.dynamic_index_in_dim(value, 1 - side, 0, keepdims=False)

    def halves(value, width):
        left, right = value[:, :width], value[:, width:]
        return jnp.where(low_side, left, right), jnp.where(low_side, right, left)

    weight_in = lax.all_gather(whole(proj_in, swap(proj_in), 1), "seq", axis=0, tiled=True)
    weight_conv = lax.all_gather(whole(conv_weight, swap(conv_weight), 2), "seq", axis=1, tiled=True)
    weight_out = lax.all_gather(whole(proj_out, swap(proj_out), 0), "seq", axis=1, tiled=True)
    vectors = lax.all_gather(
        jnp.concatenate(
            [first_gain, first_shift, out_bias, in_bias, mid_gain, mid_shift, conv_bias, last_gain, last_shift]
        ),
        "ch",
        axis=0,
        tiled=False,
    )
    wide = [vectors[:, i * half : (i + 1) * half].reshape(-1) for i in range(3)]
    narrow = [
        vectors[:, 3 * half + i * inner_half : 3 * half + (i + 1) * inner_half].reshape(-1) for i in range(6)
    ]
    g1, b1, bias_out = wide
    bias_in, g2, b2, bias_conv, g3, b3 = narrow

    x = whole(own_of(tokens), swap(other_of(tokens)), 1).astype(jnp.float32)
    gy = whole(own_of(cotangent), swap(other_of(cotangent)), 1)

    places = lax.axis_index("seq") * rows + jnp.arange(rows + 2 * HALO, dtype=jnp.int32) - HALO
    inside = (places >= 0) & (places < rows * lax.axis_size("seq"))
    bounds = jnp.cumsum(own_of(seq_lengths))[:-1]
    segment = jnp.sum((places[:, None] >= bounds[None, :]).astype(jnp.int32), axis=1)
    segment = jnp.where(inside, segment, -1)
    middle = segment[HALO : HALO + rows]
    taps = [
        (segment[tap * DILATION_STEP : tap * DILATION_STEP + rows] == middle).astype(jnp.bfloat16)[:, None]
        for tap in range(KERNEL_TAPS)
    ]
    keep = own_of(residue_mask).astype(jnp.float32)[:, None]

    n1, r1, z1 = norm(x, g1, b1)
    a1, s1 = gelu_both(z1)
    a1 = a1.astype(jnp.bfloat16)
    h1 = dot(a1, weight_in) + bias_in
    n2, r2, z2 = norm(h1, g2, b2)
    a2, s2 = gelu_both(z2)
    a2 = framed((a2 * keep).astype(jnp.bfloat16), HALO)
    s2 = s2 * keep
    a_win = windows(a2, taps, rows)
    h3 = dot(a_win, weight_conv.reshape(KERNEL_TAPS * inner, inner)) + bias_conv
    n3, r3, z3 = norm(h3, g3, b3)
    a3, s3 = gelu_both(z3)
    a3 = a3.astype(jnp.bfloat16)
    out = (x + dot(a3, weight_out) + bias_out).astype(jnp.bfloat16)
    out_own, out_other = halves(out, half)
    out_back = swap(out_other)

    grad_out = dot(a3, gy, ((0,), (0,)))
    da3 = dot(gy, weight_out, ((1,), (1,)))
    dh3, grad_g3, grad_b3 = norm_back(da3 * s3, n3, r3, g3)
    dh3 = dh3.astype(jnp.bfloat16)
    d_win = windows(framed(dh3, HALO), taps, rows)
    grad_conv = dot(a_win, dh3, ((0,), (0,))).reshape(KERNEL_TAPS, inner, inner)
    flipped = jnp.flip(weight_conv, 0).transpose(0, 2, 1).reshape(KERNEL_TAPS * inner, inner)
    da2 = dot(d_win, flipped)
    dh1, grad_g2, grad_b2 = norm_back(da2 * s2, n2, r2, g2)
    dh1 = dh1.astype(jnp.bfloat16)
    grad_in = dot(a1, dh1, ((0,), (0,)))
    da1 = dot(dh1, weight_in, ((1,), (1,)))
    dx, grad_g1, grad_b1 = norm_back(da1 * s1, n1, r1, g1)
    dx_own, dx_other = halves(dx, half)
    dx_back = swap(dx_other.astype(jnp.bfloat16))

    def placed(own, back):
        return jnp.where(low_side, jnp.stack([own, back], 0), jnp.stack([back, own], 0))

    block_out = placed(out_own, out_back)
    grad_tokens = placed(dx_own, dx_back.astype(jnp.float32)) + cotangent.astype(jnp.float32)

    def owned(value, seq_dim, ch_dim):
        part = lax.psum_scatter(value, "seq", scatter_dimension=seq_dim, tiled=True)
        return lax.psum_scatter(part, "ch", scatter_dimension=ch_dim, tiled=True)

    smalls = [
        grad_g1,
        grad_b1,
        jnp.sum(gy.astype(jnp.float32), axis=0),
        jnp.sum(dh1.astype(jnp.float32), axis=0),
        grad_g2,
        grad_b2,
        jnp.sum(dh3.astype(jnp.float32), axis=0),
        grad_g3,
        grad_b3,
    ]
    totals = lax.psum(jnp.concatenate([small.reshape(2, -1) for small in smalls], axis=1), ("seq", "ch"))
    totals = lax.dynamic_index_in_dim(totals, side, 0, keepdims=False)
    sizes = [half] * 3 + [inner_half] * 6
    parts = []
    at = 0
    for size in sizes:
        parts.append(totals[at : at + size])
        at += size
    return (
        block_out,
        grad_tokens,
        parts[0],
        parts[1],
        owned(grad_in, 0, 1),
        parts[3],
        parts[4],
        parts[5],
        owned(grad_conv, 1, 2),
        parts[6],
        parts[7],
        parts[8],
        owned(grad_out, 1, 0),
        parts[2],
    )


def solution(mesh):
    placed = (
        P(None, "seq", "ch"),
        P(None, "seq", "ch"),
        P(),
        P(None, "seq"),
        P("ch"),
        P("ch"),
        P("seq", "ch"),
        P("ch"),
        P("ch"),
        P("ch"),
        P(None, "seq", "ch"),
        P("ch"),
        P("ch"),
        P("ch"),
        P("ch", "seq"),
        P("ch"),
    )
    return jax.shard_map(
        body,
        mesh=mesh,
        in_specs=placed,
        out_specs=(
            P(None, "seq", "ch"),
            P(None, "seq", "ch"),
            P("ch"),
            P("ch"),
            P("seq", "ch"),
            P("ch"),
            P("ch"),
            P("ch"),
            P(None, "seq", "ch"),
            P("ch"),
            P("ch"),
            P("ch"),
            P("ch", "seq"),
            P("ch"),
        ),
        check_vma=False,
    )
```

time: 1520 us -> 584 us (0.38)
  waiting for transfers between devices: 850 us -> 65.5 us
  local copies, waits for them, and re-layouts: 213 us -> 52.2 us
  blocking collectives: 140 us -> 226 us
  matrix products: 165 us -> 99.2 us
    reduce_scatter x9 -> x3, waiting for transfers between devices: 553 us -> 13.5 us  [owned(): part = lax.psum_scatter(value, 'seq', scatter_dimension=seq_dim, tiled=True)]
    all_gather x7 -> x3, waiting for transfers between devices: 294 us -> 18.7 us  [the longest x1 18.6 us: body(): lax.all_gather(whole(proj_out, swap(proj_out), 0), 'seq', axis=1, tiled=T...]
    scatter-add x12 -> x0, local copies, waits for them, and re-layouts: 176 us -> none  [the longest x8 169 us: body(): spread_gradient = spread_gradient.at[tap_index * DILATION_STEP:tap_index...]
    all_gather x2 -> x1, blocking collectives: 42 us -> 109 us  [body(): lax.all_gather(jnp.concatenate([first_gain, first_shift, out_bias, in_bia...]
    dot_general x42 -> x9, matrix products: 165 us -> 99.2 us  [dot(): lax.dot_general(left, right, (over, ((), ())), preferred_element_type=jnp...]
    reduce_sum x7, other arithmetic: 49.5 us -> 22.6 us  [the longest x3 7.77 us: norm(): jnp.mean(centred * centred, axis=1, keepdims=True) + EPSILON]
    unnamed x16 -> x12, waiting for transfers between devices: 2.64 us -> 29.5 us
    psum x7 -> x1, blocking collectives: 98 us -> 117 us  [body(): lax.psum(jnp.concatenate([small.reshape(2, -1) for small in smalls], axis...]
  transfers between devices with their start and end apart: 24 -> 20, of which waited for: 14 -> 6; matrix products, arithmetic and copies ran while one was open for 21% -> 38% of each run, Pallas kernels for 0% -> 0%
where the time goes in v1:
time: 584 us; the launch traced here: 574 us
  blocking collectives  226 us (39%)
  matrix products  99.2 us (17%)
  other arithmetic  93.9 us (16%)
  waiting for transfers between devices  65.5 us (11%)
  local copies, waits for them, and re-layouts  52.2 us (9%)
  starting transfers between devices  22.2 us (4%)
  between operations  15.2 us (3%)
    psum x1, blocking collectives, body(): lax.psum(jnp.concatenate([small.reshape(2, -1) for small in smalls], axis...  117 us
    all_gather x1, blocking collectives, body(): lax.all_gather(jnp.concatenate([first_gain, first_shift, out_bias, in_bia...  109 us
    dot_general x9, matrix products, dot(): lax.dot_general(left, right, (over, ((), ())), preferred_element_type=jnp...  99.2 us
    unnamed x12, waiting for transfers between devices  29.5 us
    unnamed x105, local copies, waits for them, and re-layouts  27.1 us
    all_gather x1, waiting for transfers between devices, body(): lax.all_gather(whole(proj_out, swap(proj_out), 0), 'seq', axis=1, tiled=T...  18.6 us
    unnamed x11, other arithmetic  15.3 us
    reduce_scatter x3, waiting for transfers between devices, owned(): part = lax.psum_scatter(value, 'seq', scatter_dimension=seq_dim, tiled=True)  13.5 us
  transfers between devices with their start and end apart: 20, of which 6 were waited for; matrix products, arithmetic and copies ran while one was open for 38% of the time, Pallas kernels for 0%

profile of v1, /device:TPU:24, one launch (start us, length us, event | category | flops | bytes accessed | tf_op | source)
XLA Modules:
  0.0 574.1 jit_solution(5747134058690787830)
XLA Ops:
  7.2 1.6 collective-permute-start.1
  8.8 2.9 collective-permute-done.1
  11.7 1.7 maximum_select_fusion.5
  13.5 4.5 dynamic-slice_bitcast_fusion.2
  18.1 1.6 collective-permute-start
  20.2 1.5 collective-permute-start.4
  21.7 5.4 dynamic-slice_bitcast_fusion.1
  27.8 109.2 %all-gather.1 = f32[2,1,3840]{2,1,0:T(1,128)S(1)} all-gather(f32[1,1,3840]{2,1,0:T(1,128)S(1)} %reshape.180), channel_id=2, replica_groups=mesh['seq'=16,'ch'=2] {'ch'}, dimensions={0}, use_global_device_ids=true | all-gather | bytes 46080 | tf_op jit(solution)/shard_map/all_gather | solution.py:107
  139.8 4.5 convert_reduce_fusion
  144.3 5.5 fusion.21
  149.9 9.6 %fusion.13 = bf16[2048,1280]{1,0:T(8,128)(2,1)} fusion(f32[1280]{0:T(1024)S(1)} %add.159, f32[1280]{0:T(1024)S(1)} %mul.309, f32[2048]{0:T(1024)S(1)} %add_rsqrt_fusion.2, f32[2048]{0:T(1024)S(1)} %broadcast_multiply_fusion.8, bf16[2048,640]{1,0:T(8,128)(2,1)S(1)} %get-tuple-element.45, bf16[2048,640]{1,0:T(8,128)(2,1)} %collective-permute-done, pred[]{:T(512)S(6)} %eq.16), kind=kLoop, calls=%fused_computation.17 | loop fusion | flops 49807360 | bytes 10512385 | tf_op jit(solution)/shard_map/convert_element_type | solution.py:139
  159.6 6.9 %add_reduce_fusion.1 = (f32[2048]{0:T(1024)S(1)}, f32[2048,640]{1,0:T(8,128)S(1)}) fusion(f32[640]{0:T(1024)S(1)} %add.164, bf16[2048,1280]{1,0:T(8,128)(2,1)} %fusion.13, bf16[1280,640]{1,0:T(8,128)(2,1)} %all-gather.6.cloned.1.call-done), kind=kOutput, calls=%fused_computation.72 | convolution fusion | flops 3358062592 | bytes 12134912 | tf_op jit(solution)/shard_map/dot_general | solution.py:38
  166.5 1.1 multiply_reduce_fusion.6
  167.7 3.0 multiply_convert_fusion.3
  170.7 1.9 collective-permute-start.2
  173.5 5.0 collective-permute-start.3
  179.3 3.3 fusion.48
  182.7 2.3 fusion.56
  185.0 3.7 constant_dynamic-update-slice_fusion
  188.7 2.3 fusion.45
  191.0 2.2 fusion.54
  193.3 15.0 %add_reduce_fusion = (f32[2048]{0:T(1024)S(1)}, f32[2048,640]{1,0:T(8,128)S(1)}) fusion(f32[640]{0:T(1024)S(1)} %add.174, bf16[2048,3200]{1,0:T(8,128)(2,1)} %fusion.54, bf16[3200,640]{1,0:T(8,128)(2,1)} %bitcast.59), kind=kOutput, calls=%fused_computation.71 | convolution fusion | flops 8391227392 | bytes 22456832 | tf_op jit(solution)/shard_map/dot_general | solution.py:38
  208.3 2.6 copy-done.8
  211.0 1.1 multiply_reduce_fusion.5
  212.1 18.6 %all-gather.10.cloned.1.call-done = bf16[640,1280]{0,1:T(8,128)(2,1)} async-done(((bf16[640,80]{0,1:T(8,128)(2,1)}), bf16[640,1280]{0,1:T(8,128)(2,1)}) %all-gather.10.cloned.1.call-update) | async-done | bytes 1638416 | tf_op jit(solution)/shard_map/all_gather | solution.py:106
  230.8 10.5 %multiply_reduce_fusion.1 = (f32[640]{0:T(1024)S(1)}, f32[2048]{0:T(1024)S(1)}, f32[2048]{0:T(1024)S(1)}, f32[640]{0:T(1024)S(1)}, f32[2048,640]{1,0:T(8,128)S(1)}) fusion(f32[2048]{0:T(1024)S(1)} %add_rsqrt_fusion, f32[2048]{0:T(1024)S(1)} %broadcast_multiply_fusion.4, f32[2048,640]{1,0:T(8,128)} %copy-done.8, f32[640]{0:T(1024)S(1)} %add.174, ...), kind=kOutput, calls=%fused_computation.49 | convolution fusion | flops 3406556160 | bytes 17412608 | tf_op jit(solution)/shard_map/dot_general | solution.py:38
  241.3 3.7 convert_reduce_fusion.2
  245.1 2.6 collective-permute-start.8
  247.7 8.8 %fusion.62 = f32[640,1280]{0,1:T(8,128)} fusion(bf16[2048,640]{1,0:T(8,128)(2,1)S(1)} %get-tuple-element.39, bf16[2048,640]{1,0:T(8,128)(2,1)} %collective-permute-done.7, bf16[2048,640]{1,0:T(8,128)(2,1)S(1)} %copy-done.11, pred[]{:T(512)S(6)} %eq.16), kind=kOutput, calls=%fused_computation.155 | convolution fusion | flops 3379036160 | bytes 11141121 | tf_op jit(solution)/shard_map/dot_general | solution.py:38
  256.4 4.4 reverse_bitcast_fusion
  260.9 7.8 %copy.40 = bf16[5,640,640]{2,1,0:T(8,128)(2,1)} copy(bf16[5,640,640]{1,2,0:T(8,128)(2,1)} %reverse_bitcast_fusion) | data formatting | bytes 8192000 | tf_op jit(solution)/shard_map/transpose | solution.py:160
  268.8 4.3 collective-permute-start.9
  273.7 1.4 fusion.52
  275.7 1.5 fusion.39
  277.2 1.7 fusion.50
  279.4 13.9 %multiply_reduce_fusion.2 = (f32[640]{0:T(1024)S(1)}, f32[2048]{0:T(1024)S(1)}, f32[2048]{0:T(1024)S(1)}, f32[640]{0:T(1024)S(1)}, f32[2048,640]{1,0:T(8,128)S(1)}) fusion(f32[2048]{0:T(1024)S(1)} %add_rsqrt_fusion.1, f32[2048]{0:T(1024)S(1)} %broadcast_multiply_fusion.5, f32[2048,640]{1,0:T(8,128)S(1)} %bitcast.51, f32[640]{0:T(1024)S(1)} %add.164, ...), kind=kOutput, calls=%fused_computation.51 | convolution fusion | flops 8417438720 | bytes 27742720 | tf_op jit(solution)/shard_map/dot_general | solution.py:38
  293.3 2.1 convert_reduce_fusion.3
  295.5 1.5 copy-done.16
  296.9 6.0 %fusion.67 = f32[1280,640]{1,0:T(8,128)} fusion(bf16[2048,1280]{1,0:T(8,128)(2,1)S(1)} %bitcast.58, bf16[2048,640]{1,0:T(8,128)(2,1)S(1)} %get-tuple-element.38), kind=kOutput, calls=%fused_computation.160 | convolution fusion | flops 3355443200 | bytes 11141120 | tf_op jit(solution)/shard_map/dot_general | solution.py:38
  303.0 16.0 %fusion.68 = f32[3200,640]{1,0:T(8,128)} fusion(bf16[2048,3200]{1,0:T(8,128)(2,1)} %fusion.54, bf16[2048,640]{1,0:T(8,128)(2,1)S(1)} %get-tuple-element.36), kind=kOutput, calls=%fused_computation.161 | convolution fusion | flops 8388608000 | bytes 23920640 | tf_op jit(solution)/shard_map/dot_general | solution.py:38
  319.1 1.6 copy-done.7
  320.8 8.3 %fusion.23 = bf16[2048,1280]{1,0:T(8,128)(2,1)S(1)} fusion(bf16[2048,640]{1,0:T(8,128)(2,1)} %copy-done.15, bf16[640,1280]{0,1:T(8,128)(2,1)} %all-gather.10.cloned.1.call-done, f32[1280]{0:T(1024)S(1)} %add.183, bf16[2048,640]{1,0:T(8,128)(2,1)S(1)} %copy-done.7, bf16[2048,640]{1,0:T(8,128)(2,1)} %collective-permute-done, pred[]{:T(512)S(6)} %eq.16), kind=kOutput, calls=%fused_computation.27 | convolution fusion | flops 3389521920 | bytes 14750721 | tf_op jit(solution)/shard_map/dot_general | solution.py:38
  329.1 3.2 select_bitcast_fusion.1
  332.3 1.4 collective-permute-start.6
  333.8 13.8 %fusion.20 = (f32[1280]{0:T(1024)S(1)}, f32[2048]{0:T(1024)S(1)}, f32[2048]{0:T(1024)S(1)}, f32[1280]{0:T(1024)S(1)}, f32[2048,1280]{1,0:T(8,128)S(1)}) fusion(f32[2048]{0:T(1024)S(1)} %copy-done.22, f32[2048]{0:T(1024)S(1)} %copy-done.20, bf16[2048,640]{1,0:T(8,128)(2,1)S(1)} %copy-done.7, bf16[2048,640]{1,0:T(8,128)(2,1)} %collective-permute-done, ...), kind=kOutput, calls=%fused_computation.24 | convolution fusion | flops 3434079744 | bytes 20041728 | tf_op jit(solution)/shard_map/dot_general | solution.py:38
  347.6 7.5 %fusion.19 = f32[2048,1280]{1,0:T(8,128)S(1)} fusion(f32[2048,1280]{1,0:T(8,128)S(1)} %get-tuple-element.69, f32[2048]{0:T(1024)S(1)} %broadcast_multiply_fusion.6, f32[2048]{0:T(1024)S(1)} %broadcast_multiply_fusion.7, f32[1280]{0:T(1024)S(1)} %copy-done.24, f32[2048]{0:T(1024)S(1)} %copy-done.22, f32[2048]{0:T(1024)S(1)} %copy-done.20, ...), kind=kLoop, calls=%fused_computation.23 | loop fusion | flops 44564480 | bytes 26252288 | tf_op jit(solution)/shard_map/mul | solution.py:33
  355.1 4.1 copy-done.5
  359.2 2.0 select_convert_fusion
  362.1 4.4 convert_reduce_fusion.1
  367.1 116.6 %psum.7 = f32[2,3840]{1,0:T(2,128)S(1)} all-reduce(f32[2,3840]{1,0:T(2,128)S(1)} %concatenate.77), channel_id=1, replica_groups=mesh['seq'=16,'ch'=2] {'seq','ch'}, use_global_device_ids=true, to_apply=%region_23.24 | all-reduce | flops 7680 | bytes 61440 | tf_op jit(solution)/shard_map/psum | solution.py:191
  485.2 1.8 copy.45
  487.1 7.2 %select_bitcast_fusion = f32[1,2048,640]{2,1,0:T(8,128)} fusion(f32[2048,1280]{1,0:T(8,128)} %copy-done.5, pred[]{:T(512)S(6)} %eq.16), kind=kLoop, calls=%fused_computation.54 | loop fusion | flops 1310720 | bytes 15728641 | tf_op jit(solution)/shard_map/stack | solution.py:171
  494.2 1.8 copy.41
  496.2 6.4 %maximum_select_fusion.2 = bf16[2,2048,640]{2,1,0:T(8,128)(2,1)} fusion(bf16[1,2048,640]{2,1,0:T(8,128)(2,1)} %bitcast.6, bf16[1,2048,640]{2,1,0:T(8,128)(2,1)S(1)} %copy-done.13, pred[]{:T(512)S(6)} %eq.16), kind=kLoop, calls=%fused_computation.47 | loop fusion | flops 7864320 | bytes 10485761 | tf_op jit(solution)/shard_map/jit(_where)/select_n | solution.py:171
  502.6 13.5 %reduce-scatter.15.cloned.1.call-done = f32[5,40,640]{2,1,0:T(8,128)} async-done(((f32[5,640,640]{2,1,0:T(8,128)}), f32[5,40,640]{2,1,0:T(8,128)}) %reduce-scatter.15.cloned.1.call-update) | async-done | bytes 512016 | tf_op jit(solution)/shard_map/reduce_scatter | solution.py:177
  516.1 3.3 copy.43
  519.4 2.8 reshape.185
  522.2 2.2 bitcast_convert_fusion
  525.2 6.8 %fusion.25 = f32[2,2048,640]{2,1,0:T(8,128)} fusion(f32[1,2048,640]{2,1,0:T(8,128)S(1)} %bitcast_convert_fusion, f32[1,2048,640]{2,1,0:T(8,128)S(1)} %bitcast.53, bf16[2,2048,640]{2,1,0:T(8,128)(2,1)} %param.17, pred[]{:T(512)S(6)} %eq.16), kind=kLoop, calls=%fused_computation.30 | loop fusion | flops 13107200 | bytes 26214400 | tf_op jit(solution)/shard_map/add | solution.py:174
  532.0 1.7 copy.46
  533.7 12.8 %reduce-scatter.19.cloned.1.call-done = f32[320,80]{1,0:T(8,128)} async-done(((f32[640,80]{1,0:T(8,128)}), f32[320,80]{1,0:T(8,128)}) %reduce-scatter.19.cloned.1.call-update) | async-done | bytes 102416
  546.5 1.7 copy.42
  548.2 16.6 %reduce-scatter.21.cloned.1.call-done = f32[320,200]{1,0:T(8,128)} async-done(((f32[640,200]{1,0:T(8,128)}), f32[320,200]{1,0:T(8,128)}) %reduce-scatter.21.cloned.1.call-update) | async-done | bytes 256016
  564.8 1.3 reshape.186
  (183 shorter events, 12.5 us)
Async XLA Ops:
  7.2 131.4 %copy-start = (s32[2,128]{1,0:T(2,128)S(1)}, s32[2,128]{1,0:T(2,128)}, u32[]{:S(2)}) copy-start(s32[2,128]{1,0:T(2,128)} %param.18) | copy-start | bytes 3076
  7.2 152.4 %all-gather.6.cloned.1.call-start = ((), (), s32[]{:S(2)}) async-start(), calls=%async_computation.6 | async-start | bytes 1740800 | tf_op jit(solution)/shard_map/all_gather | solution.py:104
  7.2 4.5 collective-permute-start.1
  13.4 179.9 %all-gather.8.cloned.1.call-start = ((), (), s32[]{:S(2)}) async-start(), calls=%async_computation.7 | async-start | bytes 4352000 | tf_op jit(solution)/shard_map/all_gather | solution.py:105
  13.5 6.2 %copy-start.25 = (bf16[320,80]{0,1:T(8,128)(2,1)S(1)}, bf16[320,80]{0,1:T(8,128)(2,1)}, u32[]{:S(2)}) copy-start(bf16[320,80]{0,1:T(8,128)(2,1)} %param.30) | copy-start | bytes 153604
  13.5 6.7 %copy-start.18 = (bf16[5,40,320]{2,1,0:T(8,128)(2,1)S(1)}, bf16[5,40,320]{2,1,0:T(8,128)(2,1)}, u32[]{:S(2)}) copy-start(bf16[5,40,320]{2,1,0:T(8,128)(2,1)} %param.26) | copy-start | bytes 384004
  18.0 131.9 %copy-start.6 = (bf16[2048,640]{1,0:T(8,128)(2,1)}, bf16[2048,640]{1,0:T(8,128)(2,1)S(1)}, u32[]{:S(2)}) copy-start(bf16[2048,640]{1,0:T(8,128)(2,1)S(1)} %get-tuple-element.45) | copy-start | bytes 7864324
  18.0 9.6 %copy-start.28 = (f32[640]{0:T(1024)S(1)}, f32[640]{0:T(1024)}, u32[]{:S(2)}) copy-start(f32[640]{0:T(1024)} %param.20) | copy-start | bytes 7684
  18.0 9.6 %copy-start.29 = (f32[640]{0:T(1024)S(1)}, f32[640]{0:T(1024)}, u32[]{:S(2)}) copy-start(f32[640]{0:T(1024)} %param.21) | copy-start | bytes 7684
  18.0 9.6 %copy-start.30 = (f32[640]{0:T(1024)S(1)}, f32[640]{0:T(1024)}, u32[]{:S(2)}) copy-start(f32[640]{0:T(1024)} %param.31) | copy-start | bytes 7684
  18.0 9.6 %copy-start.32 = (f32[320]{0:T(512)S(1)}, f32[320]{0:T(512)}, u32[]{:S(2)}) copy-start(f32[320]{0:T(512)} %param.23) | copy-start | bytes 3844
  18.0 9.6 %copy-start.33 = (f32[320]{0:T(512)S(1)}, f32[320]{0:T(512)}, u32[]{:S(2)}) copy-start(f32[320]{0:T(512)} %param.24) | copy-start | bytes 3844
  18.1 9.6 %copy-start.34 = (f32[320]{0:T(512)S(1)}, f32[320]{0:T(512)}, u32[]{:S(2)}) copy-start(f32[320]{0:T(512)} %param.25) | copy-start | bytes 3844
  18.1 9.6 %copy-start.35 = (f32[320]{0:T(512)S(1)}, f32[320]{0:T(512)}, u32[]{:S(2)}) copy-start(f32[320]{0:T(512)} %param.27) | copy-start | bytes 3844
  18.1 9.6 %copy-start.36 = (f32[320]{0:T(512)S(1)}, f32[320]{0:T(512)}, u32[]{:S(2)}) copy-start(f32[320]{0:T(512)} %param.28) | copy-start | bytes 3844
  18.1 9.6 %copy-start.37 = (f32[320]{0:T(512)S(1)}, f32[320]{0:T(512)}, u32[]{:S(2)}) copy-start(f32[320]{0:T(512)} %param.29) | copy-start | bytes 3844
  18.1 121.6 %copy-start.31 = (s32[2,2048]{1,0:T(2,128)S(1)}, s32[2,2048]{1,0:T(2,128)}, u32[]{:S(2)}) copy-start(s32[2,2048]{1,0:T(2,128)} %param.19) | copy-start | bytes 49156
  18.1 121.7 %collective-permute-start = (bf16[2048,640]{1,0:T(8,128)(2,1)}, bf16[2048,640]{1,0:T(8,128)(2,1)}, u32[]{:S(2)}, u32[]{:S(2)}) collective-permute-start(bf16[2048,640]{1,0:T(8,128)(2,1)} %get-tuple-element.44), channel_id=1, source_target_pairs={{0,1},{1,0},{2,3},{3,2},{4,5},{5,4},{6,7},{7,6},{8,9},{9,8},{10,11... | collective-permute-start | bytes 7864328 | tf_op jit(solution)/shard_map/ppermute | solution.py:85
  19.7 153.0 %collective-permute-start.5 = (bf16[320,80]{0,1:T(8,128)(2,1)S(1)}, bf16[320,80]{0,1:T(8,128)(2,1)S(1)}, u32[]{:S(2)}, u32[]{:S(2)}) collective-permute-start(bf16[320,80]{0,1:T(8,128)(2,1)S(1)} %copy-done.25), channel_id=1, source_target_pairs={{0,1},{1,0},{2,3},{3,2},{4,5},{5,4},{6,7},{7,6},{8,9},{9,8},{10,11... | collective-permute-start | bytes 153608 | tf_op jit(solution)/shard_map/ppermute | solution.py:85
  20.2 117.3 %collective-permute-start.4 = (bf16[5,40,320]{2,1,0:T(8,128)(2,1)S(1)}, bf16[5,40,320]{2,1,0:T(8,128)(2,1)S(1)}, u32[]{:S(2)}, u32[]{:S(2)}) collective-permute-start(bf16[5,40,320]{2,1,0:T(8,128)(2,1)S(1)} %copy-done.18), channel_id=1, source_target_pairs={{0,1},{1,0},{2,3},{3,2},{4,5},{5,4},{6,7},{7,6},{8,9},{9,8},{10,11... | collective-permute-start | bytes 384008 | tf_op jit(solution)/shard_map/ppermute | solution.py:85
  27.1 185.0 %collective-permute-start.7 = (bf16[2048,640]{1,0:T(8,128)(2,1)}, bf16[2048,640]{1,0:T(8,128)(2,1)}, u32[]{:S(2)}, u32[]{:S(2)}) collective-permute-start(bf16[2048,640]{1,0:T(8,128)(2,1)} %get-tuple-element.41), channel_id=1, source_target_pairs={{0,1},{1,0},{2,3},{3,2},{4,5},{5,4},{6,7},{7,6},{8,9},{9,8},{10,11... | collective-permute-start | bytes 7864328 | tf_op jit(solution)/shard_map/ppermute | solution.py:85
  138.5 92.3 %all-gather.10.cloned.1.call-start = ((), (), s32[]{:S(2)}) async-start(), calls=%async_computation.8 | async-start | bytes 1740800 | tf_op jit(solution)/shard_map/all_gather | solution.py:106
  138.5 11.4 %copy-start.23 = (f32[1280]{0:T(1024)}, f32[1280]{0:T(1024)S(1)}, u32[]{:S(2)}) copy-start(f32[1280]{0:T(1024)S(1)} %mul.309) | copy-start | bytes 15364
  138.6 11.3 %copy-start.26 = (f32[1280]{0:T(1024)}, f32[1280]{0:T(1024)S(1)}, u32[]{:S(2)}) copy-start(f32[1280]{0:T(1024)S(1)} %add.159) | copy-start | bytes 15364
  144.3 5.6 copy-start.19
  149.9 9.6 %copy-start.21 = (f32[2048]{0:T(1024)}, f32[2048]{0:T(1024)S(1)}, u32[]{:S(2)}) copy-start(f32[2048]{0:T(1024)S(1)} %add_rsqrt_fusion.2) | copy-start | bytes 24580
  166.5 4.2 copy-start.2
  170.7 8.6 %collective-permute-start.2 = (bf16[64,640]{1,0:T(8,128)(2,1)S(1)}, bf16[64,640]{1,0:T(8,128)(2,1)S(1)}, u32[]{:S(2)}, u32[]{:S(2)}) collective-permute-start(bf16[64,640]{1,0:T(8,128)(2,1)S(1)} %get-tuple-element.49), channel_id=1, source_target_pairs={{0,2},{2,4},{4,6},{6,8},{8,10},{10,12},{12,14},{14,16},{16,18},{18... | collective-permute-start | bytes 245768 | tf_op jit(solution)/shard_map/ppermute | solution.py:45
  172.7 12.3 %slice-start = ((s8[5242880]{0:T(1024)(128)(4,1)}), s8[1048576]{0:T(1024)(128)(4,1)S(1)}, s32[]{:S(2)}) async-start(s8[5242880]{0:T(1024)(128)(4,1)} %bitcast.48), calls=%async_computation.15 | async-start | bytes 2097152
  173.5 311.7 %reduce-scatter.17.cloned.1.call-start = ((), (), s32[]{:S(2)}) async-start(), calls=%async_computation.11 | async-start | bytes 3481600 | tf_op jit(solution)/shard_map/reduce_scatter | solution.py:177
  173.5 9.2 %copy-start.4 = (bf16[2048,640]{1,0:T(8,128)(2,1)S(1)}, bf16[2048,640]{1,0:T(8,128)(2,1)}, u32[]{:S(2)}) copy-start(bf16[2048,640]{1,0:T(8,128)(2,1)} %copy-done.3) | copy-start | bytes 7864324
  173.5 15.2 %collective-permute-start.3 = (bf16[64,640]{1,0:T(8,128)(2,1)S(1)}, bf16[64,640]{1,0:T(8,128)(2,1)S(1)}, u32[]{:S(2)}, u32[]{:S(2)}) collective-permute-start(bf16[64,640]{1,0:T(8,128)(2,1)S(1)} %get-tuple-element.48), channel_id=1, source_target_pairs={{2,0},{4,2},{6,4},{8,6},{10,8},{12,10},{14,12},{16,14},{18,16},{20... | collective-permute-start | bytes 245768 | tf_op jit(solution)/shard_map/ppermute | solution.py:46
  179.3 5.6 slice-start.1
  208.3 2.7 copy-start.8
  208.3 22.4 %copy-start.10 = (bf16[2048,640]{1,0:T(8,128)(2,1)S(1)}, bf16[2048,640]{1,0:T(8,128)(2,1)}, u32[]{:S(2)}) copy-start(bf16[2048,640]{1,0:T(8,128)(2,1)} %get-tuple-element.40) | copy-start | bytes 7864324
  230.8 10.5 %copy-start.9 = (f32[2048,640]{1,0:T(8,128)S(1)}, f32[2048,640]{1,0:T(8,128)}, u32[]{:S(2)}) copy-start(f32[2048,640]{1,0:T(8,128)} %copy-done.8) | copy-start | bytes 15728644
  241.3 6.4 %copy-start.11 = (bf16[2048,640]{1,0:T(8,128)(2,1)S(1)}, bf16[2048,640]{1,0:T(8,128)(2,1)}, u32[]{:S(2)}) copy-start(bf16[2048,640]{1,0:T(8,128)(2,1)} %get-tuple-element.40) | copy-start | bytes 7864324
  245.0 2.6 copy-start.15
  245.1 28.0 %collective-permute-start.8 = (bf16[64,640]{1,0:T(8,128)(2,1)S(1)}, bf16[64,640]{1,0:T(8,128)(2,1)S(1)}, u32[]{:S(2)}, u32[]{:S(2)}) collective-permute-start(bf16[64,640]{1,0:T(8,128)(2,1)S(1)} %get-tuple-element.47), channel_id=1, source_target_pairs={{0,2},{2,4},{4,6},{6,8},{8,10},{10,12},{12,14},{14,16},{16,18},{18... | collective-permute-start | bytes 245768 | tf_op jit(solution)/shard_map/ppermute | solution.py:45
  268.7 225.5 %reduce-scatter.13.cloned.1.call-start = ((), (), s32[]{:S(2)}) async-start(), calls=%async_computation.9 | async-start | bytes 3481600 | tf_op jit(solution)/shard_map/reduce_scatter | solution.py:177
  268.8 6.9 %collective-permute-start.9 = (bf16[64,640]{1,0:T(8,128)(2,1)S(1)}, bf16[64,640]{1,0:T(8,128)(2,1)S(1)}, u32[]{:S(2)}, u32[]{:S(2)}) collective-permute-start(bf16[64,640]{1,0:T(8,128)(2,1)S(1)} %get-tuple-element.46), channel_id=1, source_target_pairs={{2,0},{4,2},{6,4},{8,6},{10,8},{12,10},{14,12},{16,14},{18,16},{20... | collective-permute-start | bytes 245768 | tf_op jit(solution)/shard_map/ppermute | solution.py:46
  275.2 3.7 slice-start.2
  275.7 3.2 slice-start.3
  275.7 3.7 copy-start.14
  277.2 19.7 %slice-start.6 = ((s8[5242880]{0:T(1024)(128)(4,1)}), s8[4194304]{0:T(1024)(128)(4,1)S(1)}, s32[]{:S(2)}) async-start(s8[5242880]{0:T(1024)(128)(4,1)} %bitcast.57), calls=%async_computation.21 | async-start | bytes 8388608
  279.4 17.6 %slice-start.7 = ((s8[5242880]{0:T(1024)(128)(4,1)}), s8[1048576]{0:T(1024)(128)(4,1)S(1)}, s32[]{:S(2)}) async-start(s8[5242880]{0:T(1024)(128)(4,1)} %bitcast.57), calls=%async_computation.22 | async-start | bytes 2097152
  303.0 213.2 %reduce-scatter.15.cloned.1.call-start = ((), (), s32[]{:S(2)}) async-start(), calls=%async_computation.10 | async-start | bytes 8704000 | tf_op jit(solution)/shard_map/reduce_scatter | solution.py:177
  319.1 212.9 %reduce-scatter.23.cloned.1.call-start = ((), (), s32[]{:S(2)}) async-start(), calls=%async_computation.14 | async-start | bytes 491520
  329.1 4.7 copy-start.17
  329.1 4.7 copy-start.20
  329.1 4.7 copy-start.22
  329.1 4.6 copy-start.24
  329.1 4.6 copy-start.27
  329.1 4.6 copy-start.38
  332.3 163.8 %collective-permute-start.6 = (bf16[2048,640]{1,0:T(8,128)(2,1)}, bf16[2048,640]{1,0:T(8,128)(2,1)}, u32[]{:S(2)}, u32[]{:S(2)}) collective-permute-start(bf16[2048,640]{1,0:T(8,128)(2,1)} %get-tuple-element.43), channel_id=1, source_target_pairs={{0,1},{1,0},{2,3},{3,2},{4,5},{5,4},{6,7},{7,6},{8,9},{9,8},{10,11... | collective-permute-start | bytes 7864328 | tf_op jit(solution)/shard_map/ppermute | solution.py:85
  355.1 4.1 copy-start.5
  359.2 2.9 copy-start.12
  361.2 161.1 %collective-permute-start.10 = (bf16[2048,640]{1,0:T(8,128)(2,1)}, bf16[2048,640]{1,0:T(8,128)(2,1)}, u32[]{:S(2)}, u32[]{:S(2)}) collective-permute-start(bf16[2048,640]{1,0:T(8,128)(2,1)} %select_convert_fusion), channel_id=1, source_target_pairs={{0,1},{1,0},{2,3},{3,2},{4,5},{5,4},{6,7},{7,6},{8,9},{9,8},{10,11... | collective-permute-start | bytes 7864328 | tf_op jit(solution)/shard_map/ppermute | solution.py:85
  487.0 9.2 %copy-start.13 = (bf16[1,2048,640]{2,1,0:T(8,128)(2,1)S(1)}, bf16[1,2048,640]{2,1,0:T(8,128)(2,1)}, u32[]{:S(2)}) copy-start(bf16[1,2048,640]{2,1,0:T(8,128)(2,1)} %get-tuple-element.42) | copy-start | bytes 7864324
  487.0 59.5 %reduce-scatter.19.cloned.1.call-start = ((), (), s32[]{:S(2)}) async-start(), calls=%async_computation.12 | async-start | bytes 491520
  496.1 68.7 %reduce-scatter.21.cloned.1.call-start = ((), (), s32[]{:S(2)}) async-start(), calls=%async_computation.13 | async-start | bytes 983040
  519.4 5.0 slice-start.4
  522.2 3.0 slice-start.5
  525.2 41.9 %copy-start.1 = (s32[2,128]{1,0:T(2,128)S(1)}, s32[2,128]{1,0:T(2,128)}, u32[]{:S(2)}) copy-start(s32[2,128]{1,0:T(2,128)} %param.18) | copy-start | bytes 3076
  (3 other events, 5.2 us)
Sparse Core Ops, SparseCore 0:
  13.5 39.7 all-gather.5
  138.6 50.5 all-gather.7
  191.9 38.8 all-gather.9
  268.9 66.5 reduce-scatter.16
  340.2 66.1 reduce-scatter.12
  410.4 105.6 reduce-scatter.14
  518.4 13.2 reduce-scatter.22
  534.0 12.3 reduce-scatter.18
  548.7 16.0 reduce-scatter.20

commit v2 on v1

v2 whole, which is shorter than its diff:
```python
import jax
import jax.numpy as jnp
from jax import lax
from jax.experimental import pallas as pl
from jax.experimental.pallas import tpu as pltpu
from jax.sharding import PartitionSpec as P

KERNEL_TAPS = 5
DILATION_STEP = 32
HALO = 64

EPSILON = 1e-05
ROOT_HALF = 0.7071067811865476
ROOT_TAU = 0.3989422804014327
SWAP = [(0, 1), (1, 0)]


def gelu_both(value):
    half = 0.5 * (1.0 + lax.erf(value * ROOT_HALF))
    return value * half, half + value * jnp.exp(-0.5 * value * value) * ROOT_TAU


def norm(value):
    middle = jnp.mean(value, axis=1, keepdims=True)
    centred = value - middle
    scale = lax.rsqrt(jnp.mean(centred * centred, axis=1, keepdims=True) + EPSILON)
    return centred * scale, scale


def norm_back(grad_zed, normed, scale, gain):
    grad_normed = grad_zed * gain
    first = jnp.mean(grad_normed, axis=1, keepdims=True)
    second = jnp.mean(grad_normed * normed, axis=1, keepdims=True)
    return scale * (grad_normed - first - normed * second)


def dot(left, right, over=((1,), (0,))):
    return lax.dot_general(left, right, (over, ((), ())), preferred_element_type=jnp.float32)


def column_sums(value):
    return jnp.sum(value, axis=0, keepdims=True)


def ordered(side, own, other):
    low = side == 0
    own, other = own.astype(jnp.float32), other.astype(jnp.float32)
    return jnp.where(low, own, other), jnp.where(low, other, own)


def windowed(framed_ref, taps, base, count):
    return jnp.concatenate(
        [
            framed_ref[pl.ds(base + tap * DILATION_STEP, count), :] * taps[:, tap : tap + 1]
            for tap in range(KERNEL_TAPS)
        ],
        axis=1,
    )


def first_kernel(side_ref, own_ref, other_ref, keep_ref, weight_ref, wide_ref, narrow_ref, a1_ref, s1_ref, h1_ref, a2_ref, s2_ref):
    x = jnp.concatenate(ordered(side_ref[0], own_ref[...], other_ref[...]), axis=1)
    normed, _ = norm(x)
    act, slope = gelu_both(normed * wide_ref[0:1, :] + wide_ref[1:2, :])
    act = act.astype(jnp.bfloat16)
    a1_ref[...] = act
    s1_ref[...] = slope
    h1 = dot(act, weight_ref[...]) + narrow_ref[0:1, :]
    h1_ref[...] = h1
    normed, _ = norm(h1)
    act, slope = gelu_both(normed * narrow_ref[1:2, :] + narrow_ref[2:3, :])
    keep = keep_ref[...]
    a2_ref[...] = (act * keep).astype(jnp.bfloat16)
    s2_ref[...] = slope * keep


def second_kernel(side_ref, own_ref, other_ref, taps_ref, framed_ref, conv_ref, weight_ref, wide_ref, narrow_ref, h3_ref, a3_ref, s3_ref, out_own_ref, out_other_ref):
    count = own_ref.shape[0]
    half = own_ref.shape[1]
    base = pl.multiple_of(pl.program_id(0) * count, count)
    h3 = dot(windowed(framed_ref, taps_ref[...], base, count), conv_ref[...]) + narrow_ref[3:4, :]
    h3_ref[...] = h3
    normed, _ = norm(h3)
    act, slope = gelu_both(normed * narrow_ref[4:5, :] + narrow_ref[5:6, :])
    act = act.astype(jnp.bfloat16)
    a3_ref[...] = act
    s3_ref[...] = slope
    mixed = dot(act, weight_ref[...], ((1,), (1,))) + wide_ref[2:3, :]
    left, right = mixed[:, :half], mixed[:, half:]
    low = side_ref[0] == 0
    out_own_ref[...] = (own_ref[...].astype(jnp.float32) + jnp.where(low, left, right)).astype(jnp.bfloat16)
    out_other_ref[...] = (other_ref[...].astype(jnp.float32) + jnp.where(low, right, left)).astype(jnp.bfloat16)


def third_kernel(side_ref, own_ref, other_ref, h3_ref, s3_ref, weight_ref, narrow_ref, dh3_ref, gy_ref, wide_sum_ref, sum_ref):
    @pl.when(pl.program_id(0) == 0)
    def _():
        wide_sum_ref[...] = jnp.zeros_like(wide_sum_ref)
        sum_ref[...] = jnp.zeros_like(sum_ref)

    gy = jnp.concatenate(ordered(side_ref[0], own_ref[...], other_ref[...]), axis=1)
    wide_sum_ref[0:1, :] += column_sums(gy)
    gy = gy.astype(jnp.bfloat16)
    gy_ref[...] = gy
    dz3 = dot(gy, weight_ref[...]) * s3_ref[...]
    normed, scale = norm(h3_ref[...])
    dh3 = norm_back(dz3, normed, scale, narrow_ref[4:5, :]).astype(jnp.bfloat16)
    dh3_ref[...] = dh3
    sum_ref[0:1, :] += column_sums(dh3.astype(jnp.float32))
    sum_ref[1:2, :] += column_sums(dz3 * normed)
    sum_ref[2:3, :] += column_sums(dz3)


def fourth_kernel(side_ref, own_ref, other_ref, gy_own_ref, taps_ref, framed_ref, conv_ref, h1_ref, s2_ref, s1_ref, weight_ref, wide_ref, narrow_ref, dh1_ref, dx_own_ref, dx_other_ref, wide_sum_ref, sum_ref):
    @pl.when(pl.program_id(0) == 0)
    def _():
        wide_sum_ref[...] = jnp.zeros_like(wide_sum_ref)
        sum_ref[...] = jnp.zeros_like(sum_ref)

    count = own_ref.shape[0]
    half = own_ref.shape[1]
    base = pl.multiple_of(pl.program_id(0) * count, count)
    dz2 = dot(windowed(framed_ref, taps_ref[...], base, count), conv_ref[...]) * s2_ref[...]
    normed, scale = norm(h1_ref[...])
    dh1 = norm_back(dz2, normed, scale, narrow_ref[1:2, :]).astype(jnp.bfloat16)
    dh1_ref[...] = dh1
    sum_ref[0:1, :] += column_sums(dh1.astype(jnp.float32))
    sum_ref[1:2, :] += column_sums(dz2 * normed)
    sum_ref[2:3, :] += column_sums(dz2)
    dz1 = dot(dh1, weight_ref[...], ((1,), (1,))) * s1_ref[...]
    x = jnp.concatenate(ordered(side_ref[0], own_ref[...], other_ref[...]), axis=1)
    normed, scale = norm(x)
    dx = norm_back(dz1, normed, scale, wide_ref[0:1, :])
    wide_sum_ref[0:1, :] += column_sums(dz1 * normed)
    wide_sum_ref[1:2, :] += column_sums(dz1)
    low = side_ref[0] == 0
    left, right = dx[:, :half], dx[:, half:]
    dx_own_ref[...] = jnp.where(low, left, right) + gy_own_ref[...].astype(jnp.float32)
    dx_other_ref[...] = jnp.where(low, right, left).astype(jnp.bfloat16)


def grad_kernel(left_ref, right_ref, out_ref):
    out_ref[...] = dot(left_ref[...], right_ref[...], ((0,), (0,)))


def conv_grad_kernel(framed_ref, taps_ref, right_ref, out_ref):
    tap = pl.program_id(0)
    count = right_ref.shape[0]
    base = pl.multiple_of(tap * DILATION_STEP, DILATION_STEP)
    left = framed_ref[pl.ds(base, count), :] * taps_ref[0]
    out_ref[0] = dot(left, right_ref[...], ((0,), (0,)))


VMEM_LIMIT = 56 * 2**20


def once(shape):
    return pl.BlockSpec(shape, lambda *_: (0,) * len(shape), pipeline_mode=pl.Buffered(1))


def by_rows(count, width):
    return pl.BlockSpec((count, width), lambda i, *_: (i, 0))


def row_call(kernel, side, rows, count, operands, outs, flops):
    in_specs = [by_rows(count, a.shape[1]) if how == "rows" else once(a.shape) for a, how in operands]
    out_specs = [
        by_rows(count, width) if how == "rows" else pl.BlockSpec((8, width), lambda i, *_: (0, 0))
        for width, _, how in outs
    ]
    out_shape = [
        jax.ShapeDtypeStruct((rows if how == "rows" else 8, width), dtype) for width, dtype, how in outs
    ]
    moved = sum(a.size * a.dtype.itemsize for a, _ in operands)
    moved += sum(o.size * o.dtype.itemsize for o in out_shape)
    return pl.pallas_call(
        kernel,
        grid_spec=pltpu.PrefetchScalarGridSpec(
            num_scalar_prefetch=1, grid=(rows // count,), in_specs=in_specs, out_specs=out_specs
        ),
        out_shape=out_shape,
        compiler_params=pltpu.CompilerParams(
            dimension_semantics=("arbitrary",), vmem_limit_bytes=VMEM_LIMIT
        ),
        cost_estimate=pl.CostEstimate(flops=flops // 32, bytes_accessed=moved // 32, transcendentals=0),
    )(side, *[a for a, _ in operands])


def matrix_grad(left, right, tiles):
    rows, height = left.shape
    width = right.shape[1]
    return pl.pallas_call(
        grad_kernel,
        grid=(tiles,),
        in_specs=[pl.BlockSpec((rows, height // tiles), lambda i: (0, i)), once((rows, width))],
        out_specs=pl.BlockSpec((height // tiles, width), lambda i: (i, 0)),
        out_shape=jax.ShapeDtypeStruct((height, width), jnp.float32),
        compiler_params=pltpu.CompilerParams(
            dimension_semantics=("arbitrary",), vmem_limit_bytes=VMEM_LIMIT
        ),
        cost_estimate=pl.CostEstimate(
            flops=rows * height * width // 16, bytes_accessed=rows * (height + width) // 16, transcendentals=0
        ),
    )(left, right)


def conv_grad(framed_rows, taps, right):
    rows, width = right.shape
    return pl.pallas_call(
        conv_grad_kernel,
        grid=(KERNEL_TAPS,),
        in_specs=[
            once(framed_rows.shape),
            pl.BlockSpec((1, rows, 1), lambda i: (i, 0, 0)),
            once((rows, width)),
        ],
        out_specs=pl.BlockSpec((1, width, width), lambda i: (i, 0, 0)),
        out_shape=jax.ShapeDtypeStruct((KERNEL_TAPS, width, width), jnp.float32),
        compiler_params=pltpu.CompilerParams(
            dimension_semantics=("arbitrary",), vmem_limit_bytes=VMEM_LIMIT
        ),
        cost_estimate=pl.CostEstimate(
            flops=KERNEL_TAPS * rows * width * width // 16, bytes_accessed=rows * width // 8, transcendentals=0
        ),
    )(framed_rows, taps, right)


def framed(block, width):
    count = lax.axis_size("seq")
    forward = [(i, i + 1) for i in range(count - 1)]
    backward = [(i + 1, i) for i in range(count - 1)]
    low = lax.ppermute(block[block.shape[0] - width :], "seq", forward)
    high = lax.ppermute(block[:width], "seq", backward)
    return jnp.concatenate([low, block, high], axis=0)


def scattered(value, order):
    count = lax.axis_size("seq")
    place = lax.axis_index("seq")
    bits = count.bit_length() - 1
    value = value.reshape((2,) * bits + value.shape[1:])
    left = list(range(bits))
    for bit in order:
        dim = left.index(bits - 1 - bit)
        left.remove(bits - 1 - bit)
        mine = (place >> bit) & 1
        keep = lax.dynamic_index_in_dim(value, mine, dim, keepdims=False)
        send = lax.dynamic_index_in_dim(value, 1 - mine, dim, keepdims=False).astype(jnp.bfloat16)
        came = lax.ppermute(send, "seq", [(i, i ^ (1 << bit)) for i in range(count)])
        value = keep + came.astype(jnp.float32)
    return value


def body(
    tokens,
    cotangent,
    seq_lengths,
    residue_mask,
    first_gain,
    first_shift,
    proj_in,
    in_bias,
    mid_gain,
    mid_shift,
    conv_weight,
    conv_bias,
    last_gain,
    last_shift,
    proj_out,
    out_bias,
):
    micro, rows, half = tokens.shape
    inner_half = in_bias.shape[0]
    inner = 2 * inner_half
    model = 2 * half
    seq_count = lax.axis_size("seq")
    count = 256
    side = lax.axis_index("ch")
    side_array = side.astype(jnp.int32).reshape(1)
    low_side = side == 0

    def swap(value):
        return lax.ppermute(value, "ch", SWAP)

    def whole(own, other, axis):
        return jnp.where(
            low_side,
            jnp.concatenate([own, other], axis=axis),
            jnp.concatenate([other, own], axis=axis),
        )

    def own_of(value):
        return lax.dynamic_index_in_dim(value, side, 0, keepdims=False)

    def other_of(value):
        return lax.dynamic_index_in_dim(value, 1 - side, 0, keepdims=False)

    own_vectors = jnp.concatenate(
        [first_gain, first_shift, out_bias, in_bias, mid_gain, mid_shift, conv_bias, last_gain, last_shift]
    )
    part_in = proj_in.shape[0]
    part_conv = conv_weight.shape[1]
    own_weights = jnp.concatenate(
        [proj_in, proj_out.T, conv_weight.reshape(KERNEL_TAPS * part_conv, inner_half)], axis=0
    )
    own_vectors, own_weights = lax.optimization_barrier((own_vectors, own_weights))
    other_vectors, other_weights = swap(own_vectors), swap(own_weights)
    tokens_tied, other_vectors, other_weights = lax.optimization_barrier(
        (other_of(tokens), other_vectors, other_weights)
    )
    both = whole(own_weights, other_weights, 1)
    vectors = jnp.where(
        low_side, jnp.stack([own_vectors, other_vectors]), jnp.stack([other_vectors, own_vectors])
    )
    x_own = own_of(tokens)
    x_other = swap(tokens_tied)
    gy_own = own_of(cotangent)
    gy_tied, _ = lax.optimization_barrier((other_of(cotangent), x_other))
    gy_other = swap(gy_tied)

    gathered = lax.all_gather(both, "seq", axis=0)
    weight_in = gathered[:, :part_in].reshape(model, inner)
    weight_out = gathered[:, part_in : 2 * part_in].reshape(model, inner)
    weight_conv = (
        gathered[:, 2 * part_in :]
        .reshape(seq_count, KERNEL_TAPS, part_conv, inner)
        .transpose(1, 0, 2, 3)
        .reshape(KERNEL_TAPS, inner, inner)
    )
    wide = jnp.stack([vectors[:, i * half : (i + 1) * half].reshape(-1) for i in range(3)])
    narrow = jnp.stack(
        [
            vectors[:, 3 * half + i * inner_half : 3 * half + (i + 1) * inner_half].reshape(-1)
            for i in range(6)
        ]
    )

    places = lax.axis_index("seq") * rows + jnp.arange(rows + 2 * HALO, dtype=jnp.int32) - HALO
    inside = (places >= 0) & (places < rows * seq_count)
    bounds = jnp.cumsum(own_of(seq_lengths))[:-1]
    segment = jnp.sum((places[:, None] >= bounds[None, :]).astype(jnp.int32), axis=1)
    segment = jnp.where(inside, segment, -1)
    middle = segment[HALO : HALO + rows]
    tap_list = [
        (segment[tap * DILATION_STEP : tap * DILATION_STEP + rows] == middle).astype(jnp.bfloat16)
        for tap in range(KERNEL_TAPS)
    ]
    taps = jnp.stack(tap_list, axis=1)
    keep = own_of(residue_mask).astype(jnp.float32)[:, None]
    f32, bf16 = jnp.float32, jnp.bfloat16
    product = 2 * rows * model * inner

    a1, s1, h1, a2, s2 = row_call(
        first_kernel,
        side_array,
        rows,
        count,
        [(x_own, "rows"), (x_other, "rows"), (keep, "rows"), (weight_in, "once"), (wide, "once"), (narrow, "once")],
        [(model, bf16, "rows"), (model, f32, "rows"), (inner, f32, "rows"), (inner, bf16, "rows"), (inner, f32, "rows")],
        product,
    )
    a2 = framed(a2, HALO)
    h3, a3, s3, out_own, out_other = row_call(
        second_kernel,
        side_array,
        rows,
        count,
        [
            (x_own, "rows"),
            (x_other, "rows"),
            (taps, "rows"),
            (a2, "once"),
            (weight_conv.reshape(KERNEL_TAPS * inner, inner), "once"),
            (weight_out, "once"),
            (wide, "once"),
            (narrow, "once"),
        ],
        [(inner, f32, "rows"), (inner, bf16, "rows"), (inner, f32, "rows"), (half, bf16, "rows"), (half, bf16, "rows")],
        4 * product,
    )
    out_back = swap(out_other)

    dh3, gy, wide_sum_3, sum_3 = row_call(
        third_kernel,
        side_array,
        rows,
        count,
        [(gy_own, "rows"), (gy_other, "rows"), (h3, "rows"), (s3, "rows"), (weight_out, "once"), (narrow, "once")],
        [(inner, bf16, "rows"), (model, bf16, "rows"), (model, f32, "sum"), (inner, f32, "sum")],
        product,
    )
    dh3_framed = framed(dh3, HALO)
    grad_out = matrix_grad(gy, a3, 2)
    grad_conv = conv_grad(a2, jnp.stack(tap_list, axis=0)[:, :, None], dh3)
    dh3_framed, out_back = lax.optimization_barrier((dh3_framed, out_back))
    flipped = jnp.flip(weight_conv, 0).transpose(0, 2, 1).reshape(KERNEL_TAPS * inner, inner)
    dh1, dx_own, dx_other, wide_sum_1, sum_1 = row_call(
        fourth_kernel,
        side_array,
        rows,
        count,
        [
            (x_own, "rows"),
            (x_other, "rows"),
            (gy_own, "rows"),
            (taps, "rows"),
            (dh3_framed, "once"),
            (flipped, "once"),
            (h1, "rows"),
            (s2, "rows"),
            (s1, "rows"),
            (weight_in, "once"),
            (wide, "once"),
            (narrow, "once"),
        ],
        [(inner, bf16, "rows"), (half, f32, "rows"), (half, bf16, "rows"), (model, f32, "sum"), (inner, f32, "sum")],
        4 * product,
    )
    dx_back = swap(dx_other)
    grad_in = matrix_grad(a1, dh1, 2)

    def placed(own, back):
        return jnp.where(low_side, jnp.stack([own, back], 0), jnp.stack([back, own], 0))

    block_out = placed(out_own, out_back)
    grad_tokens = placed(
        dx_own, dx_back.astype(f32) + other_of(cotangent).astype(f32)
    )

    bits = list(range(seq_count.bit_length() - 1))
    swapped_bits = [bits[0]] + bits[2:] + [bits[1]]
    part = jnp.concatenate(
        [
            scattered(grad_in.reshape(seq_count, part_in, inner), bits),
            scattered(grad_out.reshape(seq_count, part_in, inner), swapped_bits),
            scattered(
                grad_conv.reshape(KERNEL_TAPS, seq_count, part_conv, inner).transpose(1, 0, 2, 3), bits
            ).reshape(KERNEL_TAPS * part_conv, inner),
        ],
        axis=0,
    )
    left, right = part[:, :inner_half], part[:, inner_half:]
    part_other = swap(jnp.where(low_side, right, left).astype(bf16))
    part = jnp.where(low_side, left, right) + part_other.astype(f32)

    smalls = jnp.concatenate(
        [
            small.reshape(2, -1)
            for small in (wide_sum_1[0], wide_sum_1[1], wide_sum_3[0], sum_1[0], sum_1[1], sum_1[2], sum_3[0], sum_3[1], sum_3[2])
        ],
        axis=1,
    )
    totals = smalls
    for bit in bits:
        totals = totals + lax.ppermute(totals, "seq", [(i, i ^ (1 << bit)) for i in range(seq_count)])
    totals = own_of(totals) + swap(other_of(totals))
    sizes = [half] * 3 + [inner_half] * 6
    parts = []
    at = 0
    for size in sizes:
        parts.append(totals[at : at + size])
        at += size
    return (
        block_out,
        grad_tokens,
        parts[0],
        parts[1],
        part[:part_in],
        parts[3],
        parts[4],
        parts[5],
        part[2 * part_in :].reshape(KERNEL_TAPS, part_conv, inner_half),
        parts[6],
        parts[7],
        parts[8],
        part[part_in : 2 * part_in].T,
        parts[2],
    )


BLOCK = 256
CHUNKS = 4
CONV_PAD = 8


def fast_kernel(
    tokens, x_other, cot, masks, w_in, w_out, w_conv, wide, narrow,
    out_own, out_back, dx_own, dx_back, grads, smalls,
    gy_other, out_send, dx_send, s1, h1, s2, h3, s3,
    a1v, a2f, a3v, gyv, dh3f,
    k_in, s_in, r0_in, r1_in, r2_in, r3_in,
    k_out, s_out, r0_out, r1_out, r2_out, r3_out,
    k_conv, s_conv, r0_conv, r1_conv, r2_conv, r3_conv,
    cross_send, cross_recv, small_send, small_recv,
    gy_sems, out_sems, dx_sems, a2_sems, dh3_sems, in_sems, out_rs_sems, conv_sems, cross_sems, small_sems,
):
    rows = a1v.shape[0]
    half = tokens.shape[2]
    inner = narrow.shape[1]
    part = rows // CHUNKS
    side = lax.axis_index("ch")
    place = lax.axis_index("seq")
    last = lax.axis_size("seq") - 1
    low = side == 0
    bits = [lax.rem(place // (1 << bit), 2) for bit in range(4)]
    across = {"ch": 1 - side}
    pairs = [{"seq": place + (1 << bit) * (1 - 2 * bits[bit])} for bit in range(4)]
    before, after = {"seq": place - 1}, {"seq": place + 1}

    def remote(src, dst, sems, at, device):
        return pltpu.make_async_remote_copy(
            src_ref=src,
            dst_ref=dst,
            send_sem=sems.at[0, at],
            recv_sem=sems.at[1, at],
            device_id=device,
            device_id_type=pl.DeviceIdType.MESH,
        )

    def chunk(ref, at):
        return ref.at[pl.ds(pl.multiple_of(at * part, part), part)]

    def gy_copy(at):
        return remote(chunk(cot.at[1 - side], at), chunk(gy_other, at), gy_sems, at, across)

    def out_copy(at):
        return remote(chunk(out_send, at), chunk(out_back, at), out_sems, at, across)

    def dx_copy(at):
        return remote(chunk(dx_send, at), chunk(dx_back, at), dx_sems, at, across)

    def halo_low(framed_rows, sems):
        return remote(framed_rows.at[pl.ds(HALO, HALO)], framed_rows.at[pl.ds(HALO + rows, HALO)], sems, 0, before)

    def halo_high(framed_rows, sems):
        return remote(framed_rows.at[pl.ds(rows, HALO)], framed_rows.at[pl.ds(0, HALO)], sems, 1, after)

    def halo_start(framed_rows, sems):
        @pl.when(place > 0)
        def _():
            halo_low(framed_rows, sems).start()

        @pl.when(place < last)
        def _():
            halo_high(framed_rows, sems).start()

    def halo_wait(framed_rows, sems):
        @pl.when(place > 0)
        def _():
            halo_low(framed_rows, sems).wait_send()
            halo_high(framed_rows, sems).wait_recv()

        @pl.when(place < last)
        def _():
            halo_high(framed_rows, sems).wait_send()
            halo_low(framed_rows, sems).wait_recv()

    def middle_first(step):
        late = step // 2
        return (step + 1) * (1 - late) + late * (step - 2) * 3

    def pipeline(step, blocks, ins, outs):
        def spec(ref):
            return pl.BlockSpec((BLOCK, ref.shape[-1]), lambda i: (i, 0))

        pltpu.emit_pipeline(
            step, grid=(blocks,), in_specs=[spec(r) for r in ins], out_specs=[spec(r) for r in outs]
        )(*ins, *outs)

    barrier = pltpu.get_barrier_semaphore()
    ring = [{"seq": lax.rem(place + last, last + 1)}, {"seq": lax.rem(place + 1, last + 1)}]
    for device in [across] + pairs + ring:
        pl.semaphore_signal(barrier, inc=1, device_id=device, device_id_type=pl.DeviceIdType.MESH)
    pl.semaphore_wait(barrier, 7)

    for at in range(CHUNKS):
        gy_copy(at).start()
    smalls[...] = jnp.zeros_like(smalls)

    @pl.when(place == 0)
    def _():
        a2f[0:HALO, :] = jnp.zeros((HALO, inner), jnp.bfloat16)
        dh3f[0:HALO, :] = jnp.zeros((HALO, inner), jnp.bfloat16)

    @pl.when(place == last)
    def _():
        a2f[HALO + rows :, :] = jnp.zeros((HALO, inner), jnp.bfloat16)
        dh3f[HALO + rows :, :] = jnp.zeros((HALO, inner), jnp.bfloat16)

    def first(own, other, s1_block, h1_block, s2_block):
        base = pl.multiple_of(pl.program_id(0) * BLOCK, BLOCK)
        x = jnp.concatenate(ordered(side, own[...], other[...]), axis=1)
        normed, _ = norm(x)
        act, slope = gelu_both(normed * wide[0:1, :] + wide[1:2, :])
        act = act.astype(jnp.bfloat16)
        a1v[pl.ds(base, BLOCK), :] = act
        s1_block[...] = slope
        value = dot(act, w_in[...]) + narrow[0:1, :]
        h1_block[...] = value
        normed, _ = norm(value)
        act, slope = gelu_both(normed * narrow[1:2, :] + narrow[2:3, :])
        keep = masks[pl.ds(base, BLOCK), KERNEL_TAPS : KERNEL_TAPS + 1].astype(jnp.float32)
        a2f[pl.ds(HALO + base, BLOCK), :] = (act * keep).astype(jnp.bfloat16)
        s2_block[...] = slope * keep

    pipeline(first, rows // BLOCK, [tokens.at[side], x_other], [s1, h1, s2])
    halo_start(a2f, a2_sems)

    def forward_chunk(step, _):
        at = middle_first(step)

        @pl.when(step == 2)
        def _():
            halo_wait(a2f, a2_sems)

        def second(own, other, h3_block, s3_block, own_block, other_block):
            base = pl.multiple_of(at * part + pl.program_id(0) * BLOCK, BLOCK)
            taps = masks[pl.ds(base, BLOCK), :]
            value = dot(windowed(a2f, taps, base, BLOCK), w_conv[...]) + narrow[3:4, :]
            h3_block[...] = value
            normed, _ = norm(value)
            act, slope = gelu_both(normed * narrow[4:5, :] + narrow[5:6, :])
            act = act.astype(jnp.bfloat16)
            a3v[pl.ds(base, BLOCK), :] = act
            s3_block[...] = slope
            mixed = dot(act, w_out[...], ((1,), (1,))) + wide[2:3, :]
            left, right = mixed[:, :half], mixed[:, half:]
            own_block[...] = (own[...].astype(jnp.float32) + jnp.where(low, left, right)).astype(jnp.bfloat16)
            other_block[...] = (other[...].astype(jnp.float32) + jnp.where(low, right, left)).astype(jnp.bfloat16)

        pipeline(
            second,
            part // BLOCK,
            [chunk(tokens.at[side], at), chunk(x_other, at)],
            [chunk(h3, at), chunk(s3, at), chunk(out_own, at), chunk(out_send, at)],
        )
        out_copy(at).start()
        return 0

    lax.fori_loop(0, CHUNKS, forward_chunk, 0)

    def add_small(row, value):
        smalls[row : row + 1, :] += value

    def add_wide(row, value):
        smalls[row : row + 1, :] += value[:, :half]
        smalls[row + 1 : row + 2, :] += value[:, half:]

    def third_chunk(at, _):
        gy_copy(at).wait_recv()

        def third(own, other, h3_block, s3_block):
            base = pl.multiple_of(at * part + pl.program_id(0) * BLOCK, BLOCK)
            gy = jnp.concatenate(ordered(side, own[...], other[...]), axis=1)
            add_wide(4, column_sums(gy))
            gy = gy.astype(jnp.bfloat16)
            gyv[pl.ds(base, BLOCK), :] = gy
            dz3 = dot(gy, w_out[...]) * s3_block[...]
            normed, scale = norm(h3_block[...])
            dh3 = norm_back(dz3, normed, scale, narrow[4:5, :]).astype(jnp.bfloat16)
            dh3f[pl.ds(HALO + base, BLOCK), :] = dh3
            add_small(9, column_sums(dh3.astype(jnp.float32)))
            add_small(10, column_sums(dz3 * normed))
            add_small(11, column_sums(dz3))

        pipeline(
            third,
            part // BLOCK,
            [chunk(cot.at[side], at), chunk(gy_other, at), chunk(h3, at), chunk(s3, at)],
            [],
        )
        return 0

    lax.fori_loop(0, CHUNKS, third_chunk, 0)
    halo_start(dh3f, dh3_sems)

    def split(keep_ref, send_ref, at, row, even, odd):
        height = even.shape[0]
        mine_first = bits[0] == 0
        keep_ref[at, row : row + height, :] = jnp.where(mine_first, even, odd)
        send_ref[at, row : row + height, :] = jnp.where(mine_first, odd, even).astype(jnp.bfloat16)

    def wide_grad(left_ref, right_ref, keep_ref, send_ref):
        height = keep_ref.shape[1]

        def tile(at, _):
            columns = pl.ds(pl.multiple_of(at * half, 128), half)
            value = dot(left_ref[:, columns], right_ref[...], ((0,), (0,)))
            for pair in range(half // (2 * height)):
                top = 2 * pair * height
                split(
                    keep_ref,
                    send_ref,
                    at * (half // (2 * height)) + pair,
                    0,
                    value[top : top + height],
                    value[top + height : top + 2 * height],
                )
            return 0

        lax.fori_loop(0, 2, tile, 0)

    def conv_grads():
        height = inner // 16
        right = dh3f.at[pl.ds(HALO, rows)]
        for taps in ((0, 1), (2, 3), (4,)):
            values = []
            for tap in taps:
                left = a2f[tap * DILATION_STEP : tap * DILATION_STEP + rows, :] * masks[:, tap : tap + 1]
                values.append(dot(left, right[...], ((0,), (0,))))
            if len(values) == 1:
                tail = [jnp.zeros((CONV_PAD, inner), jnp.float32)]
            else:
                tail = []
            for pair in range(8):
                top = 2 * pair * height
                even = jnp.concatenate([v[top : top + height] for v in values] + tail, axis=0)
                odd = jnp.concatenate([v[top + height : top + 2 * height] for v in values] + tail, axis=0)
                split(k_conv, s_conv, pair, taps[0] * height, even, odd)

    in_set = (k_in, s_in, (r0_in, r1_in, r2_in, r3_in), in_sems)
    out_set = (k_out, s_out, (r0_out, r1_out, r2_out, r3_out), out_rs_sems)
    conv_set = (k_conv, s_conv, (r0_conv, r1_conv, r2_conv, r3_conv), conv_sems)
    starts = (0, 0, 4, 6)
    lengths = (8, 4, 2, 1)

    def sum_copy(group, level):
        _, send, received, sems = group
        return remote(
            send.at[pl.ds(starts[level], lengths[level])], received[level], sems, level, pairs[level]
        )

    def sum_step(group, level):
        keep, send, received, _ = group
        sum_copy(group, level).wait()
        came = received[level]
        fixed = 0
        for bit in range(level):
            fixed = fixed + bits[bit + 1] * (1 << bit)
        if level == 3:
            keep[fixed] = keep[fixed] + came[0].astype(jnp.float32)
            return
        mine = bits[level + 1]

        def one(item, _):
            other = 2 * item + 1 - mine
            same = 2 * item + mine
            send[starts[level + 1] + item] = (
                keep[other * (1 << level) + fixed] + came[other].astype(jnp.float32)
            ).astype(jnp.bfloat16)
            at = same * (1 << level) + fixed
            keep[at] = keep[at] + came[same].astype(jnp.float32)
            return 0

        lax.fori_loop(0, lengths[level + 1], one, 0)
        sum_copy(group, level + 1).start()

    wide_grad(gyv, a3v, k_out, s_out)
    sum_copy(out_set, 0).start()
    conv_grads()
    sum_copy(conv_set, 0).start()
    sum_step(out_set, 0)
    halo_wait(dh3f, dh3_sems)

    def fourth_chunk(step, _):
        at = middle_first(step)

        def fourth(own, other, gy_own, h1_block, s2_block, s1_block, own_block, other_block):
            base = pl.multiple_of(at * part + pl.program_id(0) * BLOCK, BLOCK)
            taps = masks[pl.ds(base, BLOCK), :]
            da2 = jnp.zeros((BLOCK, inner), jnp.float32)
            for tap in range(KERNEL_TAPS):
                window = dh3f[pl.ds(base + tap * DILATION_STEP, BLOCK), :] * taps[:, tap : tap + 1]
                weight = w_conv[(KERNEL_TAPS - 1 - tap) * inner : (KERNEL_TAPS - tap) * inner, :]
                da2 = da2 + dot(window, weight, ((1,), (1,)))
            dz2 = da2 * s2_block[...]
            normed, scale = norm(h1_block[...])
            dh1 = norm_back(dz2, normed, scale, narrow[1:2, :]).astype(jnp.bfloat16)
            a3v[pl.ds(base, BLOCK), :] = dh1
            add_small(6, column_sums(dh1.astype(jnp.float32)))
            add_small(7, column_sums(dz2 * normed))
            add_small(8, column_sums(dz2))
            dz1 = dot(dh1, w_in[...], ((1,), (1,))) * s1_block[...]
            x = jnp.concatenate(ordered(side, own[...], other[...]), axis=1)
            normed, scale = norm(x)
            dx = norm_back(dz1, normed, scale, wide[0:1, :])
            add_wide(0, column_sums(dz1 * normed))
            add_wide(2, column_sums(dz1))
            left, right = dx[:, :half], dx[:, half:]
            own_block[...] = jnp.where(low, left, right) + gy_own[...].astype(jnp.float32)
            other_block[...] = jnp.where(low, right, left).astype(jnp.bfloat16)

        pipeline(
            fourth,
            part // BLOCK,
            [
                chunk(tokens.at[side], at),
                chunk(x_other, at),
                chunk(cot.at[side], at),
                chunk(h1, at),
                chunk(s2, at),
                chunk(s1, at),
            ],
            [chunk(dx_own, at), chunk(dx_send, at)],
        )
        dx_copy(at).start()
        for level in range(3):

            @pl.when(step == level)
            def _():
                sum_step(out_set, level + 1)
                sum_step(conv_set, level)

        return 0

    lax.fori_loop(0, CHUNKS, fourth_chunk, 0)

    wide_grad(a1v, a3v, k_in, s_in)
    sum_copy(in_set, 0).start()

    def small_copy(level):
        device = pairs[level] if level < 4 else across
        return remote(small_send.at[level], small_recv.at[level], small_sems, level, device)

    def small_start(level):
        small_send[level] = smalls[...]
        small_copy(level).start()

    def small_step(level):
        small_copy(level).wait()
        smalls[...] += small_recv[level]

    small_start(0)
    sum_step(conv_set, 3)
    for level in range(4):
        sum_step(in_set, level)
        small_step(level)
        small_start(level + 1)

    wanted = half // 2 + 64
    mine = 4 * bits[3] + 2 * bits[2] + bits[1]
    row = 0
    for keep in (k_in, k_out, k_conv):
        height = keep.shape[1]
        value = keep[mine]
        left, right = value[:, :wanted], value[:, inner - wanted :]
        grads[row : row + height, :] = jnp.where(low, left, right)
        cross_send[row : row + height, :] = jnp.where(low, right, left).astype(jnp.bfloat16)
        row += height
    cross = remote(cross_send, cross_recv, cross_sems, 0, across)
    cross.start()
    for at in range(CHUNKS):
        gy_copy(at).wait_send()
        out_copy(at).wait()
    small_step(4)
    cross.wait()
    grads[...] += cross_recv[...].astype(jnp.float32)
    for at in range(CHUNKS):
        dx_copy(at).wait()


def fast_call(tokens, x_other, cot, masks, w_in, w_out, w_conv, wide, narrow, part_in, part_conv):
    _, rows, half = tokens.shape
    model = 2 * half
    inner = narrow.shape[1]
    f32, bf16 = jnp.float32, jnp.bfloat16
    tall = KERNEL_TAPS * part_conv + CONV_PAD
    any_spec = pl.BlockSpec(memory_space=pl.ANY)
    vmem_spec = pl.BlockSpec(memory_space=pltpu.VMEM)
    total = 2 * part_in + tall
    wanted = half // 2 + 64

    def sums(height):
        return [pltpu.VMEM((8, height, inner), f32), pltpu.VMEM((8, height, inner), bf16)] + [
            pltpu.VMEM((length, height, inner), bf16) for length in (8, 4, 2, 1)
        ]

    def sems(count):
        return pltpu.SemaphoreType.DMA((2, count))

    shapes = [
        ((rows, half), bf16),
        ((rows, half), bf16),
        ((rows, half), f32),
        ((rows, half), bf16),
        ((total, wanted), f32),
        ((16, inner), f32),
        ((rows, half), bf16),
        ((rows, half), bf16),
        ((rows, half), bf16),
        ((rows, model), f32),
        ((rows, inner), f32),
        ((rows, inner), f32),
        ((rows, inner), f32),
        ((rows, inner), f32),
    ]
    flops = 6 * rows * (2 * model * inner + KERNEL_TAPS * inner * inner)
    results = pl.pallas_call(
        fast_kernel,
        out_shape=[jax.ShapeDtypeStruct(shape, dtype) for shape, dtype in shapes],
        in_specs=[any_spec] * 3 + [vmem_spec] * 6,
        out_specs=[any_spec] * 4 + [vmem_spec] * 2 + [any_spec] * 8,
        scratch_shapes=[
            pltpu.VMEM((rows, model), bf16),
            pltpu.VMEM((rows + 2 * HALO, inner), bf16),
            pltpu.VMEM((rows, inner), bf16),
            pltpu.VMEM((rows, model), bf16),
            pltpu.VMEM((rows + 2 * HALO, inner), bf16),
        ]
        + sums(part_in)
        + sums(part_in)
        + sums(tall)
        + [
            pltpu.VMEM((total, wanted), bf16),
            pltpu.VMEM((total, wanted), bf16),
            pltpu.VMEM((5, 16, inner), f32),
            pltpu.VMEM((5, 16, inner), f32),
            sems(CHUNKS),
            sems(CHUNKS),
            sems(CHUNKS),
            sems(2),
            sems(2),
            sems(4),
            sems(4),
            sems(4),
            sems(1),
            sems(5),
        ],
        compiler_params=pltpu.CompilerParams(
            collective_id=0, has_side_effects=True, vmem_limit_bytes=63 * 2**20
        ),
        cost_estimate=pl.CostEstimate(flops=flops, bytes_accessed=120 * 2**20, transcendentals=0),
    )(tokens, x_other, cot, masks, w_in, w_out, w_conv, wide, narrow)
    return results[:6]


def fast_body(
    tokens,
    cotangent,
    seq_lengths,
    residue_mask,
    first_gain,
    first_shift,
    proj_in,
    in_bias,
    mid_gain,
    mid_shift,
    conv_weight,
    conv_bias,
    last_gain,
    last_shift,
    proj_out,
    out_bias,
):
    micro, rows, half = tokens.shape
    inner_half = in_bias.shape[0]
    inner = 2 * inner_half
    model = 2 * half
    seq_count = lax.axis_size("seq")
    side = lax.axis_index("ch")
    low_side = side == 0
    f32, bf16 = jnp.float32, jnp.bfloat16

    def swap(value):
        return lax.ppermute(value, "ch", SWAP)

    def own_of(value):
        return lax.dynamic_index_in_dim(value, side, 0, keepdims=False)

    def other_of(value):
        return lax.dynamic_index_in_dim(value, 1 - side, 0, keepdims=False)

    own_vectors = jnp.concatenate(
        [first_gain, first_shift, out_bias, in_bias, mid_gain, mid_shift, conv_bias, last_gain, last_shift]
    )
    part_in = proj_in.shape[0]
    part_conv = conv_weight.shape[1]
    own_weights = jnp.concatenate(
        [proj_in, proj_out.T, conv_weight.reshape(KERNEL_TAPS * part_conv, inner_half)], axis=0
    )
    own_vectors, own_weights = lax.optimization_barrier((own_vectors, own_weights))
    other_vectors, other_weights = swap(own_vectors), swap(own_weights)
    tokens_tied, other_vectors, other_weights = lax.optimization_barrier(
        (other_of(tokens), other_vectors, other_weights)
    )
    both = jnp.where(
        low_side,
        jnp.concatenate([own_weights, other_weights], axis=1),
        jnp.concatenate([other_weights, own_weights], axis=1),
    )
    vectors = jnp.where(
        low_side, jnp.stack([own_vectors, other_vectors]), jnp.stack([other_vectors, own_vectors])
    )
    x_other = swap(tokens_tied)
    gathered = lax.all_gather(both, "seq", axis=0)
    weight_in = gathered[:, :part_in].reshape(model, inner)
    weight_out = gathered[:, part_in : 2 * part_in].reshape(model, inner)
    weight_conv = (
        gathered[:, 2 * part_in :]
        .reshape(seq_count, KERNEL_TAPS, part_conv, inner)
        .transpose(1, 0, 2, 3)
        .reshape(KERNEL_TAPS * inner, inner)
    )
    wide = jnp.stack([vectors[:, i * half : (i + 1) * half].reshape(-1) for i in range(3)])
    narrow = jnp.stack(
        [
            vectors[:, 3 * half + i * inner_half : 3 * half + (i + 1) * inner_half].reshape(-1)
            for i in range(6)
        ]
    )

    places = lax.axis_index("seq") * rows + jnp.arange(rows + 2 * HALO, dtype=jnp.int32) - HALO
    inside = (places >= 0) & (places < rows * seq_count)
    bounds = jnp.cumsum(own_of(seq_lengths))[:-1]
    segment = jnp.sum((places[:, None] >= bounds[None, :]).astype(jnp.int32), axis=1)
    segment = jnp.where(inside, segment, -1)
    middle = segment[HALO : HALO + rows]
    columns = [
        (segment[tap * DILATION_STEP : tap * DILATION_STEP + rows] == middle).astype(bf16)
        for tap in range(KERNEL_TAPS)
    ]
    zero = jnp.zeros((rows,), bf16)
    masks = jnp.stack(columns + [own_of(residue_mask).astype(bf16), zero, zero], axis=1)

    out_own, out_back, dx_own, dx_back, grads, smalls = fast_call(
        tokens, x_other, cotangent, masks, weight_in, weight_out, weight_conv, wide, narrow, part_in, part_conv
    )

    def placed(own, back):
        return jnp.where(low_side, jnp.stack([own, back], 0), jnp.stack([back, own], 0))

    block_out = placed(out_own, out_back)
    grad_tokens = placed(dx_own, dx_back.astype(f32) + other_of(cotangent).astype(f32))
    grads = jnp.where(low_side, grads[:, :inner_half], grads[:, grads.shape[1] - inner_half :])

    def wide_part(row):
        return lax.dynamic_index_in_dim(smalls, row + side, 0, keepdims=False)

    def narrow_part(row):
        return lax.dynamic_slice_in_dim(smalls[row], side * inner_half, inner_half, 0)

    return (
        block_out,
        grad_tokens,
        wide_part(0),
        wide_part(2),
        grads[:part_in],
        narrow_part(6),
        narrow_part(7),
        narrow_part(8),
        grads[2 * part_in : 2 * part_in + KERNEL_TAPS * part_conv].reshape(KERNEL_TAPS, part_conv, inner_half),
        narrow_part(9),
        narrow_part(10),
        narrow_part(11),
        grads[part_in : 2 * part_in].T,
        wide_part(4),
    )


def solution(mesh):
    placed = (
        P(None, "seq", "ch"),
        P(None, "seq", "ch"),
        P(),
        P(None, "seq"),
        P("ch"),
        P("ch"),
        P("seq", "ch"),
        P("ch"),
        P("ch"),
        P("ch"),
        P(None, "seq", "ch"),
        P("ch"),
        P("ch"),
        P("ch"),
        P("ch", "seq"),
        P("ch"),
    )
    run = fast_body if mesh.shape["seq"] == 16 else body
    return jax.shard_map(
        run,
        mesh=mesh,
        in_specs=placed,
        out_specs=(
            P(None, "seq", "ch"),
            P(None, "seq", "ch"),
            P("ch"),
            P("ch"),
            P("seq", "ch"),
            P("ch"),
            P("ch"),
            P("ch"),
            P(None, "seq", "ch"),
            P("ch"),
            P("ch"),
            P("ch"),
            P("ch", "seq"),
            P("ch"),
        ),
        check_vma=False,
    )
```

time: 584 us -> 308 us (0.53); the launches traced: 574 us -> 304 us
  blocking collectives: 226 us -> 0 us
  Pallas kernels: 0 us -> 185 us
  matrix products: 99.2 us -> 0 us
  other arithmetic: 93.9 us -> 16.8 us
  local copies, waits for them, and re-layouts: 52.2 us -> 19.4 us
  starting transfers between devices: 22.2 us -> 3.62 us
    pallas_call x0 -> x1, Pallas kernels: none -> 185 us  [fast_call(): pl.pallas_call(fast_kernel, out_shape=[jax.ShapeDtypeStruct(shape, dtype)...]
    psum x1 -> x0, blocking collectives: 117 us -> none  [body(): lax.psum(jnp.concatenate([small.reshape(2, -1) for small in smalls], axis...]
    all_gather x1 -> x0, blocking collectives: 109 us -> none  [body(): lax.all_gather(jnp.concatenate([first_gain, first_shift, out_bias, in_bia...]
    dot_general x9 -> x0, matrix products: 99.2 us -> none  [dot(): lax.dot_general(left, right, (over, ((), ())), preferred_element_type=jnp...]
    all_gather x3 -> x1, waiting for transfers between devices: 18.7 us -> 62 us  [fast_body(): gathered = lax.all_gather(both, 'seq', axis=0)]
    unnamed x12 -> x1, waiting for transfers between devices: 29.5 us -> 0.02 us
    unnamed x105 -> x22, local copies, waits for them, and re-layouts: 27.1 us -> 1.62 us
    reduce_sum x8 -> x1, other arithmetic: 23.2 us -> 0.68 us  [fast_body(): jnp.sum((places[:, None] >= bounds[None, :]).astype(jnp.int32), axis=1)]
  transfers between devices with their start and end apart: 20 -> 4, of which waited for: 6 -> 2; matrix products, arithmetic and copies ran while one was open for 38% -> 4% of each run, Pallas kernels for 0% -> 0%
where the time goes in v2:
time: 308 us; the launch traced here: 304 us
  Pallas kernels  185 us (60%)
  waiting for transfers between devices  65.3 us (21%)
  local copies, waits for them, and re-layouts  19.4 us (6%)
  other arithmetic  16.8 us (5%)
  between operations  14.2 us (5%)
  starting transfers between devices  3.62 us (1%)
    pallas_call x1, Pallas kernels, fast_call(): pl.pallas_call(fast_kernel, out_shape=[jax.ShapeDtypeStruct(shape, dtype)...  185 us
    all_gather x1, waiting for transfers between devices, fast_body(): gathered = lax.all_gather(both, 'seq', axis=0)  62 us
    select_n x2, other arithmetic, placed(): jnp.where(low_side, jnp.stack([own, back], 0), jnp.stack([back, own], 0))  8.22 us
  transfers between devices with their start and end apart: 4, of which 2 were waited for; matrix products, arithmetic and copies ran while one was open for 4% of the time, Pallas kernels for 0%

profile of v2, /device:TPU:24, one launch (start us, length us, event | category | flops | bytes accessed | tf_op | source)
XLA Modules:
  0.0 303.9 jit_solution(636600443916683565)
XLA Ops:
  7.2 0.0 copy-start
  7.2 0.0 copy-start.6
  7.2 0.0 all-gather.2.cloned.1.call-start
  7.3 1.0 pad_maximum_fusion
  8.2 0.9 concatenate.30
  9.1 1.5 collective-permute-start.1
  10.6 0.5 collective-permute-start
  11.1 3.5 %dynamic-slice_bitcast_fusion = bf16[2048,640]{1,0:T(8,128)(2,1)} fusion(bf16[2,2048,640]{2,1,0:T(8,128)(2,1)} %tokens.1, s32[]{:T(128)S(6)} %select_n.79), kind=kLoop, calls=%fused_computation.4 | loop fusion | bytes 5242884 | tf_op jit(solution)/shard_map/jit(dynamic_index_in_dim)/squeeze | solution.py:971
  14.6 3.2 %collective-permute-done = f32[3840]{0:T(1024)S(1)} collective-permute-done((f32[3840]{0:T(1024)S(1)}, f32[3840]{0:T(1024)S(1)}, u32[]{:S(2)}, u32[]{:S(2)}) %collective-permute-start) | collective-permute-done | bytes 15392 | tf_op jit(solution)/shard_map/ppermute | solution.py:965
  17.8 0.0 collective-permute-done.1
  17.8 1.1 maximum_select_fusion.2
  18.9 0.0 all-gather.2.cloned.1.call-update
  18.9 1.6 collective-permute-start.2
  20.5 0.0 copy-done
  20.5 0.1 copy.41
  20.6 0.2 reduce-window.4
  20.8 0.1 slice_reduce_fusion
  20.9 0.7 convert_reduce_fusion
  21.6 0.1 fusion.4
  21.8 0.0 copy-done.6
  21.8 0.1 stack.89
  21.9 1.0 copy.43.masks
  23.0 0.1 maximum_select_fusion.3
  23.0 0.1 fusion.17
  23.1 0.1 stack_reshape.30
  23.2 0.1 stack_reshape.31
  23.3 0.1 stack_reshape.32
  23.4 0.1 stack_reshape.33
  23.4 0.1 stack_reshape.34
  23.5 0.1 stack_reshape.35
  23.7 0.6 stack.95.narrow
  24.3 0.6 pad_maximum_fusion.1.wide
  24.9 62.0 %all-gather.2.cloned.1.call-done = bf16[16,360,640]{2,1,0:T(8,128)(2,1)} async-done(((bf16[1,360,640]{2,1,0:T(8,128)(2,1)}), bf16[16,360,640]{2,1,0:T(8,128)(2,1)}) %all-gather.2.cloned.1.call-update) | async-done | bytes 7372816 | tf_op jit(solution)/shard_map/all_gather | solution.py:995
  87.0 0.0 slice-start
  87.0 0.0 copy-start.2
  87.0 2.2 slice-done
  89.1 2.6 copy.42
  91.7 1.1 copy-done.2
  92.8 1.9 fusion.15
  94.7 0.0 collective-permute-done.2.x_other
  94.7 184.6 %shard_map.263 = (bf16[2048,640]{1,0:T(8,128)(2,1)}, bf16[2048,640]{1,0:T(8,128)(2,1)}, f32[2048,640]{1,0:T(8,128)}, bf16[2048,640]{1,0:T(8,128)(2,1)}, f32[368,...) custom-call(bf16[2,2048,640]{2,1,0:T(8,128)(2,1)} %tokens.1, ...), custom_call_target="tpu_custom_call" | custom-call | flops 45298483200 | bytes 125829120 | tf_op jit(solution)/shard_map/pallas_call | solution.py:898
  279.3 1.4 slice_select_fusion
  280.8 0.7 slice.137
  281.5 0.0 slice-start.1
  281.5 0.7 slice_bitcast_fusion
  282.2 0.0 copy-start.5
  282.2 0.0 slice-start.2
  282.2 3.5 %fusion = f32[1,2048,640]{2,1,0:T(8,128)S(1)} fusion(bf16[2048,640]{1,0:T(8,128)(2,1)} %get-tuple-element.33, bf16[2,2048,640]{2,1,0:T(8,128)(2,1)} %cot.1, s32[]{:T(128)S(6)} %select_n.79), kind=kLoop, calls=%fused_computation.3 | loop fusion | flops 3932160 | bytes 10485764 | tf_op jit(solution)/shard_map/stack | solution.py:1030
  285.7 0.0 copy-done.5
  285.7 0.6 fusion.16
  286.3 0.7 fusion.12
  287.0 0.7 fusion.10
  287.7 0.7 fusion.8
  288.4 0.0 slice-done.1
  288.4 0.0 slice-done.2
  288.4 0.0 copy-start.3
  288.4 0.0 copy-start.4
  288.4 5.2 %maximum_select_fusion = f32[2,2048,640]{2,1,0:T(8,128)} fusion(f32[1,2048,640]{2,1,0:T(8,128)S(1)} %fusion, f32[1,2048,640]{2,1,0:T(8,128)S(1)} %bitcast.42, pred[]{:T(512)S(6)} %eq.18), kind=kLoop, calls=%fused_computation | loop fusion | flops 7864320 | bytes 20971520 | tf_op jit(solution)/shard_map/jit(_where)/select_n | solution.py:1030
  293.6 0.0 copy-start.1
  293.6 0.0 copy-done.3
  293.6 0.5 copy-done.4
  294.1 3.0 maximum_select_fusion.1
  297.1 0.0 copy-done.1
  (17 shorter events, 0.1 us)
Async XLA Ops:
  7.2 13.3 %copy-start = (s32[2,128]{1,0:T(2,128)S(1)}, s32[2,128]{1,0:T(2,128)}, u32[]{:S(2)}) copy-start(s32[2,128]{1,0:T(2,128)} %param.18) | copy-start | bytes 3076
  7.2 14.6 %copy-start.6 = (s32[2,2048]{1,0:T(2,128)S(1)}, s32[2,2048]{1,0:T(2,128)}, u32[]{:S(2)}) copy-start(s32[2,2048]{1,0:T(2,128)} %param.19) | copy-start | bytes 49156
  7.2 79.7 %all-gather.2.cloned.1.call-start = ((), (), s32[]{:S(2)}) async-start(), calls=%async_computation | async-start | bytes 7833600 | tf_op jit(solution)/shard_map/all_gather | solution.py:995
  9.1 8.7 %collective-permute-start.1 = (bf16[360,320]{1,0:T(8,128)(2,1)S(1)}, bf16[360,320]{1,0:T(8,128)(2,1)S(1)}, u32[]{:S(2)}, u32[]{:S(2)}) collective-permute-start(bf16[360,320]{1,0:T(8,128)(2,1)S(1)} %pad_maximum_fusion), channel_id=1, source_target_pairs={{0,1},{1,0},{2,3},{3,2},{4,5},{5,4},{6,7},{7,6},{8,9},{9,8},{10,11... | collective-permute-start | bytes 691208 | tf_op jit(solution)/shard_map/ppermute | solution.py:965
  10.6 7.2 %collective-permute-start = (f32[3840]{0:T(1024)S(1)}, f32[3840]{0:T(1024)S(1)}, u32[]{:S(2)}, u32[]{:S(2)}) collective-permute-start(f32[3840]{0:T(1024)S(1)} %concatenate.30), channel_id=1, source_target_pairs={{0,1},{1,0},{2,3},{3,2},{4,5},{5,4},{6,7},{7,6},{8,9},{9,8},{10,11... | collective-permute-start | bytes 46088 | tf_op jit(solution)/shard_map/ppermute | solution.py:965
  18.9 75.8 %collective-permute-start.2 = (bf16[2048,640]{1,0:T(8,128)(2,1)}, bf16[2048,640]{1,0:T(8,128)(2,1)}, u32[]{:S(2)}, u32[]{:S(2)}) collective-permute-start(bf16[2048,640]{1,0:T(8,128)(2,1)} %dynamic-slice_bitcast_fusion), channel_id=1, source_target_pairs={{0,1},{1,0},{2,3},{3,2},{4,5},{5,4},{6,7},{7,6},{8,9},{9,8},{10,11... | collective-permute-start | bytes 7864328 | tf_op jit(solution)/shard_map/ppermute | solution.py:965
  87.0 2.2 slice-start
  87.0 5.8 %copy-start.2 = (bf16[16,360,640]{2,1,0:T(8,128)(2,1)S(1)}, bf16[16,360,640]{2,1,0:T(8,128)(2,1)}, u32[]{:S(2)}) copy-start(bf16[16,360,640]{2,1,0:T(8,128)(2,1)} %all-gather.2.cloned.1.call-done) | copy-start | bytes 22118404
  281.5 6.9 %slice-start.1 = ((s8[5242880]{0:T(1024)(128)(4,1)}), s8[4194304]{0:T(1024)(128)(4,1)S(1)}, s32[]{:S(2)}) async-start(s8[5242880]{0:T(1024)(128)(4,1)} %bitcast.40), calls=%async_computation.2 | async-start | bytes 8388608
  282.2 3.5 %copy-start.5 = (f32[16,640]{1,0:T(8,128)S(1)}, f32[16,640]{1,0:T(8,128)}, u32[]{:S(2)}) copy-start(f32[16,640]{1,0:T(8,128)} %get-tuple-element.34) | copy-start | bytes 122884
  282.2 6.2 %slice-start.2 = ((s8[5242880]{0:T(1024)(128)(4,1)}), s8[1048576]{0:T(1024)(128)(4,1)S(1)}, s32[]{:S(2)}) async-start(s8[5242880]{0:T(1024)(128)(4,1)} %bitcast.40), calls=%async_computation.3 | async-start | bytes 2097152
  288.4 5.2 %copy-start.3 = (bf16[2048,640]{1,0:T(8,128)(2,1)S(1)}, bf16[2048,640]{1,0:T(8,128)(2,1)}, u32[]{:S(2)}) copy-start(bf16[2048,640]{1,0:T(8,128)(2,1)} %get-tuple-element.30) | copy-start | bytes 7864324
  288.4 5.7 %copy-start.4 = (bf16[2048,640]{1,0:T(8,128)(2,1)S(1)}, bf16[2048,640]{1,0:T(8,128)(2,1)}, u32[]{:S(2)}) copy-start(bf16[2048,640]{1,0:T(8,128)(2,1)} %get-tuple-element.31) | copy-start | bytes 7864324
  293.6 3.5 %copy-start.1 = (s32[2,128]{1,0:T(2,128)S(1)}, s32[2,128]{1,0:T(2,128)}, u32[]{:S(2)}) copy-start(s32[2,128]{1,0:T(2,128)} %param.18) | copy-start | bytes 3076
Sparse Core Ops, SparseCore 0:
  19.1 67.8 all-gather.1

commit v3 on v2

--- a/solution.py
+++ b/solution.py
@@ -481,18 +481,23 @@
 BLOCK = 256
 CHUNKS = 4
 CONV_PAD = 8
+EARLY = 384
+FIRST = 512
+HEAD = 4
 
 
 def fast_kernel(
-    tokens, x_other, cot, masks, w_in, w_out, w_conv, wide, narrow,
-    out_own, out_back, dx_own, dx_back, grads, smalls,
-    gy_other, out_send, dx_send, s1, h1, s2, h3, s3,
-    a1v, a2f, a3v, gyv, dh3f,
+    tokens, x_other, cot, gy_early, gathered, masks, wide, narrow,
+    out_own, out_back, dx_own, dx_back, dx_tail, grads_out, sums_out,
+    s1, h1, s2, h3, s3,
+    a1v, a2f, a3v, gyv, dh3f, out_send, w_in, w_out, w_conv,
     k_in, s_in, r0_in, r1_in, r2_in, r3_in,
     k_out, s_out, r0_out, r1_out, r2_out, r3_out,
-    k_conv, s_conv, r0_conv, r1_conv, r2_conv, r3_conv,
-    cross_send, cross_recv, small_send, small_recv,
-    gy_sems, out_sems, dx_sems, a2_sems, dh3_sems, in_sems, out_rs_sems, conv_sems, cross_sems, small_sems,
+    k_low, s_low, r0_low, r1_low, r2_low, r3_low,
+    k_mid, s_mid, r0_mid, r1_mid, r2_mid, r3_mid,
+    k_top, s_top, r0_top, r1_top, r2_top, r3_top,
+    smalls, grads, cross_send, cross_recv, small_send, small_recv, load_sems,
+    gy_sems, out_sems, dx_sems, a2_sems, dh3_sems, in_sems, out_rs_sems, low_sems, mid_sems, top_sems, cross_sems, small_sems,
 ):
     rows = a1v.shape[0]
     half = tokens.shape[2]
@@ -517,17 +522,42 @@
             device_id_type=pl.DeviceIdType.MESH,
         )
 
-    def chunk(ref, at):
-        return ref.at[pl.ds(pl.multiple_of(at * part, part), part)]
+    def block(ref, at):
+        return ref.at[pl.ds(pl.multiple_of(at * BLOCK, BLOCK), BLOCK)]
+
+    early = gy_early.shape[0]
 
     def gy_copy(at):
-        return remote(chunk(cot.at[1 - side], at), chunk(gy_other, at), gy_sems, at, across)
+        begin = max(at * part, early)
+        piece = pl.ds(begin, (at + 1) * part - begin)
+        return remote(cot.at[1 - side, piece], gyv.at[side, piece], gy_sems, at, across)
+
+    gy_chunks = [at for at in range(CHUNKS) if (at + 1) * part > early]
+    part_in = w_in.shape[1]
+    tail_rows = k_top.shape[1]
+    loads = [
+        pltpu.make_async_copy(src, dst, load_sems.at[at])
+        for at, (src, dst) in enumerate(
+            (
+                (gathered.at[:, pl.ds(0, part_in)], w_in),
+                (gathered.at[:, pl.ds(part_in, part_in)], w_out),
+                (gathered.at[pl.ds(0, 8), pl.ds(2 * part_in, part_in)], s_low),
+                (gathered.at[pl.ds(8, 8), pl.ds(2 * part_in, part_in)], r0_low),
+                (gathered.at[pl.ds(0, 8), pl.ds(3 * part_in, part_in)], s_mid),
+                (gathered.at[pl.ds(8, 8), pl.ds(3 * part_in, part_in)], r0_mid),
+                (gathered.at[pl.ds(0, 8), pl.ds(4 * part_in, tail_rows)], s_top),
+                (gathered.at[pl.ds(8, 8), pl.ds(4 * part_in, tail_rows)], r0_top),
+                (gy_early, gyv.at[1 - side, pl.ds(0, early)]),
+                (cot.at[side], gyv.at[side]),
+            )
+        )
+    ]
 
     def out_copy(at):
-        return remote(chunk(out_send, at), chunk(out_back, at), out_sems, at, across)
+        return remote(block(out_send, at), block(out_back, at), out_sems, at, across)
 
     def dx_copy(at):
-        return remote(chunk(dx_send, at), chunk(dx_back, at), dx_sems, at, across)
+        return remote(block(gyv.at[1 - side], at), block(dx_back, at), dx_sems, at, across)
 
     def halo_low(framed_rows, sems):
         return remote(framed_rows.at[pl.ds(HALO, HALO)], framed_rows.at[pl.ds(HALO + rows, HALO)], sems, 0, before)
@@ -555,17 +585,24 @@
             halo_high(framed_rows, sems).wait_send()
             halo_low(framed_rows, sems).wait_recv()
 
+    blocks = rows // BLOCK
+
     def middle_first(step):
-        late = step // 2
-        return (step + 1) * (1 - late) + late * (step - 2) * 3
-
-    def pipeline(step, blocks, ins, outs):
+        late = step // (blocks - 2)
+        return (step + 1) * (1 - late) + late * (step - (blocks - 2)) * (blocks - 1)
+
+    def in_order(step):
+        return step
+
+    def pipeline(step, order, ins, outs, tail=None):
         def spec(ref):
-            return pl.BlockSpec((BLOCK, ref.shape[-1]), lambda i: (i, 0))
-
-        pltpu.emit_pipeline(
-            step, grid=(blocks,), in_specs=[spec(r) for r in ins], out_specs=[spec(r) for r in outs]
-        )(*ins, *outs)
+            return pl.BlockSpec((BLOCK, ref.shape[-1]), lambda i: (order(i), 0))
+
+        out_specs = [spec(r) for r in outs]
+        if tail is not None:
+            outs = outs + [tail]
+            out_specs.append(pl.BlockSpec((BLOCK, half), lambda i: (jnp.maximum(i - HEAD, 0), 0)))
+        pltpu.emit_pipeline(step, grid=(blocks,), in_specs=[spec(r) for r in ins], out_specs=out_specs)(*ins, *outs)
 
     barrier = pltpu.get_barrier_semaphore()
     ring = [{"seq": lax.rem(place + last, last + 1)}, {"seq": lax.rem(place + 1, last + 1)}]
@@ -573,8 +610,10 @@
         pl.semaphore_signal(barrier, inc=1, device_id=device, device_id_type=pl.DeviceIdType.MESH)
     pl.semaphore_wait(barrier, 7)
 
-    for at in range(CHUNKS):
+    for at in gy_chunks:
         gy_copy(at).start()
+    for load in loads:
+        load.start()
     smalls[...] = jnp.zeros_like(smalls)
 
     @pl.when(place == 0)
@@ -595,7 +634,7 @@
         act = act.astype(jnp.bfloat16)
         a1v[pl.ds(base, BLOCK), :] = act
         s1_block[...] = slope
-        value = dot(act, w_in[...]) + narrow[0:1, :]
+        value = dot(act, w_in[...].reshape(2 * half, inner)) + narrow[0:1, :]
         h1_block[...] = value
         normed, _ = norm(value)
         act, slope = gelu_both(normed * narrow[1:2, :] + narrow[2:3, :])
@@ -603,41 +642,57 @@
         a2f[pl.ds(HALO + base, BLOCK), :] = (act * keep).astype(jnp.bfloat16)
         s2_block[...] = slope * keep
 
-    pipeline(first, rows // BLOCK, [tokens.at[side], x_other], [s1, h1, s2])
+    loads[0].wait()
+    pipeline(first, in_order, [tokens.at[side], x_other], [s1, h1, s2])
+    for at in range(2, 8):
+        loads[at].wait()
+    height = inner // 16
+
+    def relay(pair, _):
+        for group, sources in enumerate(((s_low, s_mid, s_top), (r0_low, r0_mid, r0_top))):
+            at = pl.multiple_of((4 * group + pair) * 2 * height, 2 * height)
+            tap = 0
+            for source in sources:
+                even = source[2 * pair].astype(jnp.float32)
+                odd = source[2 * pair + 1].astype(jnp.float32)
+                for top in range(0, source.shape[1] - CONV_PAD, height):
+                    w_conv[tap, pl.ds(at, 2 * height), :] = jnp.concatenate(
+                        [even[top : top + height], odd[top : top + height]], axis=0
+                    ).astype(jnp.bfloat16)
+                    tap += 1
+        return 0
+
+    lax.fori_loop(0, 4, relay, 0)
+    loads[1].wait()
     halo_start(a2f, a2_sems)
 
-    def forward_chunk(step, _):
+    def second(own, other, h3_block, s3_block, own_block):
+        step = pl.program_id(0)
         at = middle_first(step)
-
-        @pl.when(step == 2)
+        base = pl.multiple_of(at * BLOCK, BLOCK)
+
+        @pl.when(step == blocks - 2)
         def _():
             halo_wait(a2f, a2_sems)
 
-        def second(own, other, h3_block, s3_block, own_block, other_block):
-            base = pl.multiple_of(at * part + pl.program_id(0) * BLOCK, BLOCK)
-            taps = masks[pl.ds(base, BLOCK), :]
-            value = dot(windowed(a2f, taps, base, BLOCK), w_conv[...]) + narrow[3:4, :]
-            h3_block[...] = value
-            normed, _ = norm(value)
-            act, slope = gelu_both(normed * narrow[4:5, :] + narrow[5:6, :])
-            act = act.astype(jnp.bfloat16)
-            a3v[pl.ds(base, BLOCK), :] = act
-            s3_block[...] = slope
-            mixed = dot(act, w_out[...], ((1,), (1,))) + wide[2:3, :]
-            left, right = mixed[:, :half], mixed[:, half:]
-            own_block[...] = (own[...].astype(jnp.float32) + jnp.where(low, left, right)).astype(jnp.bfloat16)
-            other_block[...] = (other[...].astype(jnp.float32) + jnp.where(low, right, left)).astype(jnp.bfloat16)
-
-        pipeline(
-            second,
-            part // BLOCK,
-            [chunk(tokens.at[side], at), chunk(x_other, at)],
-            [chunk(h3, at), chunk(s3, at), chunk(out_own, at), chunk(out_send, at)],
-        )
+        taps = masks[pl.ds(base, BLOCK), :]
+        weight = w_conv[...].reshape(KERNEL_TAPS * inner, inner)
+        value = dot(windowed(a2f, taps, base, BLOCK), weight) + narrow[3:4, :]
+        h3_block[...] = value
+        normed, _ = norm(value)
+        act, slope = gelu_both(normed * narrow[4:5, :] + narrow[5:6, :])
+        act = act.astype(jnp.bfloat16)
+        a3v[pl.ds(base, BLOCK), :] = act
+        s3_block[...] = slope
+        mixed = dot(act, w_out[...].reshape(2 * half, inner), ((1,), (1,))) + wide[2:3, :]
+        left, right = mixed[:, :half], mixed[:, half:]
+        own_block[...] = (own[...].astype(jnp.float32) + jnp.where(low, left, right)).astype(jnp.bfloat16)
+        out_send[pl.ds(base, BLOCK), :] = (
+            other[...].astype(jnp.float32) + jnp.where(low, right, left)
+        ).astype(jnp.bfloat16)
         out_copy(at).start()
-        return 0
-
-    lax.fori_loop(0, CHUNKS, forward_chunk, 0)
+
+    pipeline(second, middle_first, [tokens.at[side], x_other], [h3, s3, out_own])
 
     def add_small(row, value):
         smalls[row : row + 1, :] += value
@@ -646,101 +701,107 @@
         smalls[row : row + 1, :] += value[:, :half]
         smalls[row + 1 : row + 2, :] += value[:, half:]
 
-    def third_chunk(at, _):
-        gy_copy(at).wait_recv()
-
-        def third(own, other, h3_block, s3_block):
-            base = pl.multiple_of(at * part + pl.program_id(0) * BLOCK, BLOCK)
-            gy = jnp.concatenate(ordered(side, own[...], other[...]), axis=1)
-            add_wide(4, column_sums(gy))
-            gy = gy.astype(jnp.bfloat16)
-            gyv[pl.ds(base, BLOCK), :] = gy
-            dz3 = dot(gy, w_out[...]) * s3_block[...]
-            normed, scale = norm(h3_block[...])
-            dh3 = norm_back(dz3, normed, scale, narrow[4:5, :]).astype(jnp.bfloat16)
-            dh3f[pl.ds(HALO + base, BLOCK), :] = dh3
-            add_small(9, column_sums(dh3.astype(jnp.float32)))
-            add_small(10, column_sums(dz3 * normed))
-            add_small(11, column_sums(dz3))
-
-        pipeline(
-            third,
-            part // BLOCK,
-            [chunk(cot.at[side], at), chunk(gy_other, at), chunk(h3, at), chunk(s3, at)],
-            [],
-        )
-        return 0
-
-    lax.fori_loop(0, CHUNKS, third_chunk, 0)
+    per = part // BLOCK
+
+    def third(h3_block, s3_block):
+        at = pl.program_id(0)
+        base = pl.multiple_of(at * BLOCK, BLOCK)
+        for later in gy_chunks:
+
+            @pl.when(at == later * per)
+            def _():
+                gy_copy(later).wait_recv()
+
+        gy = jnp.concatenate([gyv[0, pl.ds(base, BLOCK), :], gyv[1, pl.ds(base, BLOCK), :]], axis=1)
+        add_wide(4, column_sums(gy.astype(jnp.float32)))
+        dz3 = dot(gy, w_out[...].reshape(2 * half, inner)) * s3_block[...]
+        normed, scale = norm(h3_block[...])
+        dh3 = norm_back(dz3, normed, scale, narrow[4:5, :]).astype(jnp.bfloat16)
+        dh3f[pl.ds(HALO + base, BLOCK), :] = dh3
+        add_small(9, column_sums(dh3.astype(jnp.float32)))
+        add_small(10, column_sums(dz3 * normed))
+        add_small(11, column_sums(dz3))
+
+    loads[8].wait()
+    loads[9].wait()
+    pipeline(third, in_order, [h3, s3], [])
     halo_start(dh3f, dh3_sems)
 
-    def split(keep_ref, send_ref, at, row, even, odd):
-        height = even.shape[0]
+    def slot(pair, order):
+        two = (pair % 4) if order[0] == 1 else (pair % 4) // 2 + 2 * (pair % 2)
+        return pair // 4 * 4 + two
+
+    def split(group, at, even, odd):
+        keep_ref, send_ref = group[0], group[1]
         mine_first = bits[0] == 0
-        keep_ref[at, row : row + height, :] = jnp.where(mine_first, even, odd)
-        send_ref[at, row : row + height, :] = jnp.where(mine_first, odd, even).astype(jnp.bfloat16)
-
-    def wide_grad(left_ref, right_ref, keep_ref, send_ref):
-        height = keep_ref.shape[1]
+        keep_ref[at] = jnp.where(mine_first, even, odd)
+        send_ref[at] = jnp.where(mine_first, odd, even).astype(jnp.bfloat16)
+
+    def wide_grad(left_of, right_ref, group):
+        tall_rows = group[0].shape[1]
 
         def tile(at, _):
-            columns = pl.ds(pl.multiple_of(at * half, 128), half)
-            value = dot(left_ref[:, columns], right_ref[...], ((0,), (0,)))
-            for pair in range(half // (2 * height)):
-                top = 2 * pair * height
+            value = dot(left_of(at), right_ref[...], ((0,), (0,)))
+            for pair in range(4):
+                top = 2 * pair * tall_rows
                 split(
-                    keep_ref,
-                    send_ref,
-                    at * (half // (2 * height)) + pair,
-                    0,
-                    value[top : top + height],
-                    value[top + height : top + 2 * height],
+                    group,
+                    at * 4 + slot(pair, group[4]),
+                    value[top : top + tall_rows],
+                    value[top + tall_rows : top + 2 * tall_rows],
                 )
             return 0
 
         lax.fori_loop(0, 2, tile, 0)
-
-    def conv_grads():
-        height = inner // 16
+        sum_copy(group, 0).start()
+
+    def conv_grad_of(taps, group):
         right = dh3f.at[pl.ds(HALO, rows)]
-        for taps in ((0, 1), (2, 3), (4,)):
-            values = []
-            for tap in taps:
-                left = a2f[tap * DILATION_STEP : tap * DILATION_STEP + rows, :] * masks[:, tap : tap + 1]
-                values.append(dot(left, right[...], ((0,), (0,))))
-            if len(values) == 1:
-                tail = [jnp.zeros((CONV_PAD, inner), jnp.float32)]
-            else:
-                tail = []
-            for pair in range(8):
-                top = 2 * pair * height
-                even = jnp.concatenate([v[top : top + height] for v in values] + tail, axis=0)
-                odd = jnp.concatenate([v[top + height : top + 2 * height] for v in values] + tail, axis=0)
-                split(k_conv, s_conv, pair, taps[0] * height, even, odd)
-
-    in_set = (k_in, s_in, (r0_in, r1_in, r2_in, r3_in), in_sems)
-    out_set = (k_out, s_out, (r0_out, r1_out, r2_out, r3_out), out_rs_sems)
-    conv_set = (k_conv, s_conv, (r0_conv, r1_conv, r2_conv, r3_conv), conv_sems)
+        values = []
+        for tap in taps:
+            left = a2f[tap * DILATION_STEP : tap * DILATION_STEP + rows, :] * masks[:, tap : tap + 1]
+            values.append(dot(left, right[...], ((0,), (0,))))
+        if len(values) == 1:
+            tail = [jnp.zeros((CONV_PAD, inner), jnp.float32)]
+        else:
+            tail = []
+        for pair in range(8):
+            top = 2 * pair * height
+            split(
+                group,
+                slot(pair, group[4]),
+                jnp.concatenate([v[top : top + height] for v in values] + tail, axis=0),
+                jnp.concatenate([v[top + height : top + 2 * height] for v in values] + tail, axis=0),
+            )
+        sum_copy(group, 0).start()
+
+    y_first, z_first = (1, 2, 3), (2, 1, 3)
+    in_set = (k_in, s_in, (r0_in, r1_in, r2_in, r3_in), in_sems, y_first)
+    out_set = (k_out, s_out, (r0_out, r1_out, r2_out, r3_out), out_rs_sems, z_first)
+    low_set = (k_low, s_low, (r0_low, r1_low, r2_low, r3_low), low_sems, y_first)
+    mid_set = (k_mid, s_mid, (r0_mid, r1_mid, r2_mid, r3_mid), mid_sems, z_first)
+    top_set = (k_top, s_top, (r0_top, r1_top, r2_top, r3_top), top_sems, y_first)
     starts = (0, 0, 4, 6)
     lengths = (8, 4, 2, 1)
 
     def sum_copy(group, level):
-        _, send, received, sems = group
+        _, send, received, sems, order = group
+        bit = 0 if level == 0 else order[level - 1]
         return remote(
-            send.at[pl.ds(starts[level], lengths[level])], received[level], sems, level, pairs[level]
+            send.at[pl.ds(starts[level], lengths[level])], received[level], sems, level, pairs[bit]
         )
 
     def sum_step(group, level):
-        keep, send, received, _ = group
+        keep, send, received, _, order = group
         sum_copy(group, level).wait()
         came = received[level]
         fixed = 0
-        for bit in range(level):
-            fixed = fixed + bits[bit + 1] * (1 << bit)
+        for at in range(level):
+            fixed = fixed + bits[order[at]] * (1 << at)
         if level == 3:
             keep[fixed] = keep[fixed] + came[0].astype(jnp.float32)
             return
-        mine = bits[level + 1]
+        mine = bits[order[level]]
 
         def one(item, _):
             other = 2 * item + 1 - mine
@@ -755,68 +816,73 @@
         lax.fori_loop(0, lengths[level + 1], one, 0)
         sum_copy(group, level + 1).start()
 
-    wide_grad(gyv, a3v, k_out, s_out)
-    sum_copy(out_set, 0).start()
-    conv_grads()
-    sum_copy(conv_set, 0).start()
-    sum_step(out_set, 0)
+    def at_step(step, when, *steps):
+        @pl.when(step == when)
+        def _():
+            for group, level in steps:
+                sum_step(group, level)
+
+    conv_grad_of((0, 1), low_set)
+    conv_grad_of((2, 3), mid_set)
+    conv_grad_of((4,), top_set)
+    wide_grad(lambda at: gyv[at], a3v, out_set)
+
+    def fourth(h1_block, s2_block):
+        step = pl.program_id(0)
+        base = pl.multiple_of(step * BLOCK, BLOCK)
+        taps = masks[pl.ds(base, BLOCK), :]
+        da2 = jnp.zeros((BLOCK, inner), jnp.float32)
+        for tap in range(KERNEL_TAPS):
+            window = dh3f[pl.ds(base + tap * DILATION_STEP, BLOCK), :] * taps[:, tap : tap + 1]
+            da2 = da2 + dot(window, w_conv[KERNEL_TAPS - 1 - tap], ((1,), (1,)))
+        dz2 = da2 * s2_block[...]
+        normed, scale = norm(h1_block[...])
+        dh1 = norm_back(dz2, normed, scale, narrow[1:2, :]).astype(jnp.bfloat16)
+        a3v[pl.ds(base, BLOCK), :] = dh1
+        add_small(6, column_sums(dh1.astype(jnp.float32)))
+        add_small(7, column_sums(dz2 * normed))
+        add_small(8, column_sums(dz2))
+        at_step(step, 0, (low_set, 0), (mid_set, 0), (top_set, 0))
+        at_step(step, 1, (out_set, 0))
+        at_step(step, 5, (low_set, 1))
+        at_step(step, 6, (mid_set, 1))
+        at_step(step, 7, (top_set, 1))
+
     halo_wait(dh3f, dh3_sems)
-
-    def fourth_chunk(step, _):
-        at = middle_first(step)
-
-        def fourth(own, other, gy_own, h1_block, s2_block, s1_block, own_block, other_block):
-            base = pl.multiple_of(at * part + pl.program_id(0) * BLOCK, BLOCK)
-            taps = masks[pl.ds(base, BLOCK), :]
-            da2 = jnp.zeros((BLOCK, inner), jnp.float32)
-            for tap in range(KERNEL_TAPS):
-                window = dh3f[pl.ds(base + tap * DILATION_STEP, BLOCK), :] * taps[:, tap : tap + 1]
-                weight = w_conv[(KERNEL_TAPS - 1 - tap) * inner : (KERNEL_TAPS - tap) * inner, :]
-                da2 = da2 + dot(window, weight, ((1,), (1,)))
-            dz2 = da2 * s2_block[...]
-            normed, scale = norm(h1_block[...])
-            dh1 = norm_back(dz2, normed, scale, narrow[1:2, :]).astype(jnp.bfloat16)
-            a3v[pl.ds(base, BLOCK), :] = dh1
-            add_small(6, column_sums(dh1.astype(jnp.float32)))
-            add_small(7, column_sums(dz2 * normed))
-            add_small(8, column_sums(dz2))
-            dz1 = dot(dh1, w_in[...], ((1,), (1,))) * s1_block[...]
-            x = jnp.concatenate(ordered(side, own[...], other[...]), axis=1)
-            normed, scale = norm(x)
-            dx = norm_back(dz1, normed, scale, wide[0:1, :])
-            add_wide(0, column_sums(dz1 * normed))
-            add_wide(2, column_sums(dz1))
-            left, right = dx[:, :half], dx[:, half:]
-            own_block[...] = jnp.where(low, left, right) + gy_own[...].astype(jnp.float32)
-            other_block[...] = jnp.where(low, right, left).astype(jnp.bfloat16)
-
-        pipeline(
-            fourth,
-            part // BLOCK,
-            [
-                chunk(tokens.at[side], at),
-                chunk(x_other, at),
-                chunk(cot.at[side], at),
-                chunk(h1, at),
-                chunk(s2, at),
-                chunk(s1, at),
-            ],
-            [chunk(dx_own, at), chunk(dx_send, at)],
-        )
-        dx_copy(at).start()
-        for level in range(3):
-
-            @pl.when(step == level)
-            def _():
-                sum_step(out_set, level + 1)
-                sum_step(conv_set, level)
-
-        return 0
-
-    lax.fori_loop(0, CHUNKS, fourth_chunk, 0)
-
-    wide_grad(a1v, a3v, k_in, s_in)
-    sum_copy(in_set, 0).start()
+    pipeline(fourth, in_order, [h1, s2], [])
+    wide_grad(lambda at: a1v[:, pl.ds(pl.multiple_of(at * half, 128), half)], a3v, in_set)
+    sum_step(out_set, 1)
+    sum_step(low_set, 2)
+
+    def fifth(own, other, s1_block, own_block, tail_block):
+        step = pl.program_id(0)
+        base = pl.multiple_of(step * BLOCK, BLOCK)
+        dh1 = a3v[pl.ds(base, BLOCK), :]
+        dz1 = dot(dh1, w_in[...].reshape(2 * half, inner), ((1,), (1,))) * s1_block[...]
+        x = jnp.concatenate(ordered(side, own[...], other[...]), axis=1)
+        normed, scale = norm(x)
+        dx = norm_back(dz1, normed, scale, wide[0:1, :])
+        add_wide(0, column_sums(dz1 * normed))
+        add_wide(2, column_sums(dz1))
+        left, right = dx[:, :half], dx[:, half:]
+        own_block[...] = jnp.where(low, left, right) + gyv[side, pl.ds(base, BLOCK), :].astype(jnp.float32)
+        sent = jnp.where(low, right, left).astype(jnp.bfloat16)
+        gyv[1 - side, pl.ds(base, BLOCK), :] = sent
+        tail_block[...] = sent
+
+        @pl.when(step < HEAD)
+        def _():
+            dx_copy(step).start()
+
+        at_step(step, 0, (mid_set, 2), (in_set, 0))
+        at_step(step, 2, (out_set, 2), (top_set, 2))
+        at_step(step, 4, (low_set, 3))
+        at_step(step, 5, (mid_set, 3))
+        at_step(step, 6, (in_set, 1))
+        at_step(step, 7, (top_set, 3), (out_set, 3))
+
+    pipeline(fifth, in_order, [tokens.at[side], x_other, s1], [dx_own], dx_tail)
+
 
     def small_copy(level):
         device = pairs[level] if level < 4 else across
@@ -831,16 +897,21 @@
         smalls[...] += small_recv[level]
 
     small_start(0)
-    sum_step(conv_set, 3)
-    for level in range(4):
-        sum_step(in_set, level)
-        small_step(level)
-        small_start(level + 1)
+    sum_step(in_set, 2)
+    small_step(0)
+    small_start(1)
+    small_step(1)
+    small_start(2)
+    small_step(2)
+    small_start(3)
+    sum_step(in_set, 3)
+    small_step(3)
+    small_start(4)
 
     wanted = half // 2 + 64
-    mine = 4 * bits[3] + 2 * bits[2] + bits[1]
     row = 0
-    for keep in (k_in, k_out, k_conv):
+    for keep, _, _, _, order in (in_set, out_set, low_set, mid_set, top_set):
+        mine = bits[order[0]] + 2 * bits[order[1]] + 4 * bits[order[2]]
         height = keep.shape[1]
         value = keep[mine]
         left, right = value[:, :wanted], value[:, inner - wanted :]
@@ -849,17 +920,27 @@
         row += height
     cross = remote(cross_send, cross_recv, cross_sems, 0, across)
     cross.start()
-    for at in range(CHUNKS):
+    for at in gy_chunks:
         gy_copy(at).wait_send()
+    for at in range(blocks):
         out_copy(at).wait()
     small_step(4)
+    quarter = half // 2
+    for index in range(3):
+        both = smalls[2 * index : 2 * index + 2, :]
+        sums_out[:, index * half : (index + 1) * half] = jnp.where(low, both[0:1], both[1:2])
+    for index in range(6):
+        both = smalls[6 + index : 7 + index, :]
+        at = 3 * half + index * wanted
+        sums_out[:, at : at + quarter] = jnp.where(low, both[:, :quarter], both[:, quarter:])
     cross.wait()
-    grads[...] += cross_recv[...].astype(jnp.float32)
-    for at in range(CHUNKS):
+    total = grads[...] + cross_recv[...].astype(jnp.float32)
+    grads_out[...] = jnp.where(low, total[:, :quarter], total[:, wanted - quarter :])
+    for at in range(HEAD):
         dx_copy(at).wait()
 
 
-def fast_call(tokens, x_other, cot, masks, w_in, w_out, w_conv, wide, narrow, part_in, part_conv):
+def fast_call(tokens, x_other, cot, gy_early, gathered, masks, wide, narrow, part_in, part_conv):
     _, rows, half = tokens.shape
     model = 2 * half
     inner = narrow.shape[1]
@@ -883,11 +964,9 @@
         ((rows, half), bf16),
         ((rows, half), f32),
         ((rows, half), bf16),
-        ((total, wanted), f32),
-        ((16, inner), f32),
-        ((rows, half), bf16),
-        ((rows, half), bf16),
-        ((rows, half), bf16),
+        ((rows - HEAD * BLOCK, half), bf16),
+        ((total, half // 2), f32),
+        ((1, 3 * half + 6 * wanted), f32),
         ((rows, model), f32),
         ((rows, inner), f32),
         ((rows, inner), f32),
@@ -898,28 +977,36 @@
     results = pl.pallas_call(
         fast_kernel,
         out_shape=[jax.ShapeDtypeStruct(shape, dtype) for shape, dtype in shapes],
-        in_specs=[any_spec] * 3 + [vmem_spec] * 6,
-        out_specs=[any_spec] * 4 + [vmem_spec] * 2 + [any_spec] * 8,
+        in_specs=[any_spec] * 5 + [vmem_spec] * 3,
+        out_specs=[any_spec] * 5 + [vmem_spec] * 2 + [any_spec] * 5,
         scratch_shapes=[
             pltpu.VMEM((rows, model), bf16),
             pltpu.VMEM((rows + 2 * HALO, inner), bf16),
             pltpu.VMEM((rows, inner), bf16),
-            pltpu.VMEM((rows, model), bf16),
+            pltpu.VMEM((2, rows, half), bf16),
             pltpu.VMEM((rows + 2 * HALO, inner), bf16),
+            pltpu.VMEM((rows, half), bf16),
+            pltpu.VMEM((16, part_in, inner), bf16),
+            pltpu.VMEM((16, part_in, inner), bf16),
+            pltpu.VMEM((KERNEL_TAPS, inner, inner), bf16),
         ]
-        + sums(part_in)
-        + sums(part_in)
-        + sums(tall)
+        + sums(part_in) * 4
+        + sums(tall - 2 * part_in)
         + [
+            pltpu.VMEM((16, inner), f32),
+            pltpu.VMEM((total, wanted), f32),
             pltpu.VMEM((total, wanted), bf16),
             pltpu.VMEM((total, wanted), bf16),
             pltpu.VMEM((5, 16, inner), f32),
             pltpu.VMEM((5, 16, inner), f32),
+            pltpu.SemaphoreType.DMA((10,)),
             sems(CHUNKS),
-            sems(CHUNKS),
-            sems(CHUNKS),
+            sems(rows // BLOCK),
+            sems(HEAD),
             sems(2),
             sems(2),
+            sems(4),
+            sems(4),
             sems(4),
             sems(4),
             sems(4),
@@ -930,8 +1017,39 @@
             collective_id=0, has_side_effects=True, vmem_limit_bytes=63 * 2**20
         ),
         cost_estimate=pl.CostEstimate(flops=flops, bytes_accessed=120 * 2**20, transcendentals=0),
-    )(tokens, x_other, cot, masks, w_in, w_out, w_conv, wide, narrow)
-    return results[:6]
+    )(tokens, x_other, cot, gy_early, gathered, masks, wide, narrow)
+    return results[:7]
+
+
+def finish_kernel(side_ref, tail_ref, cot_ref, whole_ref, out_ref):
+    out_ref[0] = tail_ref[...].astype(jnp.float32) + cot_ref[0].astype(jnp.float32)
+
+
+def finish_call(side, tail, cot, grad_tokens, first):
+    half = tail.shape[1]
+
+    def theirs(i, side_ref):
+        return (1 - side_ref[0], first + i, 0)
+
+    return pl.pallas_call(
+        finish_kernel,
+        grid_spec=pltpu.PrefetchScalarGridSpec(
+            num_scalar_prefetch=1,
+            grid=(tail.shape[0] // BLOCK,),
+            in_specs=[
+                pl.BlockSpec((BLOCK, half), lambda i, side_ref: (i, 0)),
+                pl.BlockSpec((1, BLOCK, half), theirs),
+                pl.BlockSpec(memory_space=pl.ANY),
+            ],
+            out_specs=pl.BlockSpec((1, BLOCK, half), theirs),
+        ),
+        out_shape=jax.ShapeDtypeStruct(grad_tokens.shape, grad_tokens.dtype),
+        input_output_aliases={3: 0},
+        compiler_params=pltpu.CompilerParams(
+            dimension_semantics=("arbitrary",), vmem_limit_bytes=56 * 2**20
+        ),
+        cost_estimate=pl.CostEstimate(flops=tail.size, bytes_accessed=8 * tail.size, transcendentals=0),
+    )(side, tail, cot, grad_tokens)
 
 
 def fast_body(
@@ -976,13 +1094,19 @@
     part_in = proj_in.shape[0]
     part_conv = conv_weight.shape[1]
     own_weights = jnp.concatenate(
-        [proj_in, proj_out.T, conv_weight.reshape(KERNEL_TAPS * part_conv, inner_half)], axis=0
-    )
-    own_vectors, own_weights = lax.optimization_barrier((own_vectors, own_weights))
+        [
+            proj_in,
+            proj_out.T,
+            conv_weight.reshape(KERNEL_TAPS * part_conv, inner_half),
+            jnp.zeros((CONV_PAD, inner_half), bf16),
+        ],
+        axis=0,
+    )
+    x_send = other_of(tokens)
+    own_vectors, own_weights, first_send = lax.optimization_barrier(
+        (own_vectors, own_weights, x_send[:FIRST])
+    )
     other_vectors, other_weights = swap(own_vectors), swap(own_weights)
-    tokens_tied, other_vectors, other_weights = lax.optimization_barrier(
-        (other_of(tokens), other_vectors, other_weights)
-    )
     both = jnp.where(
         low_side,
         jnp.concatenate([own_weights, other_weights], axis=1),
@@ -991,16 +1115,11 @@
     vectors = jnp.where(
         low_side, jnp.stack([own_vectors, other_vectors]), jnp.stack([other_vectors, own_vectors])
     )
-    x_other = swap(tokens_tied)
+    x_first, x_second = swap(first_send), swap(x_send[FIRST:])
+    gy_tied, x_first = lax.optimization_barrier((cotangent[:, :EARLY], x_first))
+    gy_early = swap(other_of(gy_tied))
+    x_other = jnp.concatenate([x_first, x_second], axis=0)
     gathered = lax.all_gather(both, "seq", axis=0)
-    weight_in = gathered[:, :part_in].reshape(model, inner)
-    weight_out = gathered[:, part_in : 2 * part_in].reshape(model, inner)
-    weight_conv = (
-        gathered[:, 2 * part_in :]
-        .reshape(seq_count, KERNEL_TAPS, part_conv, inner)
-        .transpose(1, 0, 2, 3)
-        .reshape(KERNEL_TAPS * inner, inner)
-    )
     wide = jnp.stack([vectors[:, i * half : (i + 1) * half].reshape(-1) for i in range(3)])
     narrow = jnp.stack(
         [
@@ -1022,8 +1141,17 @@
     zero = jnp.zeros((rows,), bf16)
     masks = jnp.stack(columns + [own_of(residue_mask).astype(bf16), zero, zero], axis=1)
 
-    out_own, out_back, dx_own, dx_back, grads, smalls = fast_call(
-        tokens, x_other, cotangent, masks, weight_in, weight_out, weight_conv, wide, narrow, part_in, part_conv
+    out_own, out_back, dx_own, dx_back, dx_tail, grads, sums = fast_call(
+        tokens,
+        x_other,
+        cotangent,
+        gy_early,
+        gathered,
+        masks,
+        wide,
+        narrow,
+        part_in,
+        part_conv,
     )
 
     def placed(own, back):
@@ -1031,29 +1159,29 @@
 
     block_out = placed(out_own, out_back)
     grad_tokens = placed(dx_own, dx_back.astype(f32) + other_of(cotangent).astype(f32))
-    grads = jnp.where(low_side, grads[:, :inner_half], grads[:, grads.shape[1] - inner_half :])
-
-    def wide_part(row):
-        return lax.dynamic_index_in_dim(smalls, row + side, 0, keepdims=False)
-
-    def narrow_part(row):
-        return lax.dynamic_slice_in_dim(smalls[row], side * inner_half, inner_half, 0)
+    side_array = side.astype(jnp.int32).reshape(1)
+    grad_tokens = finish_call(side_array, swap(dx_tail), cotangent, grad_tokens, HEAD)
+    wanted = inner_half + 64
+
+    def narrow_part(index):
+        at = 3 * half + index * wanted
+        return sums[0, at : at + inner_half]
 
     return (
         block_out,
         grad_tokens,
-        wide_part(0),
-        wide_part(2),
+        sums[0, :half],
+        sums[0, half : 2 * half],
         grads[:part_in],
-        narrow_part(6),
-        narrow_part(7),
-        narrow_part(8),
+        narrow_part(0),
+        narrow_part(1),
+        narrow_part(2),
         grads[2 * part_in : 2 * part_in + KERNEL_TAPS * part_conv].reshape(KERNEL_TAPS, part_conv, inner_half),
-        narrow_part(9),
-        narrow_part(10),
-        narrow_part(11),
+        narrow_part(3),
+        narrow_part(4),
+        narrow_part(5),
         grads[part_in : 2 * part_in].T,
-        wide_part(4),
+        sums[0, 2 * half : 3 * half],
     )
 
 

time: 308 us -> 281 us (0.912)
  Pallas kernels: 185 us -> 149 us
  waiting for transfers between devices: 65.3 us -> 74.9 us
  local copies, waits for them, and re-layouts: 19.4 us -> 15.2 us
  starting transfers between devices: 3.62 us -> 6.87 us
    ppermute x3 -> x6, waiting for transfers between devices: 3.23 us -> 74.9 us  [swap(): return lax.ppermute(value, 'ch', SWAP)]
    all_gather x1, waiting for transfers between devices: 62 us -> 0.01 us  [fast_body(): gathered = lax.all_gather(both, 'seq', axis=0)]
    pallas_call x1, Pallas kernels: 185 us -> 145 us  [fast_call(): pl.pallas_call(fast_kernel, out_shape=[jax.ShapeDtypeStruct(shape, dtype)...]
    pallas_call x0 -> x1, Pallas kernels: none -> 4 us  [finish_call(): pl.pallas_call(finish_kernel, grid_spec=pltpu.PrefetchScalarGridSpec(num_...]
    squeeze x1, local copies, waits for them, and re-layouts: 3.46 us -> 0.04 us  [other_of(): return lax.dynamic_index_in_dim(value, 1 - side, 0, keepdims=False)]
    ppermute x3 -> x6, starting transfers between devices: 3.58 us -> 6.83 us  [swap(): return lax.ppermute(value, 'ch', SWAP)]
    slice x4 -> x6, local copies, waits for them, and re-layouts: 4.73 us -> 7.75 us  [the longest x1 2.98 us: fast_body(): x_first, x_second = (swap(first_send), swap(x_send[FIRST:]))]
  transfers between devices with their start and end apart: 4 -> 7, of which waited for: 2 -> 5; matrix products, arithmetic and copies ran while one was open for 4% -> 9% of each run, Pallas kernels for 0% -> 0%
where the time goes in v3:
time: 281 us; the launch traced here: 278 us
  Pallas kernels  149 us (53%)
  waiting for transfers between devices  74.9 us (27%)
  other arithmetic  18 us (6%)
  local copies, waits for them, and re-layouts  15.2 us (5%)
  between operations  14.2 us (5%)
  starting transfers between devices  6.87 us (2%)
    pallas_call x1, Pallas kernels, fast_call(): pl.pallas_call(fast_kernel, out_shape=[jax.ShapeDtypeStruct(shape, dtype)...  145 us
    ppermute x6, waiting for transfers between devices, swap(): return lax.ppermute(value, 'ch', SWAP)  74.9 us
    select_n x2, other arithmetic, placed(): jnp.where(low_side, jnp.stack([own, back], 0), jnp.stack([back, own], 0))  8.23 us
    ppermute x6, starting transfers between devices, swap(): return lax.ppermute(value, 'ch', SWAP)  6.83 us
  transfers between devices with their start and end apart: 7, of which 5 were waited for; matrix products, arithmetic and copies ran while one was open for 9% of the time, Pallas kernels for 0%

profile of v3, /device:TPU:24, one launch (start us, length us, event | category | flops | bytes accessed | tf_op | source)
XLA Modules:
  0.0 278.0 jit_solution(15497023442440265671)
XLA Ops:
  7.2 0.0 copy-start
  7.2 0.0 copy-start.7
  7.2 0.0 all-gather.2.cloned.1.call-start
  7.3 0.1 pad.24.clone
  7.3 0.0 slice-start
  7.3 2.1 dynamic-slice_bitcast_fusion.1
  9.4 1.0 maximum_maximum_fusion
  10.5 0.9 concatenate.33
  11.4 1.5 collective-permute-start.3
  12.9 7.0 %collective-permute-done.3 = bf16[368,320]{1,0:T(8,128)(2,1)S(1)} collective-permute-done((bf16[368,320]{1,0:T(8,128)(2,1)S(1)}, bf16[368,320]{1,0:T(8,128)(2,1)S(1)}, u32[]{:S(2)}, u32[]{:S(2)}) %collective-permute-start.3) | collective-permute-done | bytes 235552 | tf_op jit(solution)/shard_map/ppermute | solution.py:1083
  19.8 1.1 maximum_select_fusion.2
  21.0 0.0 all-gather.2.cloned.1.call-update
  21.0 1.6 collective-permute-start.4
  22.6 0.5 collective-permute-start
  23.1 3.0 %dynamic-slice_bitcast_fusion = bf16[1536,640]{1,0:T(8,128)(2,1)} fusion(bf16[2,2048,640]{2,1,0:T(8,128)(2,1)} %tokens.1, s32[]{:T(128)S(6)} %select_n.55, s32[]{:T(128)S(6)} %add.47), kind=kLoop, calls=%fused_computation.5 | loop fusion | bytes 3932168 | tf_op jit(solution)/shard_map/slice | solution.py:1118
  26.1 1.5 collective-permute-start.1
  27.6 0.0 copy-done
  27.6 0.1 copy.40
  27.7 0.2 reduce-window.4
  27.9 0.1 slice_reduce_fusion
  28.0 0.7 convert_reduce_fusion
  28.7 0.1 fusion.4
  28.8 0.0 copy-done.7
  28.9 0.1 stack.89
  29.0 1.0 copy.41.masks
  30.0 0.0 collective-permute-done.4
  30.0 0.1 maximum_select_fusion.3
  30.1 0.1 fusion.6
  30.2 0.1 stack_reshape.35
  30.3 0.1 stack_reshape.34
  30.4 0.1 stack_reshape.33
  30.4 0.1 stack_reshape.32
  30.5 0.1 stack_reshape.31
  30.6 0.1 stack_reshape.30
  30.7 0.6 stack.95.narrow
  31.3 9.2 %collective-permute-done = bf16[512,640]{1,0:T(8,128)(2,1)} collective-permute-done((bf16[512,640]{1,0:T(8,128)(2,1)}, bf16[512,640]{1,0:T(8,128)(2,1)}, u32[]{:S(2)}, u32[]{:S(2)}) %collective-permute-start) | collective-permute-done | bytes 655392 | tf_op jit(solution)/shard_map/ppermute | solution.py:1083
  40.5 0.0 slice-done
  40.6 0.6 collective-permute-start.2
  41.2 0.6 pad_maximum_fusion.1.wide
  41.8 40.8 %collective-permute-done.1 = bf16[1536,640]{1,0:T(8,128)(2,1)S(1)} collective-permute-done((bf16[1536,640]{1,0:T(8,128)(2,1)}, bf16[1536,640]{1,0:T(8,128)(2,1)S(1)}, u32[]{:S(2)}, u32[]{:S(2)}) %collective-permute-start.1) | collective-permute-done | bytes 1966112 | tf_op jit(solution)/shard_map/ppermute | solution.py:1083
  82.6 2.8 %pad_maximum_fusion.x_other = bf16[2048,640]{1,0:T(8,128)(2,1)} fusion(bf16[1536,640]{1,0:T(8,128)(2,1)S(1)} %collective-permute-done.1, bf16[512,640]{1,0:T(8,128)(2,1)} %collective-permute-done), kind=kLoop, calls=%fused_computation.4 | loop fusion | flops 5242880 | bytes 5242880 | tf_op jit(solution)/shard_map/concatenate | solution.py:1121
  85.4 5.6 %collective-permute-done.2.gy_early = bf16[384,640]{1,0:T(8,128)(2,1)S(1)} collective-permute-done((bf16[384,640]{1,0:T(8,128)(2,1)S(1)}, bf16[384,640]{1,0:T(8,128)(2,1)S(1)}, u32[]{:S(2)}, u32[]{:S(2)}) %collective-permute-start.2) | collective-permute-done | bytes 491552 | tf_op jit(solution)/shard_map/ppermute | solution.py:1083
  90.9 0.0 all-gather.2.cloned.1.call-done.gathered
  90.9 0.8 copy-done.8
  91.7 144.7 %shard_map.263 = (bf16[2048,640]{1,0:T(8,128)(2,1)}, bf16[2048,640]{1,0:T(8,128)(2,1)}, f32[2048,640]{1,0:T(8,128)}, bf16[2048,640]{1,0:T(8,128)(2,1)}, bf16[102...) custom-call(bf16[2,2048,640]{2,1,0:T(8,128)(2,1)} %tokens.1, ...), custom_call_target="tpu_custom_call" | custom-call | flops 45298483200 | bytes 125829120 | tf_op jit(solution)/shard_map/pallas_call | solution.py:977
  236.4 1.3 slice_reduce_fusion.4
  237.8 1.2 collective-permute-start.5
  238.9 0.0 copy-start.6
  238.9 0.0 copy-start.2
  238.9 3.2 %fusion = f32[1,2048,640]{2,1,0:T(8,128)S(1)} fusion(bf16[2048,640]{1,0:T(8,128)(2,1)} %get-tuple-element.35, bf16[2,2048,640]{2,1,0:T(8,128)(2,1)} %cot_ref.1, s32[]{:T(128)S(6)} %select_n.55), kind=kLoop, calls=%fused_computation.3 | loop fusion | flops 3932160 | bytes 10485764 | tf_op jit(solution)/shard_map/stack | solution.py:1158
  242.1 1.4 slice_reduce_fusion.1
  243.5 0.0 copy-done.6
  243.5 0.7 slice.124
  244.2 0.7 slice_bitcast_fusion
  244.9 0.0 copy-done.2
  244.9 0.0 copy-start.3
  244.9 5.2 %maximum_select_fusion.whole_ref = f32[2,2048,640]{2,1,0:T(8,128)} fusion(f32[1,2048,640]{2,1,0:T(8,128)S(1)} %fusion, f32[1,2048,640]{2,1,0:T(8,128)S(1)} %bitcast.38, pred[]{:T(512)S(6)} %eq.18), kind=kLoop, calls=%fused_computation | loop fusion | flops 7864320 | bytes 20971520 | tf_op jit(solution)/shard_map/jit(_where)/select_n | solution.py:1158
  250.1 0.0 copy-done.3
  250.1 0.5 copy-done.4
  250.6 3.0 %maximum_select_fusion.1 = bf16[2,2048,640]{2,1,0:T(8,128)(2,1)} fusion(bf16[1,2048,640]{2,1,0:T(8,128)(2,1)S(1)} %bitcast.40, bf16[1,2048,640]{2,1,0:T(8,128)(2,1)S(1)} %bitcast.39, pred[]{:T(512)S(6)} %eq.18), kind=kLoop, calls=%fused_computation.1 | loop fusion | flops 7864320 | bytes 10485761 | tf_op jit(solution)/shard_map/jit(_where)/select_n | solution.py:1158
  253.7 12.4 %collective-permute-done.5.tail_ref = bf16[1024,640]{1,0:T(8,128)(2,1)S(1)} collective-permute-done((bf16[1024,640]{1,0:T(8,128)(2,1)}, bf16[1024,640]{1,0:T(8,128)(2,1)S(1)}, u32[]{:S(2)}, u32[]{:S(2)}) %collective-permute-start.5) | collective-permute-done | bytes 1310752 | tf_op jit(solution)/shard_map/ppermute | solution.py:1083
  266.1 1.1 copy-done.5
  267.2 4.0 %shard_map.264 = f32[2,2048,640]{2,1,0:T(8,128)} custom-call(s32[1]{0:T(128)} %bitcast.11.side_ref, bf16[1024,640]{1,0:T(8,128)(2,1)} %copy-done.5, bf16[2,2048,640]{2,1,0:T(8,128)(2,1)} %cot_ref.1, f32[2,2048,640]{2,1,0:T(8,128)} %maximum_select_fusion.whole_ref), custom_call_target="tpu_custom_call", output_to_operand_aliasing={{}: (3, {})} | custom-call | flops 655360 | bytes 5242880 | tf_op jit(solution)/shard_map/pallas_call | solution.py:1034
  271.2 0.0 copy-done.1
  (22 shorter events, 0.2 us)
Async XLA Ops:
  7.2 20.4 %copy-start = (s32[2,128]{1,0:T(2,128)S(1)}, s32[2,128]{1,0:T(2,128)}, u32[]{:S(2)}) copy-start(s32[2,128]{1,0:T(2,128)} %param.18) | copy-start | bytes 3076
  7.2 21.6 %copy-start.7 = (s32[2,2048]{1,0:T(2,128)S(1)}, s32[2,2048]{1,0:T(2,128)}, u32[]{:S(2)}) copy-start(s32[2,2048]{1,0:T(2,128)} %param.19) | copy-start | bytes 49156
  7.2 83.7 %all-gather.2.cloned.1.call-start = ((), (), s32[]{:S(2)}) async-start(), calls=%async_computation | async-start | bytes 8007680 | tf_op jit(solution)/shard_map/all_gather | solution.py:1122
  7.3 33.2 %slice-start = ((bf16[2,2048,640]{2,1,0:T(8,128)(2,1)}), bf16[2,384,640]{2,1,0:T(8,128)(2,1)S(1)}, s32[]{:S(2)}) async-start(bf16[2,2048,640]{2,1,0:T(8,128)(2,1)} %cot_ref.1), calls=%async_computation.1 | async-start | bytes 1966080 | tf_op jit(solution)/shard_map/slice | solution.py:1119
  11.4 8.5 %collective-permute-start.3 = (bf16[368,320]{1,0:T(8,128)(2,1)S(1)}, bf16[368,320]{1,0:T(8,128)(2,1)S(1)}, u32[]{:S(2)}, u32[]{:S(2)}) collective-permute-start(bf16[368,320]{1,0:T(8,128)(2,1)S(1)} %maximum_maximum_fusion), channel_id=1, source_target_pairs={{0,1},{1,0},{2,3},{3,2},{4,5},{5,4},{6,7},{7,6},{8,9},{9,8},{10,11... | collective-permute-start | bytes 706568 | tf_op jit(solution)/shard_map/ppermute | solution.py:1083
  21.0 9.0 %collective-permute-start.4 = (f32[3840]{0:T(1024)S(1)}, f32[3840]{0:T(1024)S(1)}, u32[]{:S(2)}, u32[]{:S(2)}) collective-permute-start(f32[3840]{0:T(1024)S(1)} %concatenate.33), channel_id=1, source_target_pairs={{0,1},{1,0},{2,3},{3,2},{4,5},{5,4},{6,7},{7,6},{8,9},{9,8},{10,11... | collective-permute-start | bytes 46088 | tf_op jit(solution)/shard_map/ppermute | solution.py:1083
  22.6 18.0 %collective-permute-start = (bf16[512,640]{1,0:T(8,128)(2,1)}, bf16[512,640]{1,0:T(8,128)(2,1)}, u32[]{:S(2)}, u32[]{:S(2)}) collective-permute-start(bf16[512,640]{1,0:T(8,128)(2,1)} %dynamic-slice_bitcast_fusion.1), channel_id=1, source_target_pairs={{0,1},{1,0},{2,3},{3,2},{4,5},{5,4},{6,7},{7,6},{8,9},{9,8},{10,11... | collective-permute-start | bytes 1966088 | tf_op jit(solution)/shard_map/ppermute | solution.py:1083
  26.1 56.5 %collective-permute-start.1 = (bf16[1536,640]{1,0:T(8,128)(2,1)}, bf16[1536,640]{1,0:T(8,128)(2,1)S(1)}, u32[]{:S(2)}, u32[]{:S(2)}) collective-permute-start(bf16[1536,640]{1,0:T(8,128)(2,1)} %dynamic-slice_bitcast_fusion), channel_id=1, source_target_pairs={{0,1},{1,0},{2,3},{3,2},{4,5},{5,4},{6,7},{7,6},{8,9},{9,8},{10,11... | collective-permute-start | bytes 5898248 | tf_op jit(solution)/shard_map/ppermute | solution.py:1083
  40.6 50.3 %collective-permute-start.2 = (bf16[384,640]{1,0:T(8,128)(2,1)S(1)}, bf16[384,640]{1,0:T(8,128)(2,1)S(1)}, u32[]{:S(2)}, u32[]{:S(2)}) collective-permute-start(bf16[384,640]{1,0:T(8,128)(2,1)S(1)} %dynamic-slice_bitcast_fusion.2), channel_id=1, source_target_pairs={{0,1},{1,0},{2,3},{3,2},{4,5},{5,4},{6,7},{7,6},{8,9},{9,8},{10,11... | collective-permute-start | bytes 1474568 | tf_op jit(solution)/shard_map/ppermute | solution.py:1083
  90.9 0.8 copy-start.8
  237.8 28.3 %collective-permute-start.5 = (bf16[1024,640]{1,0:T(8,128)(2,1)}, bf16[1024,640]{1,0:T(8,128)(2,1)S(1)}, u32[]{:S(2)}, u32[]{:S(2)}) collective-permute-start(bf16[1024,640]{1,0:T(8,128)(2,1)} %get-tuple-element.33), channel_id=1, source_target_pairs={{0,1},{1,0},{2,3},{3,2},{4,5},{5,4},{6,7},{7,6},{8,9},{9,8},{10,11... | collective-permute-start | bytes 3932168 | tf_op jit(solution)/shard_map/ppermute | solution.py:1083
  238.9 4.6 %copy-start.6 = (f32[368,320]{1,0:T(8,128)S(1)}, f32[368,320]{1,0:T(8,128)}, u32[]{:S(2)}) copy-start(f32[368,320]{1,0:T(8,128)} %get-tuple-element.37) | copy-start | bytes 1413124
  238.9 6.0 %copy-start.2 = (f32[2048,640]{1,0:T(8,128)S(1)}, f32[2048,640]{1,0:T(8,128)}, u32[]{:S(2)}) copy-start(f32[2048,640]{1,0:T(8,128)} %get-tuple-element.34) | copy-start | bytes 15728644
  244.9 5.2 %copy-start.3 = (bf16[2048,640]{1,0:T(8,128)(2,1)S(1)}, bf16[2048,640]{1,0:T(8,128)(2,1)}, u32[]{:S(2)}) copy-start(bf16[2048,640]{1,0:T(8,128)(2,1)} %get-tuple-element.31) | copy-start | bytes 7864324
  244.9 5.7 %copy-start.4 = (bf16[2048,640]{1,0:T(8,128)(2,1)S(1)}, bf16[2048,640]{1,0:T(8,128)(2,1)}, u32[]{:S(2)}) copy-start(bf16[2048,640]{1,0:T(8,128)(2,1)} %get-tuple-element.32) | copy-start | bytes 7864324
  266.1 1.1 copy-start.5
  267.1 4.0 %copy-start.1 = (s32[2,128]{1,0:T(2,128)S(1)}, s32[2,128]{1,0:T(2,128)}, u32[]{:S(2)}) copy-start(s32[2,128]{1,0:T(2,128)} %param.18) | copy-start | bytes 3076
Sparse Core Ops, SparseCore 0:
  21.1 68.8 all-gather.1

commit v4 on v3

--- a/solution.py
+++ b/solution.py
@@ -481,15 +481,14 @@
 BLOCK = 256
 CHUNKS = 4
 CONV_PAD = 8
-EARLY = 384
-FIRST = 512
-HEAD = 4
+HEAD = 5
 
 
 def fast_kernel(
-    tokens, x_other, cot, gy_early, gathered, masks, wide, narrow,
-    out_own, out_back, dx_own, dx_back, dx_tail, grads_out, sums_out,
-    s1, h1, s2, h3, s3,
+    tokens, cot, own_weights, own_vectors, masks,
+    out_own, out_back, dx_own, dx_back, dx_tail, dx_end, grads_out, sums_out,
+    x_other, g_conv, s1, h1, s2, h3, s3,
+    other_vectors, other_weights, wide, narrow, stage,
     a1v, a2f, a3v, gyv, dh3f, out_send, w_in, w_out, w_conv,
     k_in, s_in, r0_in, r1_in, r2_in, r3_in,
     k_out, s_out, r0_out, r1_out, r2_out, r3_out,
@@ -497,7 +496,7 @@
     k_mid, s_mid, r0_mid, r1_mid, r2_mid, r3_mid,
     k_top, s_top, r0_top, r1_top, r2_top, r3_top,
     smalls, grads, cross_send, cross_recv, small_send, small_recv, load_sems,
-    gy_sems, out_sems, dx_sems, a2_sems, dh3_sems, in_sems, out_rs_sems, low_sems, mid_sems, top_sems, cross_sems, small_sems,
+    swap_sems, token_sems, in_gather, out_gather, conv_gather, gy_sems, out_sems, dx_sems, a2_sems, dh3_sems, in_sems, out_rs_sems, low_sems, mid_sems, top_sems, cross_sems, small_sems,
 ):
     rows = a1v.shape[0]
     half = tokens.shape[2]
@@ -525,34 +524,18 @@
     def block(ref, at):
         return ref.at[pl.ds(pl.multiple_of(at * BLOCK, BLOCK), BLOCK)]
 
-    early = gy_early.shape[0]
 
     def gy_copy(at):
-        begin = max(at * part, early)
-        piece = pl.ds(begin, (at + 1) * part - begin)
+        piece = pl.ds(at * part, part)
         return remote(cot.at[1 - side, piece], gyv.at[side, piece], gy_sems, at, across)
 
-    gy_chunks = [at for at in range(CHUNKS) if (at + 1) * part > early]
-    part_in = w_in.shape[1]
+    def token_copy(at):
+        piece = pl.ds(pl.multiple_of(at * part, part), part)
+        return remote(tokens.at[1 - side, piece], x_other.at[piece], token_sems, at, across)
+
+    part_in = w_in.shape[4]
     tail_rows = k_top.shape[1]
-    loads = [
-        pltpu.make_async_copy(src, dst, load_sems.at[at])
-        for at, (src, dst) in enumerate(
-            (
-                (gathered.at[:, pl.ds(0, part_in)], w_in),
-                (gathered.at[:, pl.ds(part_in, part_in)], w_out),
-                (gathered.at[pl.ds(0, 8), pl.ds(2 * part_in, part_in)], s_low),
-                (gathered.at[pl.ds(8, 8), pl.ds(2 * part_in, part_in)], r0_low),
-                (gathered.at[pl.ds(0, 8), pl.ds(3 * part_in, part_in)], s_mid),
-                (gathered.at[pl.ds(8, 8), pl.ds(3 * part_in, part_in)], r0_mid),
-                (gathered.at[pl.ds(0, 8), pl.ds(4 * part_in, tail_rows)], s_top),
-                (gathered.at[pl.ds(8, 8), pl.ds(4 * part_in, tail_rows)], r0_top),
-                (gy_early, gyv.at[1 - side, pl.ds(0, early)]),
-                (cot.at[side], gyv.at[side]),
-            )
-        )
-    ]
-
+    own_gy = pltpu.make_async_copy(cot.at[side], gyv.at[side], load_sems.at[0])
     def out_copy(at):
         return remote(block(out_send, at), block(out_back, at), out_sems, at, across)
 
@@ -586,6 +569,7 @@
             halo_low(framed_rows, sems).wait_recv()
 
     blocks = rows // BLOCK
+    per = part // BLOCK
 
     def middle_first(step):
         late = step // (blocks - 2)
@@ -594,15 +578,20 @@
     def in_order(step):
         return step
 
-    def pipeline(step, order, ins, outs, tail=None):
+    def pipeline(step, order, ins, outs, tail=None, count=None):
         def spec(ref):
             return pl.BlockSpec((BLOCK, ref.shape[-1]), lambda i: (order(i), 0))
 
         out_specs = [spec(r) for r in outs]
         if tail is not None:
-            outs = outs + [tail]
-            out_specs.append(pl.BlockSpec((BLOCK, half), lambda i: (jnp.maximum(i - HEAD, 0), 0)))
-        pltpu.emit_pipeline(step, grid=(blocks,), in_specs=[spec(r) for r in ins], out_specs=out_specs)(*ins, *outs)
+            ahead, end = tail
+            most = blocks - 2 - HEAD
+            outs = outs + [ahead, end]
+            out_specs.append(
+                pl.BlockSpec((BLOCK, half), lambda i: (jnp.minimum(jnp.maximum(i - HEAD, 0), most), 0))
+            )
+            out_specs.append(pl.BlockSpec((BLOCK, half), lambda i: (0, 0)))
+        pltpu.emit_pipeline(step, grid=(count or blocks,), in_specs=[spec(r) for r in ins], out_specs=out_specs)(*ins, *outs)
 
     barrier = pltpu.get_barrier_semaphore()
     ring = [{"seq": lax.rem(place + last, last + 1)}, {"seq": lax.rem(place + 1, last + 1)}]
@@ -610,10 +599,17 @@
         pl.semaphore_signal(barrier, inc=1, device_id=device, device_id_type=pl.DeviceIdType.MESH)
     pl.semaphore_wait(barrier, 7)
 
-    for at in gy_chunks:
+    swaps = [
+        remote(own_weights, other_weights, swap_sems, 0, across),
+        remote(own_vectors, other_vectors, swap_sems, 1, across),
+    ]
+    for swap in swaps:
+        swap.start()
+    for at in range(CHUNKS):
+        token_copy(at).start()
+    for at in range(CHUNKS):
         gy_copy(at).start()
-    for load in loads:
-        load.start()
+    own_gy.start()
     smalls[...] = jnp.zeros_like(smalls)
 
     @pl.when(place == 0)
@@ -626,45 +622,115 @@
         a2f[HALO + rows :, :] = jnp.zeros((HALO, inner), jnp.bfloat16)
         dh3f[HALO + rows :, :] = jnp.zeros((HALO, inner), jnp.bfloat16)
 
-    def first(own, other, s1_block, h1_block, s2_block):
-        base = pl.multiple_of(pl.program_id(0) * BLOCK, BLOCK)
-        x = jnp.concatenate(ordered(side, own[...], other[...]), axis=1)
-        normed, _ = norm(x)
-        act, slope = gelu_both(normed * wide[0:1, :] + wide[1:2, :])
-        act = act.astype(jnp.bfloat16)
-        a1v[pl.ds(base, BLOCK), :] = act
-        s1_block[...] = slope
-        value = dot(act, w_in[...].reshape(2 * half, inner)) + narrow[0:1, :]
-        h1_block[...] = value
-        normed, _ = norm(value)
-        act, slope = gelu_both(normed * narrow[1:2, :] + narrow[2:3, :])
-        keep = masks[pl.ds(base, BLOCK), KERNEL_TAPS : KERNEL_TAPS + 1].astype(jnp.float32)
-        a2f[pl.ds(HALO + base, BLOCK), :] = (act * keep).astype(jnp.bfloat16)
-        s2_block[...] = slope * keep
-
-    loads[0].wait()
-    pipeline(first, in_order, [tokens.at[side], x_other], [s1, h1, s2])
-    for at in range(2, 8):
-        loads[at].wait()
+    def both(own, other):
+        left, right = ordered(side, own, other)
+        return jnp.concatenate([left, right], axis=1)
+
+    for swap in swaps:
+        swap.wait()
+    rows_here = both(own_weights[...], other_weights[...]).astype(jnp.bfloat16)
+    here = (bits[3], bits[2], bits[1], bits[0])
+    w_in[here] = rows_here[:part_in]
+    w_out[here] = rows_here[part_in : 2 * part_in]
+    stage[0, 0, 0] = rows_here[2 * part_in :]
+    own_conv = pltpu.make_async_copy(stage.at[0, 0, 0], g_conv.at[here], load_sems.at[1])
+    own_conv.start()
+    quarter = half // 2
+    wanted = quarter + 64
+    for index in range(3):
+        lanes = slice(index * half, (index + 1) * half)
+        wide[index : index + 1, :] = both(own_vectors[:, lanes], other_vectors[:, lanes])
+    for index in range(6):
+        lanes = slice(3 * half + index * wanted, 3 * half + index * wanted + quarter)
+        narrow[index : index + 1, :] = both(own_vectors[:, lanes], other_vectors[:, lanes])
+
+    def gather_copy(group, level):
+        ref, sems, order = group
+        every = slice(None)
+        at = tuple(every if bit in order[:level] else bits[bit] for bit in (3, 2, 1, 0))
+        return remote(ref.at[at], ref.at[at], sems, level, pairs[order[level]])
+
+    in_rows = (w_in, in_gather, (3, 2, 1, 0))
+    out_rows = (w_out, out_gather, (1, 3, 2, 0))
+    conv_rows = (g_conv, conv_gather, (3, 2, 1, 0))
+
+    def gather_next(group, level):
+        gather_copy(group, level).wait()
+        if level < 3:
+            gather_copy(group, level + 1).start()
+
+    gather_copy(in_rows, 0).start()
+    gather_copy(out_rows, 0).start()
+    own_conv.wait()
+    gather_next(in_rows, 0)
+    gather_copy(conv_rows, 0).start()
+    gather_next(in_rows, 1)
+    gather_next(in_rows, 2)
+    gather_next(conv_rows, 0)
+    gather_next(out_rows, 0)
+    gather_next(in_rows, 3)
+
+    def first_chunk(at, _):
+        token_copy(at).wait_recv()
+
+        def first(own, other, s1_block, h1_block, s2_block):
+            base = pl.multiple_of((at * per + pl.program_id(0)) * BLOCK, BLOCK)
+            x = jnp.concatenate(ordered(side, own[...], other[...]), axis=1)
+            normed, _ = norm(x)
+            act, slope = gelu_both(normed * wide[0:1, :] + wide[1:2, :])
+            act = act.astype(jnp.bfloat16)
+            a1v[pl.ds(base, BLOCK), :] = act
+            s1_block[...] = slope
+            value = dot(act, w_in[...].reshape(2 * half, inner)) + narrow[0:1, :]
+            h1_block[...] = value
+            normed, _ = norm(value)
+            act, slope = gelu_both(normed * narrow[1:2, :] + narrow[2:3, :])
+            keep = masks[pl.ds(base, BLOCK), KERNEL_TAPS : KERNEL_TAPS + 1].astype(jnp.float32)
+            a2f[pl.ds(HALO + base, BLOCK), :] = (act * keep).astype(jnp.bfloat16)
+            s2_block[...] = slope * keep
+
+        pipeline(first, lambda i: at * per + i, [tokens.at[side], x_other], [s1, h1, s2], count=per)
+        for level, (group, ready) in enumerate(((conv_rows, 1), (out_rows, 1), (out_rows, 2))):
+
+            @pl.when(at == level)
+            def _():
+                gather_next(group, ready)
+
+        return 0
+
+    lax.fori_loop(0, CHUNKS, first_chunk, 0)
+    halo_start(a2f, a2_sems)
+    gather_next(conv_rows, 2)
+    gather_next(out_rows, 3)
+    gather_next(conv_rows, 3)
+
     height = inner // 16
 
+    def conv_load(pair):
+        return pltpu.make_async_copy(g_conv.at[pair // 2, pair % 2], stage.at[pair % 2], load_sems.at[2 + pair % 2])
+
+    conv_load(0).start()
+    conv_load(1).start()
+
     def relay(pair, _):
-        for group, sources in enumerate(((s_low, s_mid, s_top), (r0_low, r0_mid, r0_top))):
-            at = pl.multiple_of((4 * group + pair) * 2 * height, 2 * height)
-            tap = 0
-            for source in sources:
-                even = source[2 * pair].astype(jnp.float32)
-                odd = source[2 * pair + 1].astype(jnp.float32)
-                for top in range(0, source.shape[1] - CONV_PAD, height):
-                    w_conv[tap, pl.ds(at, 2 * height), :] = jnp.concatenate(
-                        [even[top : top + height], odd[top : top + height]], axis=0
-                    ).astype(jnp.bfloat16)
-                    tap += 1
+        conv_load(pair).wait()
+        for low_bit in range(2):
+            even = stage[pair % 2, low_bit, 0].astype(jnp.float32)
+            odd = stage[pair % 2, low_bit, 1].astype(jnp.float32)
+            at = pl.multiple_of((2 * pair + low_bit) * 2 * height, 2 * height)
+            for tap in range(KERNEL_TAPS):
+                top = tap * height
+                w_conv[tap, pl.ds(at, 2 * height), :] = jnp.concatenate(
+                    [even[top : top + height], odd[top : top + height]], axis=0
+                ).astype(jnp.bfloat16)
+
+        @pl.when(pair < 2)
+        def _():
+            conv_load(pair + 2).start()
+
         return 0
 
     lax.fori_loop(0, 4, relay, 0)
-    loads[1].wait()
-    halo_start(a2f, a2_sems)
 
     def second(own, other, h3_block, s3_block, own_block):
         step = pl.program_id(0)
@@ -701,12 +767,10 @@
         smalls[row : row + 1, :] += value[:, :half]
         smalls[row + 1 : row + 2, :] += value[:, half:]
 
-    per = part // BLOCK
-
     def third(h3_block, s3_block):
         at = pl.program_id(0)
         base = pl.multiple_of(at * BLOCK, BLOCK)
-        for later in gy_chunks:
+        for later in range(CHUNKS):
 
             @pl.when(at == later * per)
             def _():
@@ -722,8 +786,7 @@
         add_small(10, column_sums(dz3 * normed))
         add_small(11, column_sums(dz3))
 
-    loads[8].wait()
-    loads[9].wait()
+    own_gy.wait()
     pipeline(third, in_order, [h3, s3], [])
     halo_start(dh3f, dh3_sems)
 
@@ -854,7 +917,7 @@
     sum_step(out_set, 1)
     sum_step(low_set, 2)
 
-    def fifth(own, other, s1_block, own_block, tail_block):
+    def fifth(own, other, s1_block, own_block, tail_block, end_block):
         step = pl.program_id(0)
         base = pl.multiple_of(step * BLOCK, BLOCK)
         dh1 = a3v[pl.ds(base, BLOCK), :]
@@ -868,9 +931,13 @@
         own_block[...] = jnp.where(low, left, right) + gyv[side, pl.ds(base, BLOCK), :].astype(jnp.float32)
         sent = jnp.where(low, right, left).astype(jnp.bfloat16)
         gyv[1 - side, pl.ds(base, BLOCK), :] = sent
-        tail_block[...] = sent
-
-        @pl.when(step < HEAD)
+        end_block[...] = sent
+
+        @pl.when(step < blocks - 1)
+        def _():
+            tail_block[...] = sent
+
+        @pl.when(step < HEAD - 1)
         def _():
             dx_copy(step).start()
 
@@ -881,7 +948,7 @@
         at_step(step, 6, (in_set, 1))
         at_step(step, 7, (top_set, 3), (out_set, 3))
 
-    pipeline(fifth, in_order, [tokens.at[side], x_other, s1], [dx_own], dx_tail)
+    pipeline(fifth, in_order, [tokens.at[side], x_other, s1], [dx_own], (dx_tail, dx_end))
 
 
     def small_copy(level):
@@ -908,7 +975,6 @@
     small_step(3)
     small_start(4)
 
-    wanted = half // 2 + 64
     row = 0
     for keep, _, _, _, order in (in_set, out_set, low_set, mid_set, top_set):
         mine = bits[order[0]] + 2 * bits[order[1]] + 4 * bits[order[2]]
@@ -920,12 +986,13 @@
         row += height
     cross = remote(cross_send, cross_recv, cross_sems, 0, across)
     cross.start()
-    for at in gy_chunks:
+    dx_copy(HEAD - 1).start()
+    for at in range(CHUNKS):
+        token_copy(at).wait_send()
         gy_copy(at).wait_send()
     for at in range(blocks):
         out_copy(at).wait()
     small_step(4)
-    quarter = half // 2
     for index in range(3):
         both = smalls[2 * index : 2 * index + 2, :]
         sums_out[:, index * half : (index + 1) * half] = jnp.where(low, both[0:1], both[1:2])
@@ -940,10 +1007,10 @@
         dx_copy(at).wait()
 
 
-def fast_call(tokens, x_other, cot, gy_early, gathered, masks, wide, narrow, part_in, part_conv):
+def fast_call(tokens, cot, own_weights, own_vectors, masks, part_in, part_conv):
     _, rows, half = tokens.shape
     model = 2 * half
-    inner = narrow.shape[1]
+    inner = 2 * own_weights.shape[1]
     f32, bf16 = jnp.float32, jnp.bfloat16
     tall = KERNEL_TAPS * part_conv + CONV_PAD
     any_spec = pl.BlockSpec(memory_space=pl.ANY)
@@ -964,9 +1031,12 @@
         ((rows, half), bf16),
         ((rows, half), f32),
         ((rows, half), bf16),
-        ((rows - HEAD * BLOCK, half), bf16),
+        ((rows - (HEAD + 1) * BLOCK, half), bf16),
+        ((BLOCK, half), bf16),
         ((total, half // 2), f32),
         ((1, 3 * half + 6 * wanted), f32),
+        ((rows, half), bf16),
+        ((2, 2, 2, 2, tall, inner), bf16),
         ((rows, model), f32),
         ((rows, inner), f32),
         ((rows, inner), f32),
@@ -977,17 +1047,22 @@
     results = pl.pallas_call(
         fast_kernel,
         out_shape=[jax.ShapeDtypeStruct(shape, dtype) for shape, dtype in shapes],
-        in_specs=[any_spec] * 5 + [vmem_spec] * 3,
-        out_specs=[any_spec] * 5 + [vmem_spec] * 2 + [any_spec] * 5,
+        in_specs=[any_spec] * 2 + [vmem_spec] * 3,
+        out_specs=[any_spec] * 6 + [vmem_spec] * 2 + [any_spec] * 7,
         scratch_shapes=[
+            pltpu.VMEM(own_vectors.shape, f32),
+            pltpu.VMEM(own_weights.shape, bf16),
+            pltpu.VMEM((8, model), f32),
+            pltpu.VMEM((8, inner), f32),
+            pltpu.VMEM((2, 2, 2, tall, inner), bf16),
             pltpu.VMEM((rows, model), bf16),
             pltpu.VMEM((rows + 2 * HALO, inner), bf16),
             pltpu.VMEM((rows, inner), bf16),
             pltpu.VMEM((2, rows, half), bf16),
             pltpu.VMEM((rows + 2 * HALO, inner), bf16),
             pltpu.VMEM((rows, half), bf16),
-            pltpu.VMEM((16, part_in, inner), bf16),
-            pltpu.VMEM((16, part_in, inner), bf16),
+            pltpu.VMEM((2, 2, 2, 2, part_in, inner), bf16),
+            pltpu.VMEM((2, 2, 2, 2, part_in, inner), bf16),
             pltpu.VMEM((KERNEL_TAPS, inner, inner), bf16),
         ]
         + sums(part_in) * 4
@@ -999,7 +1074,12 @@
             pltpu.VMEM((total, wanted), bf16),
             pltpu.VMEM((5, 16, inner), f32),
             pltpu.VMEM((5, 16, inner), f32),
-            pltpu.SemaphoreType.DMA((10,)),
+            pltpu.SemaphoreType.DMA((4,)),
+            sems(2),
+            sems(CHUNKS),
+            sems(4),
+            sems(4),
+            sems(4),
             sems(CHUNKS),
             sems(rows // BLOCK),
             sems(HEAD),
@@ -1014,15 +1094,48 @@
             sems(5),
         ],
         compiler_params=pltpu.CompilerParams(
-            collective_id=0, has_side_effects=True, vmem_limit_bytes=63 * 2**20
+            collective_id=0, has_side_effects=True, vmem_limit_bytes=65280 * 2**10
         ),
         cost_estimate=pl.CostEstimate(flops=flops, bytes_accessed=120 * 2**20, transcendentals=0),
-    )(tokens, x_other, cot, gy_early, gathered, masks, wide, narrow)
-    return results[:7]
+    )(tokens, cot, own_weights, own_vectors, masks)
+    return results[:8]
 
 
 def finish_kernel(side_ref, tail_ref, cot_ref, whole_ref, out_ref):
     out_ref[0] = tail_ref[...].astype(jnp.float32) + cot_ref[0].astype(jnp.float32)
+
+
+def assemble_kernel(side_ref, out_own, out_back, dx_own, dx_back, cot, block_out, grad_tokens):
+    side = side_ref[0]
+    block_out[side] = out_own[...]
+    block_out[1 - side] = out_back[...]
+    grad_tokens[side] = dx_own[...]
+    grad_tokens[1 - side] = dx_back[...].astype(jnp.float32) + cot[0].astype(jnp.float32)
+
+
+def assemble_call(side, out_own, out_back, dx_own, dx_back, cot):
+    rows, half = out_own.shape
+    tile = 2 * BLOCK
+    by_tile = pl.BlockSpec((tile, half), lambda i, side_ref: (i, 0))
+    pair = pl.BlockSpec((2, tile, half), lambda i, side_ref: (0, i, 0))
+    return pl.pallas_call(
+        assemble_kernel,
+        grid_spec=pltpu.PrefetchScalarGridSpec(
+            num_scalar_prefetch=1,
+            grid=(rows // tile,),
+            in_specs=[by_tile] * 4
+            + [pl.BlockSpec((1, tile, half), lambda i, side_ref: (1 - side_ref[0], i, 0))],
+            out_specs=[pair, pair],
+        ),
+        out_shape=[
+            jax.ShapeDtypeStruct((2, rows, half), jnp.bfloat16),
+            jax.ShapeDtypeStruct((2, rows, half), jnp.float32),
+        ],
+        compiler_params=pltpu.CompilerParams(
+            dimension_semantics=("arbitrary",), vmem_limit_bytes=56 * 2**20
+        ),
+        cost_estimate=pl.CostEstimate(flops=rows * half, bytes_accessed=24 * rows * half, transcendentals=0),
+    )(side, out_own, out_back, dx_own, dx_back, cot)
 
 
 def finish_call(side, tail, cot, grad_tokens, first):
@@ -1046,7 +1159,7 @@
         out_shape=jax.ShapeDtypeStruct(grad_tokens.shape, grad_tokens.dtype),
         input_output_aliases={3: 0},
         compiler_params=pltpu.CompilerParams(
-            dimension_semantics=("arbitrary",), vmem_limit_bytes=56 * 2**20
+            dimension_semantics=("arbitrary",), vmem_limit_bytes=63 * 2**20
         ),
         cost_estimate=pl.CostEstimate(flops=tail.size, bytes_accessed=8 * tail.size, transcendentals=0),
     )(side, tail, cot, grad_tokens)
@@ -1088,9 +1201,11 @@
     def other_of(value):
         return lax.dynamic_index_in_dim(value, 1 - side, 0, keepdims=False)
 
-    own_vectors = jnp.concatenate(
-        [first_gain, first_shift, out_bias, in_bias, mid_gain, mid_shift, conv_bias, last_gain, last_shift]
-    )
+    gap = jnp.zeros((64,), f32)
+    pieces = [first_gain, first_shift, out_bias]
+    for piece in (in_bias, mid_gain, mid_shift, conv_bias, last_gain, last_shift):
+        pieces += [piece, gap]
+    own_vectors = lax.optimization_barrier(jnp.concatenate(pieces))[None]
     part_in = proj_in.shape[0]
     part_conv = conv_weight.shape[1]
     own_weights = jnp.concatenate(
@@ -1101,31 +1216,6 @@
             jnp.zeros((CONV_PAD, inner_half), bf16),
         ],
         axis=0,
-    )
-    x_send = other_of(tokens)
-    own_vectors, own_weights, first_send = lax.optimization_barrier(
-        (own_vectors, own_weights, x_send[:FIRST])
-    )
-    other_vectors, other_weights = swap(own_vectors), swap(own_weights)
-    both = jnp.where(
-        low_side,
-        jnp.concatenate([own_weights, other_weights], axis=1),
-        jnp.concatenate([other_weights, own_weights], axis=1),
-    )
-    vectors = jnp.where(
-        low_side, jnp.stack([own_vectors, other_vectors]), jnp.stack([other_vectors, own_vectors])
-    )
-    x_first, x_second = swap(first_send), swap(x_send[FIRST:])
-    gy_tied, x_first = lax.optimization_barrier((cotangent[:, :EARLY], x_first))
-    gy_early = swap(other_of(gy_tied))
-    x_other = jnp.concatenate([x_first, x_second], axis=0)
-    gathered = lax.all_gather(both, "seq", axis=0)
-    wide = jnp.stack([vectors[:, i * half : (i + 1) * half].reshape(-1) for i in range(3)])
-    narrow = jnp.stack(
-        [
-            vectors[:, 3 * half + i * inner_half : 3 * half + (i + 1) * inner_half].reshape(-1)
-            for i in range(6)
-        ]
     )
 
     places = lax.axis_index("seq") * rows + jnp.arange(rows + 2 * HALO, dtype=jnp.int32) - HALO
@@ -1141,26 +1231,15 @@
     zero = jnp.zeros((rows,), bf16)
     masks = jnp.stack(columns + [own_of(residue_mask).astype(bf16), zero, zero], axis=1)
 
-    out_own, out_back, dx_own, dx_back, dx_tail, grads, sums = fast_call(
-        tokens,
-        x_other,
-        cotangent,
-        gy_early,
-        gathered,
-        masks,
-        wide,
-        narrow,
-        part_in,
-        part_conv,
-    )
-
-    def placed(own, back):
-        return jnp.where(low_side, jnp.stack([own, back], 0), jnp.stack([back, own], 0))
-
-    block_out = placed(out_own, out_back)
-    grad_tokens = placed(dx_own, dx_back.astype(f32) + other_of(cotangent).astype(f32))
+    out_own, out_back, dx_own, dx_back, dx_tail, dx_end, grads, sums = fast_call(
+        tokens, cotangent, own_weights, own_vectors, masks, part_in, part_conv
+    )
+
     side_array = side.astype(jnp.int32).reshape(1)
-    grad_tokens = finish_call(side_array, swap(dx_tail), cotangent, grad_tokens, HEAD)
+    tail_back, end_back = swap(dx_tail), swap(dx_end)
+    block_out, grad_tokens = assemble_call(side_array, out_own, out_back, dx_own, dx_back, cotangent)
+    grad_tokens = finish_call(side_array, tail_back, cotangent, grad_tokens, HEAD)
+    grad_tokens = finish_call(side_array, end_back, cotangent, grad_tokens, rows // BLOCK - 1)
     wanted = inner_half + 64
 
     def narrow_part(index):

time: 281 us -> 259 us (0.922)
  Pallas kernels: 149 us -> 239 us
  waiting for transfers between devices: 74.9 us -> 2.99 us
  other arithmetic: 18 us -> 3.44 us
  between operations: 14.2 us -> 0.76 us
  local copies, waits for them, and re-layouts: 15.2 us -> 9.07 us
  starting transfers between devices: 6.87 us -> 2.09 us
    pallas_call x1, Pallas kernels: 145 us -> 224 us  [fast_call(): pl.pallas_call(fast_kernel, out_shape=[jax.ShapeDtypeStruct(shape, dtype)...]
    ppermute x6 -> x2, waiting for transfers between devices: 74.9 us -> 2.99 us  [swap(): return lax.ppermute(value, 'ch', SWAP)]
    pallas_call x0 -> x1, Pallas kernels: none -> 11 us  [assemble_call(): pl.pallas_call(assemble_kernel, grid_spec=pltpu.PrefetchScalarGridSpec(nu...]
    select_n x4 -> x0, other arithmetic: 9.41 us -> none  [the longest x2 8.23 us: placed(): jnp.where(low_side, jnp.stack([own, back], 0), jnp.stack([back, own], 0))]
    slice x5 -> x0, local copies, waits for them, and re-layouts: 5.13 us -> none  [the longest x1 2.98 us: fast_body(): x_first, x_second = (swap(first_send), swap(x_send[FIRST:]))]
    ppermute x6 -> x2, starting transfers between devices: 6.83 us -> 2.09 us  [swap(): return lax.ppermute(value, 'ch', SWAP)]
    another operation x3 -> x1, other arithmetic: 3.98 us -> 0.17 us  [the longest x1 3.19 us: placed(): jnp.stack([own, back], 0)]
  transfers between devices with their start and end apart: 7 -> 2, of which waited for: 5 -> 2; matrix products, arithmetic and copies ran while one was open for 9% -> 2% of each run, Pallas kernels for 0% -> 5%
where the time goes in v4:
time: 259 us; the launch traced here: 258 us
  Pallas kernels  239 us (92%)
  local copies, waits for them, and re-layouts  9.07 us (4%)
  other arithmetic  3.44 us (1%)
  waiting for transfers between devices  2.99 us (1%)
    pallas_call x1, Pallas kernels, fast_call(): pl.pallas_call(fast_kernel, out_shape=[jax.ShapeDtypeStruct(shape, dtype)...  224 us
    pallas_call x1, Pallas kernels, assemble_call(): pl.pallas_call(assemble_kernel, grid_spec=pltpu.PrefetchScalarGridSpec(nu...  11 us
  transfers between devices with their start and end apart: 2, of which 2 were waited for; matrix products, arithmetic and copies ran while one was open for 2% of the time, Pallas kernels for 5%

profile of v4, /device:TPU:24, one launch (start us, length us, event | category | flops | bytes accessed | tf_op | source)
XLA Modules:
  0.0 257.7 jit_solution(18153401198102671398)
XLA Ops:
  0.6 0.0 copy-start
  0.7 0.7 copy-done
  1.3 0.7 convert_bitcast_fusion
  2.1 0.9 concatenate.7
  3.0 0.6 broadcast_in_dim.17.own_vectors
  3.6 0.1 copy.41
  3.7 0.2 reduce-window.4
  3.9 0.1 slice_reduce_fusion
  4.0 0.7 convert_reduce_fusion
  4.7 0.1 fusion.3
  4.9 0.1 stack.41
  5.0 1.0 copy.42.masks
  6.0 0.1 pad.3.clone
  6.1 1.8 maximum_maximum_fusion.own_weights
  7.8 224.3 %shard_map.263 = (bf16[2048,640]{1,0:T(8,128)(2,1)}, bf16[2048,640]{1,0:T(8,128)(2,1)}, f32[2048,640]{1,0:T(8,128)}, bf16[2048,640]{1,0:T(8,128)(2,1)}, bf16[512...) custom-call(bf16[2,2048,640]{2,1,0:T(8,128)(2,1)} %tokens.1, ...), custom_call_target="tpu_custom_call" | custom-call | flops 45298483200 | bytes 125829120 | tf_op jit(solution)/shard_map/pallas_call | solution.py:1047
  232.1 0.6 collective-permute-start.1
  232.7 1.5 collective-permute-start
  234.2 1.7 slice.68
  235.9 0.0 copy-start.3
  235.9 11.0 %shard_map.264 = (bf16[2,2048,640]{2,1,0:T(8,128)(2,1)}, f32[2,2048,640]{2,1,0:T(8,128)}) custom-call(s32[1]{0:T(128)} %bitcast.side_ref, bf16[2048,640]{1,0:T(8,128)(2,1)} %get-tuple-element.24.out_own, bf16[2048,640]{1,0:T(8,128)(2,1)} %get-tuple-element.25.out_back, f32[2048,640]{1,0:T(8,128)} %get-tuple-element.26.dx_own, ...), custom_call_target="tpu_custom_call" | custom-call | flops 1310720 | bytes 31457280 | tf_op jit(solution)/shard_map/pallas_call | solution.py:1121
  246.8 0.0 copy-done.3
  246.8 0.6 slice_reduce_fusion.4
  247.5 0.6 slice_reduce_fusion.1
  248.1 1.7 slice_bitcast_fusion
  249.7 0.3 collective-permute-done.1.tail_ref
  250.0 0.0 copy-start.2
  250.0 0.8 copy-done.2
  250.8 2.2 shard_map.265.whole_ref
  253.0 2.7 %collective-permute-done.tail_ref = bf16[256,640]{1,0:T(8,128)(2,1)} collective-permute-done((bf16[256,640]{1,0:T(8,128)(2,1)}, bf16[256,640]{1,0:T(8,128)(2,1)}, u32[]{:S(2)}, u32[]{:S(2)}) %collective-permute-start) | collective-permute-done | bytes 327712 | tf_op jit(solution)/shard_map/ppermute | solution.py:1196
  255.8 0.0 copy-start.1
  255.8 2.0 shard_map.266
  257.7 0.0 copy-done.1
  (11 shorter events, 0.1 us)
Async XLA Ops:
  0.6 0.7 copy-start
  232.1 17.9 %collective-permute-start.1 = (bf16[512,640]{1,0:T(8,128)(2,1)}, bf16[512,640]{1,0:T(8,128)(2,1)S(1)}, u32[]{:S(2)}, u32[]{:S(2)}) collective-permute-start(bf16[512,640]{1,0:T(8,128)(2,1)} %get-tuple-element.30), channel_id=1, source_target_pairs={{0,1},{1,0},{2,3},{3,2},{4,5},{5,4},{6,7},{7,6},{8,9},{9,8},{10,11... | collective-permute-start | bytes 1966088 | tf_op jit(solution)/shard_map/ppermute | solution.py:1196
  232.7 23.1 %collective-permute-start = (bf16[256,640]{1,0:T(8,128)(2,1)}, bf16[256,640]{1,0:T(8,128)(2,1)}, u32[]{:S(2)}, u32[]{:S(2)}) collective-permute-start(bf16[256,640]{1,0:T(8,128)(2,1)} %get-tuple-element.29), channel_id=1, source_target_pairs={{0,1},{1,0},{2,3},{3,2},{4,5},{5,4},{6,7},{7,6},{8,9},{9,8},{10,11... | collective-permute-start | bytes 983048 | tf_op jit(solution)/shard_map/ppermute | solution.py:1196
  235.9 11.0 %copy-start.3 = (f32[1,4224]{1,0:T(1,128)S(1)}, f32[1,4224]{1,0:T(1,128)}, u32[]{:S(2)}) copy-start(f32[1,4224]{1,0:T(1,128)} %get-tuple-element.32) | copy-start | bytes 50692
  250.0 0.8 copy-start.2
  255.8 2.0 copy-start.1

commit v5 on v4

--- a/solution.py
+++ b/solution.py
@@ -482,20 +482,28 @@
 CHUNKS = 4
 CONV_PAD = 8
 HEAD = 5
+LEAD = 128
 
 
 def fast_kernel(
-    tokens, cot, own_weights, own_vectors, masks,
+    tokens, cot, lengths, residues, proj_in, proj_out, conv_own, *rest,
+) -> None:
+    vectors, refs = rest[:9], rest[9:]
+    fast_steps(tokens, cot, lengths, residues, proj_in, proj_out, conv_own, vectors, *refs)
+
+
+def fast_steps(
+    tokens, cot, lengths, residues, proj_in, proj_out, conv_own, vectors,
     out_own, out_back, dx_own, dx_back, dx_tail, dx_end, grads_out, sums_out,
     x_other, g_conv, s1, h1, s2, h3, s3,
-    other_vectors, other_weights, wide, narrow, stage,
+    masks, own_vectors, other_vectors, wide, narrow, stage,
     a1v, a2f, a3v, gyv, dh3f, out_send, w_in, w_out, w_conv,
     k_in, s_in, r0_in, r1_in, r2_in, r3_in,
     k_out, s_out, r0_out, r1_out, r2_out, r3_out,
     k_low, s_low, r0_low, r1_low, r2_low, r3_low,
     k_mid, s_mid, r0_mid, r1_mid, r2_mid, r3_mid,
     k_top, s_top, r0_top, r1_top, r2_top, r3_top,
-    smalls, grads, cross_send, cross_recv, small_send, small_recv, load_sems,
+    smalls, cross_send, cross_recv, small_send, small_recv, load_sems,
     swap_sems, token_sems, in_gather, out_gather, conv_gather, gy_sems, out_sems, dx_sems, a2_sems, dh3_sems, in_sems, out_rs_sems, low_sems, mid_sems, top_sems, cross_sems, small_sems,
 ):
     rows = a1v.shape[0]
@@ -529,11 +537,15 @@
         piece = pl.ds(at * part, part)
         return remote(cot.at[1 - side, piece], gyv.at[side, piece], gy_sems, at, across)
 
+    token_part = (rows - LEAD) // CHUNKS
+
     def token_copy(at):
-        piece = pl.ds(pl.multiple_of(at * part, part), part)
+        piece = pl.ds(pl.multiple_of(LEAD + at * token_part, 16), token_part)
         return remote(tokens.at[1 - side, piece], x_other.at[piece], token_sems, at, across)
 
-    part_in = w_in.shape[4]
+    lead = pl.ds(0, LEAD)
+    lead_copy = remote(tokens.at[1 - side, lead], x_other.at[lead], token_sems, CHUNKS, across)
+
     tail_rows = k_top.shape[1]
     own_gy = pltpu.make_async_copy(cot.at[side], gyv.at[side], load_sems.at[0])
     def out_copy(at):
@@ -599,8 +611,27 @@
         pl.semaphore_signal(barrier, inc=1, device_id=device, device_id_type=pl.DeviceIdType.MESH)
     pl.semaphore_wait(barrier, 7)
 
+    lead_copy.start()
+    height = inner // 16
+    part_in = proj_in.shape[0]
+    quarter = half // 2
+    wanted = quarter + 64
+    cross_send[0:part_in, 0:quarter] = proj_in[...]
+    cross_send[part_in : 2 * part_in, 0:quarter] = proj_out[...]
+    cross_send[2 * part_in :, 0:quarter] = jnp.concatenate(
+        [conv_own[tap].astype(jnp.float32) for tap in range(KERNEL_TAPS)]
+        + [jnp.zeros((CONV_PAD, quarter), jnp.float32)],
+        axis=0,
+    ).astype(jnp.bfloat16)
+    cross_send[:, quarter:] = jnp.zeros((cross_send.shape[0], wanted - quarter), jnp.bfloat16)
+    own_vectors[...] = jnp.zeros_like(own_vectors)
+    at = 0
+    for vector in vectors:
+        width = vector.shape[0]
+        own_vectors[:, at : at + width] = vector[...].reshape(1, width)
+        at += width + width % 128
     swaps = [
-        remote(own_weights, other_weights, swap_sems, 0, across),
+        remote(cross_send, cross_recv, swap_sems, 0, across),
         remote(own_vectors, other_vectors, swap_sems, 1, across),
     ]
     for swap in swaps:
@@ -610,6 +641,41 @@
     for at in range(CHUNKS):
         gy_copy(at).start()
     own_gy.start()
+
+    ends = jnp.where(low, lengths[0:1, :], lengths[1:2, :]).astype(jnp.float32)
+    count = ends.shape[1]
+    upper = lax.broadcasted_iota(jnp.int32, (count, count), 0) <= lax.broadcasted_iota(jnp.int32, (count, count), 1)
+    ends = lax.dot_general(
+        jnp.broadcast_to(ends, (8, count)),
+        upper.astype(jnp.float32),
+        (((1,), (0,)), ((), ())),
+        precision=lax.Precision.HIGHEST,
+        preferred_element_type=jnp.float32,
+    )[0:1, :]
+
+    def mask_block(at, _):
+        base = pl.multiple_of(at * BLOCK, BLOCK)
+        span = BLOCK + 2 * HALO
+        spot = lax.broadcasted_iota(jnp.int32, (span, count), 0) + (place * rows + base - HALO)
+        inside = (spot >= 0) & (spot < rows * (last + 1))
+        reached = jnp.where(ends <= spot.astype(jnp.float32), 1.0, 0.0)
+        segment = jnp.sum(jnp.where(inside, reached, -1.0 / count), axis=1, keepdims=True)
+        own_segment = segment[HALO : HALO + BLOCK]
+        lane = lax.broadcasted_iota(jnp.int32, (BLOCK, 8), 1)
+        columns = jnp.zeros((BLOCK, 8), jnp.float32)
+        for tap in range(KERNEL_TAPS):
+            same = segment[tap * DILATION_STEP : tap * DILATION_STEP + BLOCK] == own_segment
+            columns = jnp.where((lane == tap) & same, 1.0, columns)
+        kept = residues[:, pl.ds(base, BLOCK)]
+        kept = jnp.where(low, kept[0:1, :], kept[1:2, :]).astype(jnp.float32)
+        square = (BLOCK, BLOCK)
+        diagonal = lax.broadcasted_iota(jnp.int32, square, 0) == lax.broadcasted_iota(jnp.int32, square, 1)
+        keep = jnp.sum(jnp.where(diagonal, kept, 0.0), axis=1, keepdims=True)
+        columns = jnp.where(lane == KERNEL_TAPS, keep, columns)
+        masks[pl.ds(base, BLOCK), :] = columns.astype(jnp.bfloat16)
+        return 0
+
+    lax.fori_loop(0, rows // BLOCK, mask_block, 0)
     smalls[...] = jnp.zeros_like(smalls)
 
     @pl.when(place == 0)
@@ -628,15 +694,13 @@
 
     for swap in swaps:
         swap.wait()
-    rows_here = both(own_weights[...], other_weights[...]).astype(jnp.bfloat16)
+    rows_here = both(cross_send[:, 0:quarter], cross_recv[:, 0:quarter]).astype(jnp.bfloat16)
     here = (bits[3], bits[2], bits[1], bits[0])
     w_in[here] = rows_here[:part_in]
     w_out[here] = rows_here[part_in : 2 * part_in]
-    stage[0, 0, 0] = rows_here[2 * part_in :]
-    own_conv = pltpu.make_async_copy(stage.at[0, 0, 0], g_conv.at[here], load_sems.at[1])
+    stage[0, 0] = rows_here[2 * part_in :]
+    own_conv = pltpu.make_async_copy(stage.at[0, 0], g_conv.at[here], load_sems.at[1])
     own_conv.start()
-    quarter = half // 2
-    wanted = quarter + 64
     for index in range(3):
         lanes = slice(index * half, (index + 1) * half)
         wide[index : index + 1, :] = both(own_vectors[:, lanes], other_vectors[:, lanes])
@@ -698,35 +762,28 @@
 
         return 0
 
+    lead_copy.wait_recv()
     lax.fori_loop(0, CHUNKS, first_chunk, 0)
     halo_start(a2f, a2_sems)
     gather_next(conv_rows, 2)
     gather_next(out_rows, 3)
     gather_next(conv_rows, 3)
 
-    height = inner // 16
-
     def conv_load(pair):
-        return pltpu.make_async_copy(g_conv.at[pair // 2, pair % 2], stage.at[pair % 2], load_sems.at[2 + pair % 2])
-
-    conv_load(0).start()
-    conv_load(1).start()
+        return pltpu.make_async_copy(g_conv.at[pair // 2, pair % 2], stage, load_sems.at[2])
 
     def relay(pair, _):
+        conv_load(pair).start()
         conv_load(pair).wait()
         for low_bit in range(2):
-            even = stage[pair % 2, low_bit, 0].astype(jnp.float32)
-            odd = stage[pair % 2, low_bit, 1].astype(jnp.float32)
+            even = stage[low_bit, 0].astype(jnp.float32)
+            odd = stage[low_bit, 1].astype(jnp.float32)
             at = pl.multiple_of((2 * pair + low_bit) * 2 * height, 2 * height)
             for tap in range(KERNEL_TAPS):
                 top = tap * height
                 w_conv[tap, pl.ds(at, 2 * height), :] = jnp.concatenate(
                     [even[top : top + height], odd[top : top + height]], axis=0
                 ).astype(jnp.bfloat16)
-
-        @pl.when(pair < 2)
-        def _():
-            conv_load(pair + 2).start()
 
         return 0
 
@@ -981,17 +1038,17 @@
         height = keep.shape[1]
         value = keep[mine]
         left, right = value[:, :wanted], value[:, inner - wanted :]
-        grads[row : row + height, :] = jnp.where(low, left, right)
         cross_send[row : row + height, :] = jnp.where(low, right, left).astype(jnp.bfloat16)
         row += height
+    for at in range(blocks):
+        out_copy(at).wait()
     cross = remote(cross_send, cross_recv, cross_sems, 0, across)
     cross.start()
     dx_copy(HEAD - 1).start()
+    lead_copy.wait_send()
     for at in range(CHUNKS):
         token_copy(at).wait_send()
         gy_copy(at).wait_send()
-    for at in range(blocks):
-        out_copy(at).wait()
     small_step(4)
     for index in range(3):
         both = smalls[2 * index : 2 * index + 2, :]
@@ -1001,16 +1058,25 @@
         at = 3 * half + index * wanted
         sums_out[:, at : at + quarter] = jnp.where(low, both[:, :quarter], both[:, quarter:])
     cross.wait()
-    total = grads[...] + cross_recv[...].astype(jnp.float32)
-    grads_out[...] = jnp.where(low, total[:, :quarter], total[:, wanted - quarter :])
+    row = 0
+    for keep, _, _, _, order in (in_set, out_set, low_set, mid_set, top_set):
+        height = keep.shape[1]
+        value = keep[bits[order[0]] + 2 * bits[order[1]] + 4 * bits[order[2]]]
+        came = cross_recv[row : row + height, :].astype(jnp.float32)
+        grads_out[row : row + height, :] = jnp.where(
+            low, value[:, :quarter] + came[:, :quarter], value[:, quarter:] + came[:, wanted - quarter :]
+        )
+        row += height
     for at in range(HEAD):
         dx_copy(at).wait()
 
 
-def fast_call(tokens, cot, own_weights, own_vectors, masks, part_in, part_conv):
+def fast_call(tokens, cot, lengths, residues, proj_in, proj_out, conv_own, vectors):
     _, rows, half = tokens.shape
     model = 2 * half
-    inner = 2 * own_weights.shape[1]
+    inner = 2 * proj_in.shape[1]
+    part_in = proj_in.shape[0]
+    part_conv = conv_own.shape[1]
     f32, bf16 = jnp.float32, jnp.bfloat16
     tall = KERNEL_TAPS * part_conv + CONV_PAD
     any_spec = pl.BlockSpec(memory_space=pl.ANY)
@@ -1047,14 +1113,15 @@
     results = pl.pallas_call(
         fast_kernel,
         out_shape=[jax.ShapeDtypeStruct(shape, dtype) for shape, dtype in shapes],
-        in_specs=[any_spec] * 2 + [vmem_spec] * 3,
+        in_specs=[any_spec] * 2 + [vmem_spec] * 14,
         out_specs=[any_spec] * 6 + [vmem_spec] * 2 + [any_spec] * 7,
         scratch_shapes=[
-            pltpu.VMEM(own_vectors.shape, f32),
-            pltpu.VMEM(own_weights.shape, bf16),
+            pltpu.VMEM((rows, 8), bf16),
+            pltpu.VMEM((1, 3 * half + 6 * wanted), f32),
+            pltpu.VMEM((1, 3 * half + 6 * wanted), f32),
             pltpu.VMEM((8, model), f32),
             pltpu.VMEM((8, inner), f32),
-            pltpu.VMEM((2, 2, 2, tall, inner), bf16),
+            pltpu.VMEM((2, 2, tall, inner), bf16),
             pltpu.VMEM((rows, model), bf16),
             pltpu.VMEM((rows + 2 * HALO, inner), bf16),
             pltpu.VMEM((rows, inner), bf16),
@@ -1069,14 +1136,13 @@
         + sums(tall - 2 * part_in)
         + [
             pltpu.VMEM((16, inner), f32),
-            pltpu.VMEM((total, wanted), f32),
             pltpu.VMEM((total, wanted), bf16),
             pltpu.VMEM((total, wanted), bf16),
             pltpu.VMEM((5, 16, inner), f32),
             pltpu.VMEM((5, 16, inner), f32),
-            pltpu.SemaphoreType.DMA((4,)),
+            pltpu.SemaphoreType.DMA((3,)),
             sems(2),
-            sems(CHUNKS),
+            sems(CHUNKS + 1),
             sems(4),
             sems(4),
             sems(4),
@@ -1097,12 +1163,13 @@
             collective_id=0, has_side_effects=True, vmem_limit_bytes=65280 * 2**10
         ),
         cost_estimate=pl.CostEstimate(flops=flops, bytes_accessed=120 * 2**20, transcendentals=0),
-    )(tokens, cot, own_weights, own_vectors, masks)
+    )(tokens, cot, lengths, residues, proj_in, proj_out, conv_own, *vectors)
     return results[:8]
 
 
 def finish_kernel(side_ref, tail_ref, cot_ref, whole_ref, out_ref):
-    out_ref[0] = tail_ref[...].astype(jnp.float32) + cot_ref[0].astype(jnp.float32)
+    at = pl.ds(pl.multiple_of(pl.program_id(0) * BLOCK, BLOCK), BLOCK)
+    out_ref[0] = tail_ref[at, :].astype(jnp.float32) + cot_ref[0].astype(jnp.float32)
 
 
 def assemble_kernel(side_ref, out_own, out_back, dx_own, dx_back, cot, block_out, grad_tokens):
@@ -1150,7 +1217,7 @@
             num_scalar_prefetch=1,
             grid=(tail.shape[0] // BLOCK,),
             in_specs=[
-                pl.BlockSpec((BLOCK, half), lambda i, side_ref: (i, 0)),
+                pl.BlockSpec(memory_space=pltpu.VMEM),
                 pl.BlockSpec((1, BLOCK, half), theirs),
                 pl.BlockSpec(memory_space=pl.ANY),
             ],
@@ -1185,59 +1252,26 @@
 ):
     micro, rows, half = tokens.shape
     inner_half = in_bias.shape[0]
-    inner = 2 * inner_half
-    model = 2 * half
-    seq_count = lax.axis_size("seq")
     side = lax.axis_index("ch")
-    low_side = side == 0
-    f32, bf16 = jnp.float32, jnp.bfloat16
 
     def swap(value):
         return lax.ppermute(value, "ch", SWAP)
 
-    def own_of(value):
-        return lax.dynamic_index_in_dim(value, side, 0, keepdims=False)
-
-    def other_of(value):
-        return lax.dynamic_index_in_dim(value, 1 - side, 0, keepdims=False)
-
-    gap = jnp.zeros((64,), f32)
-    pieces = [first_gain, first_shift, out_bias]
-    for piece in (in_bias, mid_gain, mid_shift, conv_bias, last_gain, last_shift):
-        pieces += [piece, gap]
-    own_vectors = lax.optimization_barrier(jnp.concatenate(pieces))[None]
     part_in = proj_in.shape[0]
     part_conv = conv_weight.shape[1]
-    own_weights = jnp.concatenate(
-        [
-            proj_in,
-            proj_out.T,
-            conv_weight.reshape(KERNEL_TAPS * part_conv, inner_half),
-            jnp.zeros((CONV_PAD, inner_half), bf16),
-        ],
-        axis=0,
-    )
-
-    places = lax.axis_index("seq") * rows + jnp.arange(rows + 2 * HALO, dtype=jnp.int32) - HALO
-    inside = (places >= 0) & (places < rows * seq_count)
-    bounds = jnp.cumsum(own_of(seq_lengths))[:-1]
-    segment = jnp.sum((places[:, None] >= bounds[None, :]).astype(jnp.int32), axis=1)
-    segment = jnp.where(inside, segment, -1)
-    middle = segment[HALO : HALO + rows]
-    columns = [
-        (segment[tap * DILATION_STEP : tap * DILATION_STEP + rows] == middle).astype(bf16)
-        for tap in range(KERNEL_TAPS)
-    ]
-    zero = jnp.zeros((rows,), bf16)
-    masks = jnp.stack(columns + [own_of(residue_mask).astype(bf16), zero, zero], axis=1)
-
+    vectors = (
+        first_gain, first_shift, out_bias, in_bias, mid_gain, mid_shift, conv_bias, last_gain, last_shift
+    )
     out_own, out_back, dx_own, dx_back, dx_tail, dx_end, grads, sums = fast_call(
-        tokens, cotangent, own_weights, own_vectors, masks, part_in, part_conv
-    )
+        tokens, cotangent, seq_lengths, residue_mask, proj_in, proj_out.T, conv_weight, vectors
+    )
+    conv_part = grads[2 * part_in : 2 * part_in + KERNEL_TAPS * part_conv]
 
     side_array = side.astype(jnp.int32).reshape(1)
-    tail_back, end_back = swap(dx_tail), swap(dx_end)
+    tail_back = swap(dx_tail)
     block_out, grad_tokens = assemble_call(side_array, out_own, out_back, dx_own, dx_back, cotangent)
+    dx_end, grad_tokens = lax.optimization_barrier((dx_end, grad_tokens))
+    end_back = swap(dx_end)
     grad_tokens = finish_call(side_array, tail_back, cotangent, grad_tokens, HEAD)
     grad_tokens = finish_call(side_array, end_back, cotangent, grad_tokens, rows // BLOCK - 1)
     wanted = inner_half + 64
@@ -1255,7 +1289,7 @@
         narrow_part(0),
         narrow_part(1),
         narrow_part(2),
-        grads[2 * part_in : 2 * part_in + KERNEL_TAPS * part_conv].reshape(KERNEL_TAPS, part_conv, inner_half),
+        conv_part.reshape(KERNEL_TAPS, part_conv, inner_half),
         narrow_part(3),
         narrow_part(4),
         narrow_part(5),

time: 259 us -> 252 us (0.973)
  local copies, waits for them, and re-layouts: 9.07 us -> 4.22 us
  other arithmetic: 3.44 us -> 0 us
  transfers between devices with their start and end apart: 2 -> 2, of which waited for: 2 -> 2; matrix products, arithmetic and copies ran while one was open for 2% -> 1% of each run, Pallas kernels for 5% -> 5%
where the time goes in v5:
time: 252 us; the launch traced here: 251 us
  Pallas kernels  240 us (95%)
  waiting for transfers between devices  4.6 us (2%)
  local copies, waits for them, and re-layouts  4.22 us (2%)
    pallas_call x1, Pallas kernels, fast_call(): pl.pallas_call(fast_kernel, out_shape=[jax.ShapeDtypeStruct(shape, dtype)...  224 us
    pallas_call x1, Pallas kernels, assemble_call(): pl.pallas_call(assemble_kernel, grid_spec=pltpu.PrefetchScalarGridSpec(nu...  11 us
  transfers between devices with their start and end apart: 2, of which 2 were waited for; matrix products, arithmetic and copies ran while one was open for 1% of the time, Pallas kernels for 5%

profile of v5, /device:TPU:24, one launch (start us, length us, event | category | flops | bytes accessed | tf_op | source)
XLA Modules:
  0.0 251.4 jit_solution(15626426018584110026)
XLA Ops:
  0.7 224.5 %shard_map.263 = (bf16[2048,640]{1,0:T(8,128)(2,1)}, bf16[2048,640]{1,0:T(8,128)(2,1)}, f32[2048,640]{1,0:T(8,128)}, bf16[2048,640]{1,0:T(8,128)(2,1)}, bf16[512...) custom-call(bf16[2,2048,640]{2,1,0:T(8,128)(2,1)} %tokens.1, ...), custom_call_target="tpu_custom_call" | custom-call | flops 45298483200 | bytes 125829120 | tf_op jit(solution)/shard_map/pallas_call | solution.py:1113
  225.1 0.6 collective-permute-start.1
  225.7 0.0 copy-start.1
  225.7 0.0 copy-start.3
  225.7 11.0 %shard_map.264 = (bf16[2,2048,640]{2,1,0:T(8,128)(2,1)}, f32[2,2048,640]{2,1,0:T(8,128)}) custom-call(s32[1]{0:T(128)} %bitcast.side_ref, bf16[2048,640]{1,0:T(8,128)(2,1)} %get-tuple-element.26.out_own, bf16[2048,640]{1,0:T(8,128)(2,1)} %get-tuple-element.27.out_back, f32[2048,640]{1,0:T(8,128)} %get-tuple-element.28.dx_own, ...), custom_call_target="tpu_custom_call" | custom-call | flops 1310720 | bytes 31457280 | tf_op jit(solution)/shard_map/pallas_call | solution.py:1188
  236.8 1.5 collective-permute-start
  238.3 0.0 copy-done.1
  238.3 0.7 slice.42
  239.0 0.0 copy-done.3
  239.0 0.6 slice_reduce_fusion.3
  239.6 0.6 slice_reduce_fusion
  240.3 0.7 slice_bitcast_fusion
  241.0 2.1 collective-permute-done.1.tail_ref
  243.1 0.0 copy-start
  243.1 0.8 copy-done
  243.9 2.3 shard_map.265.whole_ref
  246.2 2.5 collective-permute-done.tail_ref
  248.7 0.0 copy-start.2
  248.7 0.7 copy-done.2
  249.4 2.0 shard_map.266
Async XLA Ops:
  225.1 17.9 %collective-permute-start.1 = (bf16[512,640]{1,0:T(8,128)(2,1)}, bf16[512,640]{1,0:T(8,128)(2,1)S(1)}, u32[]{:S(2)}, u32[]{:S(2)}) collective-permute-start(bf16[512,640]{1,0:T(8,128)(2,1)} %get-tuple-element.34), channel_id=1, source_target_pairs={{0,1},{1,0},{2,3},{3,2},{4,5},{5,4},{6,7},{7,6},{8,9},{9,8},{10,11... | collective-permute-start | bytes 1966088 | tf_op jit(solution)/shard_map/ppermute | solution.py:1258
  225.7 12.5 %copy-start.1 = (f32[368,320]{1,0:T(8,128)S(1)}, f32[368,320]{1,0:T(8,128)}, u32[]{:S(2)}) copy-start(f32[368,320]{1,0:T(8,128)} %get-tuple-element.37) | copy-start | bytes 1413124
  225.7 13.3 %copy-start.3 = (f32[1,4224]{1,0:T(1,128)S(1)}, f32[1,4224]{1,0:T(1,128)}, u32[]{:S(2)}) copy-start(f32[1,4224]{1,0:T(1,128)} %get-tuple-element.36) | copy-start | bytes 50692
  236.8 11.9 %collective-permute-start = (bf16[256,640]{1,0:T(8,128)(2,1)}, bf16[256,640]{1,0:T(8,128)(2,1)S(1)}, u32[]{:S(2)}, u32[]{:S(2)}) collective-permute-start(bf16[256,640]{1,0:T(8,128)(2,1)} %get-tuple-element.33), channel_id=1, source_target_pairs={{0,1},{1,0},{2,3},{3,2},{4,5},{5,4},{6,7},{7,6},{8,9},{9,8},{10,11... | collective-permute-start | bytes 983048 | tf_op jit(solution)/shard_map/ppermute | solution.py:1258
  243.1 0.8 copy-start
  248.7 0.7 copy-start.2

commit v6 on v5

--- a/solution.py
+++ b/solution.py
@@ -517,7 +517,8 @@
     bits = [lax.rem(place // (1 << bit), 2) for bit in range(4)]
     across = {"ch": 1 - side}
     pairs = [{"seq": place + (1 << bit) * (1 - 2 * bits[bit])} for bit in range(4)]
-    before, after = {"seq": place - 1}, {"seq": place + 1}
+    before = {"seq": lax.rem(place + last, last + 1)}
+    after = {"seq": lax.rem(place + 1, last + 1)}
 
     def remote(src, dst, sems, at, device):
         return pltpu.make_async_remote_copy(
@@ -606,8 +607,7 @@
         pltpu.emit_pipeline(step, grid=(count or blocks,), in_specs=[spec(r) for r in ins], out_specs=out_specs)(*ins, *outs)
 
     barrier = pltpu.get_barrier_semaphore()
-    ring = [{"seq": lax.rem(place + last, last + 1)}, {"seq": lax.rem(place + 1, last + 1)}]
-    for device in [across] + pairs + ring:
+    for device in [across] + pairs + [before, after]:
         pl.semaphore_signal(barrier, inc=1, device_id=device, device_id_type=pl.DeviceIdType.MESH)
     pl.semaphore_wait(barrier, 7)
 
@@ -616,14 +616,19 @@
     part_in = proj_in.shape[0]
     quarter = half // 2
     wanted = quarter + 64
-    cross_send[0:part_in, 0:quarter] = proj_in[...]
-    cross_send[part_in : 2 * part_in, 0:quarter] = proj_out[...]
-    cross_send[2 * part_in :, 0:quarter] = jnp.concatenate(
-        [conv_own[tap].astype(jnp.float32) for tap in range(KERNEL_TAPS)]
-        + [jnp.zeros((CONV_PAD, quarter), jnp.float32)],
-        axis=0,
-    ).astype(jnp.bfloat16)
-    cross_send[:, quarter:] = jnp.zeros((cross_send.shape[0], wanted - quarter), jnp.bfloat16)
+    packed = cross_send.shape[0]
+
+    def pack(pieces):
+        pieces = [piece.astype(jnp.float32) for piece in pieces]
+        short = 2 * packed - sum(piece.shape[0] for piece in pieces)
+        value = jnp.concatenate(pieces + [jnp.zeros((short, quarter), jnp.float32)], axis=0)
+        cross_send[...] = jnp.concatenate([value[:packed], value[packed:]], axis=1).astype(jnp.bfloat16)
+
+    def unpack(ref):
+        value = ref[...].astype(jnp.float32)
+        return jnp.concatenate([value[:, :quarter], value[:, quarter:]], axis=0)
+
+    pack([proj_in[...], proj_out[...]] + [conv_own[tap] for tap in range(KERNEL_TAPS)])
     own_vectors[...] = jnp.zeros_like(own_vectors)
     at = 0
     for vector in vectors:
@@ -694,11 +699,11 @@
 
     for swap in swaps:
         swap.wait()
-    rows_here = both(cross_send[:, 0:quarter], cross_recv[:, 0:quarter]).astype(jnp.bfloat16)
+    rows_here = both(unpack(cross_send), unpack(cross_recv)).astype(jnp.bfloat16)
     here = (bits[3], bits[2], bits[1], bits[0])
     w_in[here] = rows_here[:part_in]
     w_out[here] = rows_here[part_in : 2 * part_in]
-    stage[0, 0] = rows_here[2 * part_in :]
+    stage[0, 0] = rows_here[2 * part_in : 2 * part_in + stage.shape[2]]
     own_conv = pltpu.make_async_copy(stage.at[0, 0], g_conv.at[here], load_sems.at[1])
     own_conv.start()
     for index in range(3):
@@ -1032,14 +1037,16 @@
     small_step(3)
     small_start(4)
 
-    row = 0
-    for keep, _, _, _, order in (in_set, out_set, low_set, mid_set, top_set):
-        mine = bits[order[0]] + 2 * bits[order[1]] + 4 * bits[order[2]]
-        height = keep.shape[1]
-        value = keep[mine]
-        left, right = value[:, :wanted], value[:, inner - wanted :]
-        cross_send[row : row + height, :] = jnp.where(low, right, left).astype(jnp.bfloat16)
-        row += height
+    def owned(group):
+        keep, order = group[0], group[4]
+        return keep[bits[order[0]] + 2 * bits[order[1]] + 4 * bits[order[2]]]
+
+    groups = (in_set, out_set, low_set, mid_set, top_set)
+    others = []
+    for group in groups:
+        value = owned(group)
+        others.append(jnp.where(low, value[:, quarter:], value[:, :quarter]))
+    pack(others)
     for at in range(blocks):
         out_copy(at).wait()
     cross = remote(cross_send, cross_recv, cross_sems, 0, across)
@@ -1058,13 +1065,13 @@
         at = 3 * half + index * wanted
         sums_out[:, at : at + quarter] = jnp.where(low, both[:, :quarter], both[:, quarter:])
     cross.wait()
+    came = unpack(cross_recv)
     row = 0
-    for keep, _, _, _, order in (in_set, out_set, low_set, mid_set, top_set):
-        height = keep.shape[1]
-        value = keep[bits[order[0]] + 2 * bits[order[1]] + 4 * bits[order[2]]]
-        came = cross_recv[row : row + height, :].astype(jnp.float32)
-        grads_out[row : row + height, :] = jnp.where(
-            low, value[:, :quarter] + came[:, :quarter], value[:, quarter:] + came[:, wanted - quarter :]
+    for group in groups:
+        value = owned(group)
+        height = value.shape[0]
+        grads_out[row : row + height, :] = (
+            jnp.where(low, value[:, :quarter], value[:, quarter:]) + came[row : row + height]
         )
         row += height
     for at in range(HEAD):
@@ -1083,6 +1090,7 @@
     vmem_spec = pl.BlockSpec(memory_space=pltpu.VMEM)
     total = 2 * part_in + tall
     wanted = half // 2 + 64
+    packed = (total + 31) // 32 * 16
 
     def sums(height):
         return [pltpu.VMEM((8, height, inner), f32), pltpu.VMEM((8, height, inner), bf16)] + [
@@ -1136,8 +1144,8 @@
         + sums(tall - 2 * part_in)
         + [
             pltpu.VMEM((16, inner), f32),
-            pltpu.VMEM((total, wanted), bf16),
-            pltpu.VMEM((total, wanted), bf16),
+            pltpu.VMEM((packed, inner), bf16),
+            pltpu.VMEM((packed, inner), bf16),
             pltpu.VMEM((5, 16, inner), f32),
             pltpu.VMEM((5, 16, inner), f32),
             pltpu.SemaphoreType.DMA((3,)),

time: 252 us -> 251 us (level)
  no operation moved by 1% of the time
where the time goes in v6:
time: 251 us; the launch traced here: 250 us
  Pallas kernels  238 us (95%)
  waiting for transfers between devices  4.6 us (2%)
  local copies, waits for them, and re-layouts  4.22 us (2%)
    pallas_call x1, Pallas kernels, fast_call(): pl.pallas_call(fast_kernel, out_shape=[jax.ShapeDtypeStruct(shape, dtype)...  223 us
    pallas_call x1, Pallas kernels, assemble_call(): pl.pallas_call(assemble_kernel, grid_spec=pltpu.PrefetchScalarGridSpec(nu...  11 us
  transfers between devices with their start and end apart: 2, of which 2 were waited for; matrix products, arithmetic and copies ran while one was open for 1% of the time, Pallas kernels for 5%

profile of v6, /device:TPU:24, one launch (start us, length us, event | category | flops | bytes accessed | tf_op | source)
XLA Modules:
  0.0 249.8 jit_solution(12758360718650509982)
XLA Ops:
  0.7 222.9 %shard_map.263 = (bf16[2048,640]{1,0:T(8,128)(2,1)}, bf16[2048,640]{1,0:T(8,128)(2,1)}, f32[2048,640]{1,0:T(8,128)}, bf16[2048,640]{1,0:T(8,128)(2,1)}, bf16[512...) custom-call(bf16[2,2048,640]{2,1,0:T(8,128)(2,1)} %tokens.1, ...), custom_call_target="tpu_custom_call" | custom-call | flops 45298483200 | bytes 125829120 | tf_op jit(solution)/shard_map/pallas_call | solution.py:1121
  223.6 0.6 collective-permute-start.1
  224.2 0.0 copy-start.1
  224.2 0.0 copy-start.3
  224.2 11.0 %shard_map.264 = (bf16[2,2048,640]{2,1,0:T(8,128)(2,1)}, f32[2,2048,640]{2,1,0:T(8,128)}) custom-call(s32[1]{0:T(128)} %bitcast.side_ref, bf16[2048,640]{1,0:T(8,128)(2,1)} %get-tuple-element.26.out_own, bf16[2048,640]{1,0:T(8,128)(2,1)} %get-tuple-element.27.out_back, f32[2048,640]{1,0:T(8,128)} %get-tuple-element.28.dx_own, ...), custom_call_target="tpu_custom_call" | custom-call | flops 1310720 | bytes 31457280 | tf_op jit(solution)/shard_map/pallas_call | solution.py:1196
  235.2 1.5 collective-permute-start
  236.7 0.0 copy-done.1
  236.7 0.7 slice.42
  237.4 0.0 copy-done.3
  237.4 0.6 slice_reduce_fusion.3
  238.1 0.6 slice_reduce_fusion
  238.7 0.7 slice_bitcast_fusion
  239.4 2.1 collective-permute-done.1.tail_ref
  241.5 0.0 copy-start
  241.5 0.8 copy-done
  242.3 2.3 shard_map.265.whole_ref
  244.6 2.5 %collective-permute-done.tail_ref = bf16[256,640]{1,0:T(8,128)(2,1)S(1)} collective-permute-done((bf16[256,640]{1,0:T(8,128)(2,1)}, bf16[256,640]{1,0:T(8,128)(2,1)S(1)}, u32[]{:S(2)}, u32[]{:S(2)}) %collective-permute-start) | collective-permute-done | bytes 327712 | tf_op jit(solution)/shard_map/ppermute | solution.py:1266
  247.1 0.0 copy-start.2
  247.1 0.7 copy-done.2
  247.8 2.0 shard_map.266
Async XLA Ops:
  223.6 17.9 %collective-permute-start.1 = (bf16[512,640]{1,0:T(8,128)(2,1)}, bf16[512,640]{1,0:T(8,128)(2,1)S(1)}, u32[]{:S(2)}, u32[]{:S(2)}) collective-permute-start(bf16[512,640]{1,0:T(8,128)(2,1)} %get-tuple-element.34), channel_id=1, source_target_pairs={{0,1},{1,0},{2,3},{3,2},{4,5},{5,4},{6,7},{7,6},{8,9},{9,8},{10,11... | collective-permute-start | bytes 1966088 | tf_op jit(solution)/shard_map/ppermute | solution.py:1266
  224.2 12.5 %copy-start.1 = (f32[368,320]{1,0:T(8,128)S(1)}, f32[368,320]{1,0:T(8,128)}, u32[]{:S(2)}) copy-start(f32[368,320]{1,0:T(8,128)} %get-tuple-element.37) | copy-start | bytes 1413124
  224.2 13.3 %copy-start.3 = (f32[1,4224]{1,0:T(1,128)S(1)}, f32[1,4224]{1,0:T(1,128)}, u32[]{:S(2)}) copy-start(f32[1,4224]{1,0:T(1,128)} %get-tuple-element.36) | copy-start | bytes 50692
  235.2 11.9 %collective-permute-start = (bf16[256,640]{1,0:T(8,128)(2,1)}, bf16[256,640]{1,0:T(8,128)(2,1)S(1)}, u32[]{:S(2)}, u32[]{:S(2)}) collective-permute-start(bf16[256,640]{1,0:T(8,128)(2,1)} %get-tuple-element.33), channel_id=1, source_target_pairs={{0,1},{1,0},{2,3},{3,2},{4,5},{5,4},{6,7},{7,6},{8,9},{9,8},{10,11... | collective-permute-start | bytes 983048 | tf_op jit(solution)/shard_map/ppermute | solution.py:1266
  241.5 0.8 copy-start
  247.1 0.7 copy-start.2

commit v7 on v6

--- a/solution.py
+++ b/solution.py
@@ -1281,7 +1281,9 @@
     dx_end, grad_tokens = lax.optimization_barrier((dx_end, grad_tokens))
     end_back = swap(dx_end)
     grad_tokens = finish_call(side_array, tail_back, cotangent, grad_tokens, HEAD)
-    grad_tokens = finish_call(side_array, end_back, cotangent, grad_tokens, rows // BLOCK - 1)
+    gy_end = lax.dynamic_index_in_dim(cotangent[:, rows - BLOCK :], 1 - side, 0, keepdims=True)
+    end = end_back.astype(jnp.float32)[None] + gy_end.astype(jnp.float32)
+    grad_tokens = lax.dynamic_update_slice(grad_tokens, end, (1 - side, rows - BLOCK, 0))
     wanted = inner_half + 64
 
     def narrow_part(index):

time: 251 us -> 249 us (level)
  no operation moved by 1% of the time
where the time goes in v7:
time: 249 us; the launch traced here: 248 us
  Pallas kernels  236 us (95%)
  waiting for transfers between devices  5.44 us (2%)
  local copies, waits for them, and re-layouts  2.69 us (1%)
    pallas_call x1, Pallas kernels, fast_call(): pl.pallas_call(fast_kernel, out_shape=[jax.ShapeDtypeStruct(shape, dtype)...  223 us
    pallas_call x1, Pallas kernels, assemble_call(): pl.pallas_call(assemble_kernel, grid_spec=pltpu.PrefetchScalarGridSpec(nu...  11 us
    ppermute x2, waiting for transfers between devices, swap(): return lax.ppermute(value, 'ch', SWAP)  5.44 us
  transfers between devices with their start and end apart: 2, of which 2 were waited for; matrix products, arithmetic and copies ran while one was open for 1% of the time, Pallas kernels for 5%

profile of v7, /device:TPU:24, one launch (start us, length us, event | category | flops | bytes accessed | tf_op | source)
XLA Modules:
  0.0 248.0 jit_solution(11483524312761402171)
XLA Ops:
  0.7 222.9 %shard_map.263 = (bf16[2048,640]{1,0:T(8,128)(2,1)}, bf16[2048,640]{1,0:T(8,128)(2,1)}, f32[2048,640]{1,0:T(8,128)}, bf16[2048,640]{1,0:T(8,128)(2,1)}, bf16[512...) custom-call(bf16[2,2048,640]{2,1,0:T(8,128)(2,1)} %tokens.1, ...), custom_call_target="tpu_custom_call" | custom-call | flops 45298483200 | bytes 125829120 | tf_op jit(solution)/shard_map/pallas_call | solution.py:1121
  223.6 0.6 collective-permute-start
  224.2 0.0 copy-start
  224.2 0.0 copy-start.1
  224.2 11.0 %shard_map.264 = (bf16[2,2048,640]{2,1,0:T(8,128)(2,1)}, f32[2,2048,640]{2,1,0:T(8,128)}) custom-call(s32[1]{0:T(128)} %bitcast.side_ref, bf16[2048,640]{1,0:T(8,128)(2,1)} %get-tuple-element.26.out_own, bf16[2048,640]{1,0:T(8,128)(2,1)} %get-tuple-element.27.out_back, f32[2048,640]{1,0:T(8,128)} %get-tuple-element.28.dx_own, ...), custom_call_target="tpu_custom_call" | custom-call | flops 1310720 | bytes 31457280 | tf_op jit(solution)/shard_map/pallas_call | solution.py:1196
  235.2 1.5 collective-permute-start.1
  236.7 0.0 copy-done
  236.7 0.7 slice.46
  237.4 0.0 copy-done.1
  237.4 0.6 slice_reduce_fusion.3
  238.1 0.6 slice_reduce_fusion
  238.7 0.7 slice_bitcast_fusion
  239.4 0.0 slice-start
  239.4 2.2 collective-permute-done.tail_ref
  241.6 2.3 shard_map.265
  243.9 3.2 %collective-permute-done.1 = bf16[256,640]{1,0:T(8,128)(2,1)S(1)} collective-permute-done((bf16[256,640]{1,0:T(8,128)(2,1)}, bf16[256,640]{1,0:T(8,128)(2,1)S(1)}, u32[]{:S(2)}, u32[]{:S(2)}) %collective-permute-start.1) | collective-permute-done | bytes 327712 | tf_op jit(solution)/shard_map/ppermute | solution.py:1266
  247.1 0.0 slice-done
  247.1 0.9 fusion
Async XLA Ops:
  223.6 18.0 %collective-permute-start = (bf16[512,640]{1,0:T(8,128)(2,1)}, bf16[512,640]{1,0:T(8,128)(2,1)}, u32[]{:S(2)}, u32[]{:S(2)}) collective-permute-start(bf16[512,640]{1,0:T(8,128)(2,1)} %get-tuple-element.31), channel_id=1, source_target_pairs={{0,1},{1,0},{2,3},{3,2},{4,5},{5,4},{6,7},{7,6},{8,9},{9,8},{10,11... | collective-permute-start | bytes 1966088 | tf_op jit(solution)/shard_map/ppermute | solution.py:1266
  224.2 12.5 %copy-start = (f32[368,320]{1,0:T(8,128)S(1)}, f32[368,320]{1,0:T(8,128)}, u32[]{:S(2)}) copy-start(f32[368,320]{1,0:T(8,128)} %get-tuple-element.37) | copy-start | bytes 1413124
  224.2 13.3 %copy-start.1 = (f32[1,4224]{1,0:T(1,128)S(1)}, f32[1,4224]{1,0:T(1,128)}, u32[]{:S(2)}) copy-start(f32[1,4224]{1,0:T(1,128)} %get-tuple-element.36) | copy-start | bytes 50692
  235.2 11.9 %collective-permute-start.1 = (bf16[256,640]{1,0:T(8,128)(2,1)}, bf16[256,640]{1,0:T(8,128)(2,1)S(1)}, u32[]{:S(2)}, u32[]{:S(2)}) collective-permute-start(bf16[256,640]{1,0:T(8,128)(2,1)} %get-tuple-element.35), channel_id=1, source_target_pairs={{0,1},{1,0},{2,3},{3,2},{4,5},{5,4},{6,7},{7,6},{8,9},{9,8},{10,11... | collective-permute-start | bytes 983048 | tf_op jit(solution)/shard_map/ppermute | solution.py:1266
  239.4 7.8 %slice-start = ((bf16[2,2048,640]{2,1,0:T(8,128)(2,1)}), bf16[2,256,640]{2,1,0:T(8,128)(2,1)S(1)}, s32[]{:S(2)}) async-start(bf16[2,2048,640]{2,1,0:T(8,128)(2,1)} %cot_ref.1), calls=%async_computation | async-start | bytes 1310720 | tf_op jit(solution)/shard_map/slice | solution.py:1284

commit v8 on v7

--- a/solution.py
+++ b/solution.py
@@ -482,7 +482,7 @@
 CHUNKS = 4
 CONV_PAD = 8
 HEAD = 5
-LEAD = 128
+LEAD = 256
 
 
 def fast_kernel(
@@ -999,7 +999,7 @@
         def _():
             tail_block[...] = sent
 
-        @pl.when(step < HEAD - 1)
+        @pl.when(step < HEAD)
         def _():
             dx_copy(step).start()
 
@@ -1051,7 +1051,6 @@
         out_copy(at).wait()
     cross = remote(cross_send, cross_recv, cross_sems, 0, across)
     cross.start()
-    dx_copy(HEAD - 1).start()
     lead_copy.wait_send()
     for at in range(CHUNKS):
         token_copy(at).wait_send()

time: 249 us -> 249 us (level)
  no operation moved by 1% of the time
where the time goes in v8:
time: 249 us; the launch traced here: 248 us
  Pallas kernels  236 us (95%)
  waiting for transfers between devices  5.44 us (2%)
  local copies, waits for them, and re-layouts  2.69 us (1%)
    pallas_call x1, Pallas kernels, fast_call(): pl.pallas_call(fast_kernel, out_shape=[jax.ShapeDtypeStruct(shape, dtype)...  223 us
    pallas_call x1, Pallas kernels, assemble_call(): pl.pallas_call(assemble_kernel, grid_spec=pltpu.PrefetchScalarGridSpec(nu...  11 us
    ppermute x2, waiting for transfers between devices, swap(): return lax.ppermute(value, 'ch', SWAP)  5.44 us
  transfers between devices with their start and end apart: 2, of which 2 were waited for; matrix products, arithmetic and copies ran while one was open for 1% of the time, Pallas kernels for 5%

profile of v8, /device:TPU:24, one launch (start us, length us, event | category | flops | bytes accessed | tf_op | source)
XLA Modules:
  0.0 248.2 jit_solution(12739220413535181912)
XLA Ops:
  0.7 223.1 %shard_map.263 = (bf16[2048,640]{1,0:T(8,128)(2,1)}, bf16[2048,640]{1,0:T(8,128)(2,1)}, f32[2048,640]{1,0:T(8,128)}, bf16[2048,640]{1,0:T(8,128)(2,1)}, bf16[512...) custom-call(bf16[2,2048,640]{2,1,0:T(8,128)(2,1)} %tokens.1, ...), custom_call_target="tpu_custom_call" | custom-call | flops 45298483200 | bytes 125829120 | tf_op jit(solution)/shard_map/pallas_call | solution.py:1120
  223.7 0.6 collective-permute-start
  224.3 0.0 copy-start
  224.3 0.0 copy-start.1
  224.3 11.0 %shard_map.264 = (bf16[2,2048,640]{2,1,0:T(8,128)(2,1)}, f32[2,2048,640]{2,1,0:T(8,128)}) custom-call(s32[1]{0:T(128)} %bitcast.side_ref, bf16[2048,640]{1,0:T(8,128)(2,1)} %get-tuple-element.26.out_own, bf16[2048,640]{1,0:T(8,128)(2,1)} %get-tuple-element.27.out_back, f32[2048,640]{1,0:T(8,128)} %get-tuple-element.28.dx_own, ...), custom_call_target="tpu_custom_call" | custom-call | flops 1310720 | bytes 31457280 | tf_op jit(solution)/shard_map/pallas_call | solution.py:1195
  235.4 1.5 collective-permute-start.1
  236.9 0.0 copy-done
  236.9 0.7 slice.46
  237.6 0.0 copy-done.1
  237.6 0.6 slice_reduce_fusion.3
  238.2 0.6 slice_reduce_fusion
  238.8 0.7 slice_bitcast_fusion
  239.6 0.0 slice-start
  239.6 2.2 collective-permute-done.tail_ref
  241.8 2.3 shard_map.265
  244.1 3.2 %collective-permute-done.1 = bf16[256,640]{1,0:T(8,128)(2,1)S(1)} collective-permute-done((bf16[256,640]{1,0:T(8,128)(2,1)}, bf16[256,640]{1,0:T(8,128)(2,1)S(1)}, u32[]{:S(2)}, u32[]{:S(2)}) %collective-permute-start.1) | collective-permute-done | bytes 327712 | tf_op jit(solution)/shard_map/ppermute | solution.py:1265
  247.3 0.0 slice-done
  247.3 0.9 fusion
Async XLA Ops:
  223.7 18.0 %collective-permute-start = (bf16[512,640]{1,0:T(8,128)(2,1)}, bf16[512,640]{1,0:T(8,128)(2,1)}, u32[]{:S(2)}, u32[]{:S(2)}) collective-permute-start(bf16[512,640]{1,0:T(8,128)(2,1)} %get-tuple-element.31), channel_id=1, source_target_pairs={{0,1},{1,0},{2,3},{3,2},{4,5},{5,4},{6,7},{7,6},{8,9},{9,8},{10,11... | collective-permute-start | bytes 1966088 | tf_op jit(solution)/shard_map/ppermute | solution.py:1265
  224.3 12.5 %copy-start = (f32[368,320]{1,0:T(8,128)S(1)}, f32[368,320]{1,0:T(8,128)}, u32[]{:S(2)}) copy-start(f32[368,320]{1,0:T(8,128)} %get-tuple-element.37) | copy-start | bytes 1413124
  224.3 13.3 %copy-start.1 = (f32[1,4224]{1,0:T(1,128)S(1)}, f32[1,4224]{1,0:T(1,128)}, u32[]{:S(2)}) copy-start(f32[1,4224]{1,0:T(1,128)} %get-tuple-element.36) | copy-start | bytes 50692
  235.4 11.9 %collective-permute-start.1 = (bf16[256,640]{1,0:T(8,128)(2,1)}, bf16[256,640]{1,0:T(8,128)(2,1)S(1)}, u32[]{:S(2)}, u32[]{:S(2)}) collective-permute-start(bf16[256,640]{1,0:T(8,128)(2,1)} %get-tuple-element.35), channel_id=1, source_target_pairs={{0,1},{1,0},{2,3},{3,2},{4,5},{5,4},{6,7},{7,6},{8,9},{9,8},{10,11... | collective-permute-start | bytes 983048 | tf_op jit(solution)/shard_map/ppermute | solution.py:1265
  239.6 7.8 %slice-start = ((bf16[2,2048,640]{2,1,0:T(8,128)(2,1)}), bf16[2,256,640]{2,1,0:T(8,128)(2,1)S(1)}, s32[]{:S(2)}) async-start(bf16[2,2048,640]{2,1,0:T(8,128)(2,1)} %cot_ref.1), calls=%async_computation | async-start | bytes 1310720 | tf_op jit(solution)/shard_map/slice | solution.py:1283
